TPU v7x, 128 devices: a whole 4x4x4 slice. The times are simulated.
128 devices in a mesh: dp: 16 (over y, z), fsdp: 8 (over x, core).
Axes of the slice: x: 4, y: 4, z: 4, core: 2. Of those that a mesh axis runs over, the one named last changes fastest.
Arguments:
- ctx: bfloat16 [16384, 4096], P(('dp', 'fsdp')), may hold values from -0.5 to 0.5
- grad_out: bfloat16 [16384, 4096], P(('dp', 'fsdp')), may hold values from -6 to 6
- weight: bfloat16 [4096, 4096], P(None, 'fsdp'), may hold values from -0.09375 to 0.09375
- error: float32 [16, 4096, 4096], P('dp', 'fsdp'), may hold values from -6 to 6
- q_init: float32 [4096, 64], P('fsdp'), may hold values from -2 to 3
Outputs:
- grad_ctx: bfloat16 [16384, 4096], P(('dp', 'fsdp'))
- q_factor: float32 [4096, 64], P('fsdp')
- new_error: float32 [16, 4096, 4096], P('dp', 'fsdp')
All inputs are finite; a program needn't handle non-finite values.
Results may differ from a plain program's by a relative error of at most 0.0007.
Values may be sent and summed in bfloat16 or wider, within the bound.
No kernel may reach another device: no remote copies, remote signals or barrier semaphores. Data moves between devices by JAX's collectives and lax.ppermute only.
A program may use at most 128 MiB of HBM per device.

v0:
```python
import jax
import jax.numpy as jnp
from jax import lax
from jax.sharding import PartitionSpec as P


def orthonormal(p_raw):
    gram_matrix = jnp.dot(p_raw.T, p_raw, precision=lax.Precision.HIGHEST)
    factor_low = jnp.linalg.cholesky(gram_matrix)
    solved = jax.scipy.linalg.solve_triangular(factor_low, p_raw.T, lower=True)
    return solved.T


def reduce_left(p_part):
    return lax.psum(p_part, ("dp", "fsdp"))


def local(ctx, grad_out, weight, error, q_init):
    columns = lax.all_to_all(grad_out, "fsdp", split_axis=1, concat_axis=0, tiled=True)
    picked = grad_out
    input_sum = lax.dot_general(
        picked,
        lax.all_gather(weight, "fsdp", axis=1, tiled=True),
        (((1,), (1,)), ((), ())),
        preferred_element_type=jnp.float32,
    )
    grad_ctx = input_sum.astype(jnp.bfloat16)
    picked = columns
    local_grad = lax.dot_general(
        picked,
        lax.all_gather(ctx, "fsdp", axis=0, tiled=True),
        (((0,), (0,)), ((), ())),
        preferred_element_type=jnp.float32,
    )
    merged = local_grad + error[0]
    p_part = lax.dot_general(
        merged,
        q_init,
        (((0,), (0,)), ((), ())),
        precision=lax.Precision.HIGHEST,
        preferred_element_type=jnp.float32,
    )
    p_raw = reduce_left(p_part)
    p_factor = orthonormal(p_raw)
    q_part = jnp.dot(merged, p_factor, precision=lax.Precision.HIGHEST)
    q_factor = lax.psum(q_part, "dp") / lax.axis_size("dp")
    approx = jnp.dot(q_factor, p_factor.T, precision=lax.Precision.HIGHEST)
    new_error = merged - approx
    return (grad_ctx, q_factor, new_error[None])


def solution(mesh):
    in_specs = (
        P(("dp", "fsdp"), None),
        P(("dp", "fsdp"), None),
        P(None, "fsdp"),
        P("dp", "fsdp", None),
        P("fsdp", None),
    )
    out_specs = (P(("dp", "fsdp"), None), P("fsdp", None), P("dp", "fsdp", None))
    return jax.shard_map(local, mesh=mesh, in_specs=in_specs, out_specs=out_specs, check_vma=False)
```

profile of v0, /device:TPU:1, one launch (start us, length us, event | category | flops | bytes accessed | tf_op | source)
XLA Modules:
  0.0 523.3 jit_solution(2902414419973342056)
XLA Ops:
  7.2 0.0 copy-start
  7.2 0.0 all-gather.5.cloned.1.call-start
  7.2 0.7 all-gather.5.cloned.1.call-update
  7.9 0.0 all-reduce.3.cloned.1.call-start
  8.0 1.6 copy.10
  9.6 23.5 %all_to_all.19 = bf16[128,8,512]{0,2,1:T(8,128)(2,1)S(1)} all-to-all(bf16[128,8,512]{0,2,1:T(8,128)(2,1)S(1)} %bitcast.31), channel_id=1, replica_groups=mesh['dp'=16,'fsdp'=8] {'fsdp'}, dimensions={1} | all-to-all | bytes 2097152 | tf_op jit(solution)/shard_map/all_to_all | solution.py:19
  33.1 0.5 copy.11
  33.6 32.6 %all-gather.5.cloned.1.call-done = bf16[1024,4096]{1,0:T(8,128)(2,1)} async-done(((bf16[128,4096]{1,0:T(8,128)(2,1)}), bf16[1024,4096]{1,0:T(8,128)(2,1)}) %all-gather.5.cloned.1.call-update) | async-done | bytes 8388624 | tf_op jit(solution)/shard_map/all_gather | solution.py:31
  66.2 9.5 %bitcast_add_fusion = f32[512,4096]{1,0:T(8,128)S(1)} fusion(f32[1,512,4096]{2,1,0:T(8,128)} %param.8, bf16[1024,512]{1,0:T(8,128)(2,1)S(1)} %bitcast.29, bf16[1024,4096]{1,0:T(8,128)(2,1)} %all-gather.5.cloned.1.call-done), kind=kOutput, calls=%fused_computation | convolution fusion | flops 4297064448 | bytes 26214400 | tf_op jit(solution)/shard_map/dot_general | solution.py:29
  75.7 0.0 copy-start.2
  75.7 3.4 copy-done.2
  79.1 6.6 %fusion.4 = f32[4096,64]{0,1:T(8,128)} fusion(f32[512,4096]{1,0:T(8,128)S(1)} %bitcast_add_fusion, f32[512,64]{0,1:T(8,128)S(1)} %copy-done), kind=kOutput, calls=%fused_computation.14 | convolution fusion | flops 1610612736 | bytes 9568256 | tf_op jit(solution)/shard_map/dot_general | solution.py:36
  85.7 0.0 all-reduce.3.cloned.1.call-update
  85.7 0.2 all-reduce.5.cloned.1.call-start
  85.9 147.5 %all-reduce.3.cloned.1.call-done = f32[4096,64]{0,1:T(8,128)} async-done(((f32[4096,64]{0,1:T(8,128)}), f32[4096,64]{0,1:T(8,128)}) %all-reduce.3.cloned.1.call-update) | async-done | bytes 1048592 | tf_op jit(solution)/shard_map/psum | solution.py:15
  233.4 2.5 fusion.5
  236.0 0.1 copy.12
  236.1 5.8 %cholesky.16 = f32[64,64]{1,0:T(8,128)S(1)} custom-call(f32[64,64]{1,0:T(8,128)S(1)} %fusion.3), custom_call_target="Cholesky" | custom-call | tf_op jit(solution)/shard_map/jit(cholesky)/cholesky | solution.py:9
  242.0 0.6 compare_reduce_fusion
  242.6 0.7 fusion
  243.3 4.9 custom-call.7
  248.2 2.3 fusion.1
  250.4 11.1 %fusion.6 = f32[512,64]{0,1:T(8,128)} fusion(f32[512,4096]{1,0:T(8,128)} %copy-done.2, f32[64,4096]{1,0:T(8,128)S(1)} %fusion.1), kind=kOutput, calls=%fused_computation.16 | convolution fusion | flops 1610612736 | bytes 9568256 | tf_op jit(solution)/shard_map/dot_general | solution.py:45
  261.6 0.0 all-reduce.5.cloned.1.call-update
  261.6 0.3 all-gather.3.cloned.1.call-start
  261.9 0.3 all-gather.3.cloned.1.call-update
  262.2 79.0 %all-reduce.5.cloned.1.call-done = f32[512,64]{0,1:T(8,128)} async-done(((f32[512,64]{0,1:T(8,128)}), f32[512,64]{0,1:T(8,128)}) %all-reduce.5.cloned.1.call-update) | async-done | bytes 131088 | tf_op jit(solution)/shard_map/psum | solution.py:46
  341.2 0.9 broadcast_multiply_fusion
  342.1 0.0 copy-start.4
  342.1 11.4 %subtract_bitcast_fusion = f32[1,512,4096]{2,1,0:T(8,128)} fusion(f32[512,4096]{1,0:T(8,128)} %copy-done.2, f32[512,64]{0,1:T(8,128)S(1)} %broadcast_multiply_fusion, f32[64,4096]{1,0:T(8,128)S(1)} %fusion.1), kind=kOutput, calls=%fused_computation.1 | convolution fusion | flops 1612709888 | bytes 17956864 | tf_op jit(solution)/shard_map/dot_general | solution.py:47
  353.5 146.4 %all-gather.3.cloned.1.call-done = bf16[4096,4096]{1,0:T(8,128)(2,1)} async-done(((bf16[4096,512]{1,0:T(8,128)(2,1)}), bf16[4096,4096]{1,0:T(8,128)(2,1)}) %all-gather.3.cloned.1.call-update) | async-done | bytes 33554448 | tf_op jit(solution)/shard_map/all_gather | solution.py:23
  499.9 16.9 %convolution_convert_fusion = bf16[128,4096]{1,0:T(8,128)(2,1)} fusion(bf16[128,4096]{1,0:T(8,128)(2,1)S(1)} %copy-done.3, bf16[4096,4096]{1,0:T(8,128)(2,1)} %all-gather.3.cloned.1.call-done), kind=kOutput, calls=%fused_computation.2 | convolution fusion | flops 4295491584 | bytes 35651584 | tf_op jit(solution)/shard_map/dot_general | solution.py:21
  (8 shorter events, 0.1 us)
Async XLA Ops:
  7.2 71.9 %copy-start = (f32[512,64]{0,1:T(8,128)S(1)}, f32[512,64]{0,1:T(8,128)}, u32[]{:S(2)}) copy-start(f32[512,64]{0,1:T(8,128)} %param.9) | copy-start | bytes 393220
  7.2 59.0 %all-gather.5.cloned.1.call-start = ((), (), s32[]{:S(2)}) async-start(), calls=%async_computation.2 | async-start | bytes 9437184 | tf_op jit(solution)/shard_map/all_gather | solution.py:31
  7.9 225.5 %all-reduce.3.cloned.1.call-start = ((), (), s32[]{:S(2)}) async-start(), calls=%async_computation.3 | async-start | bytes 2097152 | tf_op jit(solution)/shard_map/psum | solution.py:15
  75.7 3.4 copy-start.2
  85.7 255.5 %all-reduce.5.cloned.1.call-start = ((), (), s32[]{:S(2)}) async-start(), calls=%async_computation.4 | async-start | bytes 262144 | tf_op jit(solution)/shard_map/psum | solution.py:46
  261.6 238.3 %all-gather.3.cloned.1.call-start = ((), (), s32[]{:S(2)}) async-start(), calls=%async_computation.1 | async-start | bytes 37748736 | tf_op jit(solution)/shard_map/all_gather | solution.py:23
  342.1 11.4 %copy-start.4 = (f32[512,64]{0,1:T(8,128)}, f32[512,64]{0,1:T(8,128)S(1)}, u32[]{:S(2)}) copy-start(f32[512,64]{0,1:T(8,128)S(1)} %broadcast_multiply_fusion) | copy-start | bytes 393220
  342.1 157.8 %copy-start.3 = (bf16[128,4096]{1,0:T(8,128)(2,1)S(1)}, bf16[128,4096]{1,0:T(8,128)(2,1)}, u32[]{:S(2)}) copy-start(bf16[128,4096]{1,0:T(8,128)(2,1)} %param.6) | copy-start | bytes 3145732
  499.9 16.9 %copy-start.1 = (f32[512,64]{0,1:T(8,128)S(1)}, f32[512,64]{0,1:T(8,128)}, u32[]{:S(2)}) copy-start(f32[512,64]{0,1:T(8,128)} %param.9) | copy-start | bytes 393220
Sparse Core Ops, SparseCore 0:
  9.7 56.3 all-gather.4
  85.8 147.5 all-reduce.2
  261.7 79.4 all-reduce.4
  342.7 157.0 all-gather.2
where the time goes:
time: 524 us; the launch traced here: 523 us
  waiting for transfers between devices  406 us (77%)
  matrix products  60.4 us (12%)
  blocking collectives  23.5 us (4%)
  between operations  13.9 us (3%)
  other arithmetic  13 us (2%)
  local copies, waits for them, and re-layouts  5.63 us (1%)
    psum x1, waiting for transfers between devices, reduce_left(): return lax.psum(p_part, ('dp', 'fsdp'))  148 us
    all_gather x1, waiting for transfers between devices, local(): lax.all_gather(weight, 'fsdp', axis=1, tiled=True)  146 us
    psum x1, waiting for transfers between devices, local(): q_factor = lax.psum(q_part, 'dp') / lax.axis_size('dp')  79 us
    all_gather x1, waiting for transfers between devices, local(): lax.all_gather(ctx, 'fsdp', axis=0, tiled=True)  32.6 us
    all_to_all x1, blocking collectives, local(): lax.all_to_all(grad_out, 'fsdp', split_axis=1, concat_axis=0, tiled=True)  23.5 us
    dot_general x1, matrix products, local(): lax.dot_general(picked, lax.all_gather(weight, 'fsdp', axis=1, tiled=True...  16.9 us
    dot_general x1, matrix products, local(): approx = jnp.dot(q_factor, p_factor.T, precision=lax.Precision.HIGHEST)  11.4 us
    dot_general x1, matrix products, local(): q_part = jnp.dot(merged, p_factor, precision=lax.Precision.HIGHEST)  11.1 us
  transfers between devices with their start and end apart: 4, of which 4 were waited for; matrix products, arithmetic and copies ran while one was open for 3% of the time, Pallas kernels for 0%

commit v1 on v0

v1 whole, which is shorter than its diff:
```python
import functools

import jax
import jax.numpy as jnp
from jax import lax
from jax.experimental import pallas as pl
from jax.experimental.pallas import tpu as pltpu
from jax.sharding import PartitionSpec as P

F32, BF16 = jnp.float32, jnp.bfloat16
VMEM = pl.BlockSpec(memory_space=pltpu.VMEM)
SMEM = pl.BlockSpec(memory_space=pltpu.SMEM)
HBM = pl.BlockSpec(memory_space=pltpu.HBM)
RELATIVE = [(a, d) for a in range(2) for d in range(4)]
NT = (((1,), (1,)), ((), ()))
NN = (((1,), (0,)), ((), ()))


def mm(lhs, rhs, dims=NN, precision=None):
    return lax.dot_general(lhs, rhs, dims, precision=precision, preferred_element_type=F32)


def halves(value):
    high = value.astype(BF16)
    return high, (value - high.astype(F32)).astype(BF16)


def thirds(value):
    high = value.astype(BF16)
    rest = value - high.astype(F32)
    mid = rest.astype(BF16)
    return high, mid, (rest - mid.astype(F32)).astype(BF16)


def along_x(value, d):
    return lax.ppermute(value, "fsdp", [(i, ((i // 2 + d) % 4) * 2 + i % 2) for i in range(8)])


def along_y(value, d):
    return lax.ppermute(value, "dp", [(i, ((i // 4 + d) % 4) * 4 + i % 4) for i in range(16)])


def along_z(value, d):
    return lax.ppermute(value, "dp", [(i, (i // 4) * 4 + (i % 4 + d) % 4) for i in range(16)])


def other_core(value):
    return lax.ppermute(value, "fsdp", [(i, i ^ 1) for i in range(8)])


def to_relative(value, a, d):
    return lax.ppermute(value, "fsdp", [(i, ((i // 2 + d) % 4) * 2 + (i % 2 ^ a)) for i in range(8)])


def pallas(body, out_shape, flops=0, bytes_accessed=0, mib=16, **kw):
    return pl.pallas_call(
        body,
        out_shape=out_shape,
        compiler_params=pltpu.CompilerParams(vmem_limit_bytes=mib * 2**20),
        cost_estimate=pl.CostEstimate(flops=int(flops), bytes_accessed=int(bytes_accessed), transcendentals=0),
        **kw,
    )


def in_hbm(value):
    return pltpu.with_memory_space_constraint(value, pltpu.HBM)


def shaped(shape, dtype=F32):
    return jax.ShapeDtypeStruct(shape, dtype)


def after(value, *earlier):
    return lax.optimization_barrier((value, *earlier))[0]


def chunk_of(x, c, a, d):
    return lax.rem(x + d, 4) * 2 + (c ^ a)


def rank_row(z, c, a, d):
    return pl.multiple_of((c ^ a) * 32 + lax.rem(z + d, 4) * 8, 8)


def cut_body(place, grad, *outs):
    x, c = place[0], place[1]
    for d, out in enumerate(outs):
        for a in range(2):
            out[a] = grad[:, pl.ds(pl.multiple_of(chunk_of(x, c, a, d) * 512, 512), 512)]


def cut(place, grad):
    return pallas(
        cut_body, [shaped((2, 128, 512), BF16)] * 4, bytes_accessed=2 << 20, in_specs=[SMEM, VMEM], out_specs=[VMEM] * 4
    )(place, grad)


def columns(i):
    return slice(512 * i, 512 * i + 512)


def fetch(source, held, arrived):
    copies = [pltpu.make_async_copy(source.at[:, columns(i)], held.at[:, columns(i)], arrived.at[i]) for i in range(8)]
    for copy in copies:
        copy.start()
    return copies


def error_left_body(place, qt, error, out, held, arrived, pieces):
    c, z = place[1], place[3]
    copies = fetch(error, held, arrived)
    for n, (a, d) in enumerate(RELATIVE):
        rows = qt[pl.ds(rank_row(z, c, a, d), 8), :]
        high = rows.astype(BF16).astype(F32)
        pieces[8 * n : 8 * n + 8, :] = high
        pieces[64 + 8 * n : 72 + 8 * n, :] = rows - high
    q = pieces[...].astype(BF16)
    for i, copy in enumerate(copies):
        copy.wait()
        high, low = halves(held[:, columns(i)])
        first = mm(q, high)
        out[:, columns(i)] = first[:64] + first[64:] + mm(q[:64], low)


def error_left(place, qt, error):
    return pallas(
        error_left_body,
        shaped((64, 4096)),
        flops=2 * 512 * 4096 * 192,
        bytes_accessed=9 << 20,
        in_specs=[SMEM, VMEM, HBM],
        out_specs=VMEM,
        scratch_shapes=[pltpu.VMEM((512, 4096), F32), pltpu.SemaphoreType.DMA((8,)), pltpu.VMEM((128, 512), F32)],
    )(place, qt, in_hbm(error))


def left_body(place, q0, q1, q2, q3, q_far, grad, ctx, term, near, far, g_abs, g_rel):
    x, c, z = place[0], place[1], place[3]
    total = jnp.zeros((64, 128), F32)
    for a, d in RELATIVE:
        q = (q0, q1, q2, q3)[d][...] if a == 0 else q_far[64 * d : 64 * d + 64, :]
        chunk = grad[:, pl.ds(pl.multiple_of(chunk_of(x, c, a, d) * 512, 512), 512)]
        parts = mm(jnp.concatenate(thirds(q), 0), chunk, NT)
        total += parts[:64] + parts[64:128] + parts[128:]
    g_abs[...] = total
    for n, (a, d) in enumerate(RELATIVE):
        g_rel[8 * n : 8 * n + 8, :] = g_abs[pl.ds(rank_row(z, c, a, d), 8), :]
    g = jnp.concatenate(thirds(g_rel[...]), 0)
    for i in range(4):
        at = slice(1024 * i, 1024 * i + 1024)
        parts = mm(g, ctx[:, at])
        whole = term[:, at] + (parts[:64] + parts[64:128] + parts[128:])
        near[:, at] = whole[:32]
        far[:, at] = whole[32:]


def left(place, q_near, q_far, grad, ctx, term):
    return pallas(
        left_body,
        [shaped((32, 4096))] * 2,
        flops=4 * 192 * 128 * 4096,
        bytes_accessed=5 << 20,
        in_specs=[SMEM] + [VMEM] * 8,
        out_specs=[VMEM] * 2,
        scratch_shapes=[pltpu.VMEM((64, 128), F32)] * 2,
    )(place, *q_near, q_far, grad, ctx, term)


def join_body(place, v0, v1, v2, v3, out):
    z = place[3]
    for d, value in enumerate((v0, v1, v2, v3)):
        out[:, pl.ds(pl.multiple_of(lax.rem(z + d, 4) * 1024, 1024), 1024)] = value[...]


def join(place, values):
    return pallas(
        join_body, shaped((values[0].shape[0], 4096), values[0].dtype), bytes_accessed=1 << 18, in_specs=[SMEM] + [VMEM] * 4, out_specs=VMEM
    )(place, *values)


def turn_body(place, c0, c1, c2, c3, c_far, out):
    x, c = place[0], place[1]
    for a, d in RELATIVE:
        chunk = (c0, c1, c2, c3)[d][0] if a == 0 else c_far[d]
        source = chunk_of(x, c, a, 4 - d)
        out[:, pl.ds(pl.multiple_of(source * 128, 128), 128)] = chunk.T


def turn(place, chunks, far):
    return pallas(
        turn_body, shaped((512, 1024), BF16), bytes_accessed=2 << 20, in_specs=[SMEM] + [VMEM] * 5, out_specs=VMEM
    )(place, *chunks, far)


def middle_body(place, p0, p1, p2, p3, p_far, ctx, p_out, u_out):
    c, z = place[1], place[3]
    for a, d in RELATIVE:
        p_out[pl.ds(rank_row(z, c, a, d), 8), :] = (p0, p1, p2, p3)[d][...] if a == 0 else p_far[8 * d : 8 * d + 8, :]
    u = jnp.zeros((64, 128), F32)
    for i in range(4):
        at = slice(1024 * i, 1024 * i + 1024)
        parts = mm(jnp.concatenate(thirds(p_out[:, at]), 0), ctx[:, at], NT)
        u += parts[:64] + parts[64:128] + parts[128:]
    u_out[...] = u


def middle(place, p_near, p_far, ctx):
    return pallas(
        middle_body,
        [shaped((64, 4096)), shaped((64, 128))],
        flops=2 * 192 * 128 * 4096,
        bytes_accessed=4 << 20,
        in_specs=[SMEM] + [VMEM] * 6,
        out_specs=[VMEM] * 2,
    )(place, *p_near, p_far, ctx)


def right_body(p_raw, error, out, held, arrived):
    for i, copy in enumerate(fetch(error, held, arrived)):
        high, low = halves(p_raw[:, columns(i)])
        copy.wait()
        e_high, e_low = halves(held[:, columns(i)])
        parts = mm(e_high, jnp.concatenate([high, low], 0), NT)
        part = parts[:, :64] + parts[:, 64:] + mm(e_low, high, NT)
        if i == 0:
            out[...] = part
        else:
            out[...] += part


def right(p_raw, error):
    return pallas(
        right_body,
        shaped((512, 64)),
        flops=2 * 512 * 4096 * 192,
        bytes_accessed=9 << 20,
        in_specs=[VMEM, HBM],
        out_specs=VMEM,
        scratch_shapes=[pltpu.VMEM((512, 4096), F32), pltpu.SemaphoreType.DMA((8,))],
    )(p_raw, in_hbm(error))


def collect_body(place, term, turned, u0, u1, u2, u3, u_far, out, u_all):
    x, c = place[0], place[1]
    for a, d in RELATIVE:
        u = (u0, u1, u2, u3)[d][...] if a == 0 else u_far[64 * d : 64 * d + 64, :]
        first = pl.multiple_of(chunk_of(x, c, a, d) * 128, 128)
        for n, part in enumerate(thirds(u)):
            u_all[64 * n : 64 * n + 64, pl.ds(first, 128)] = part
    parts = mm(u_all[...], turned[...], NT)
    out[...] = term[...].T + (parts[:64] + parts[64:128] + parts[128:])


def collect(place, term, turned, u_near, u_far):
    return pallas(
        collect_body,
        shaped((64, 512)),
        flops=2 * 192 * 1024 * 512,
        bytes_accessed=2 << 20,
        in_specs=[SMEM] + [VMEM] * 7,
        out_specs=VMEM,
        scratch_shapes=[pltpu.VMEM((192, 1024), BF16)],
    )(place, term, turned, *u_near, u_far)


def solve_body(p_raw, inverse, out):
    squares = jnp.zeros((192, 192), F32)
    for i in range(4):
        stack = jnp.concatenate(thirds(p_raw[:, 1024 * i : 1024 * i + 1024]), 0)
        squares += mm(stack, stack, NT)
    gram = squares[:64, :64] + (
        (squares[:64, 64:128] + squares[64:128, :64]) + (squares[:64, 128:] + squares[128:, :64] + squares[64:128, 64:128])
    )
    same = lax.broadcasted_iota(jnp.int32, (64, 64), 0) == lax.broadcasted_iota(jnp.int32, (64, 64), 1)
    row = lax.broadcasted_iota(jnp.int32, (64, 128), 0)
    both = jnp.concatenate([gram, jnp.where(same, 1.0, 0.0).astype(F32)], 1)
    for k in range(64):
        scale = both[:, k : k + 1] / both[k : k + 1, k : k + 1]
        both = both - jnp.where(row > k, scale * both[k : k + 1, :], 0.0)
    diagonal = jnp.sum(jnp.where(same, both[:, :64], 0.0), 1, keepdims=True)
    solved = both[:, 64:] / jnp.sqrt(diagonal)
    inverse[...] = solved
    for i in range(4):
        at = slice(1024 * i, 1024 * i + 1024)
        high, low = halves(mm(solved, p_raw[:, at], NN, lax.Precision.HIGHEST))
        out[:, at] = jnp.concatenate([high, low, high], 0)


def solve(p_raw):
    return pallas(
        solve_body,
        [shaped((64, 64)), shaped((192, 4096), BF16)],
        flops=8 << 20,
        bytes_accessed=25 << 20,
        in_specs=[VMEM],
        out_specs=[VMEM] * 2,
    )(p_raw)


def last_body(inverse, w, turned, p, error, ctx, q_out, out, held, held_ctx, arrived, arrived_ctx, left_here):
    copies = list(zip(fetch(error, held, arrived), fetch(ctx, held_ctx, arrived_ctx)))
    q = mm(inverse[...], w[...], NN, lax.Precision.HIGHEST) * (1.0 / 16)
    q_out[...] = q
    high, low = halves(q.T)
    q_split = jnp.concatenate([high, high, low], 1)
    stores = []
    for i, (copy, copy_ctx) in enumerate(copies):
        copy_ctx.wait()
        product = mm(turned[...], held_ctx[:, columns(i)])
        approx = mm(q_split, p[:, columns(i)])
        copy.wait()
        held[:, columns(i)] = (held[:, columns(i)] + product) - approx
        stores.append(pltpu.make_async_copy(held.at[:, columns(i)], out.at[:, columns(i)], left_here.at[i]))
        stores[-1].start()
    for store in stores:
        store.wait()


def last(inverse, w, turned, p, error, ctx):
    return pallas(
        last_body,
        [shaped((64, 512)), shaped((512, 4096))],
        flops=2 * 512 * 4096 * 1216,
        bytes_accessed=27 << 20,
        mib=32,
        in_specs=[VMEM] * 4 + [HBM] * 2,
        out_specs=[VMEM, HBM],
        scratch_shapes=[pltpu.VMEM((512, 4096), F32), pltpu.VMEM((1024, 4096), BF16)] + [pltpu.SemaphoreType.DMA((8,))] * 3,
    )(inverse, w, turned, p, in_hbm(error), in_hbm(ctx))


def share_body(place, tokens, *refs):
    slabs, outs, whole = refs[:8], refs[8:12], refs[12]
    x, c, y, z = place[0], place[1], place[2], place[3]
    for e in range(4):
        total = jnp.zeros((512, 256), F32)
        for a in range(2):
            for d in range(4):
                at = pl.ds(pl.multiple_of(chunk_of(x, c, a, 4 - d) * 512, 512), 512)
                total += mm(tokens[:, :, at].reshape(512, 512), slabs[4 * a + e][d], NT)
        whole[:, pl.ds(pl.multiple_of(lax.rem(y + e, 4) * 256, 256), 256)] = total.astype(BF16)
    for d, out in enumerate(outs):
        out[...] = whole[pl.ds(pl.multiple_of(lax.rem(z + d, 4) * 128, 128), 128), :]


def share(place, tokens, mine, theirs):
    return pallas(
        share_body,
        [shaped((128, 1024), BF16)] * 4,
        flops=2 * 512 * 1024 * 4096,
        bytes_accessed=12 << 20,
        mib=24,
        in_specs=[SMEM] + [VMEM] * 9,
        out_specs=[VMEM] * 4,
        scratch_shapes=[pltpu.VMEM((512, 1024), BF16)],
    )(place, tokens, *mine, *theirs)


def pair_sum(values):
    return (values[0] + values[2]) + (values[1] + values[3])


def local(ctx, grad_out, weight, error, q_init):
    j, k = lax.axis_index("fsdp"), lax.axis_index("dp")
    x, c, y, z = j // 2, j % 2, k // 4, k % 4
    place = jnp.stack([x, c, y, z]).astype(jnp.int32)
    error = error[0]

    groups = [[e * 4 + f for f in range(4)] for e in range(4)]
    tokens = lax.all_gather(grad_out, "dp", axis_index_groups=groups)

    qt = q_init.T
    q_near = [qt] + [along_x(qt, -d) for d in (1, 2, 3)]
    piece = lax.dynamic_slice_in_dim(weight, z * 1024 + y * 256, 256, 0)
    pieces = [piece, along_x(piece, 1), along_x(after(piece, q_near[1]), 2), along_x(piece, 3)]
    term = error_left(place, qt, error)
    q_far = other_core(jnp.concatenate([qt, after(q_near[1], term, pieces[1], pieces[3]), *q_near[2:]], 0))
    near, far = left(place, q_near, after(q_far, pieces[2]), grad_out, ctx, term)
    half = near + other_core(far)

    sends = cut(place, grad_out)
    moved = [sends[0]] + [along_x(after(sends[d], near), d) if d != 2 else None for d in (1, 2, 3)]
    blocks = [half[:8]] + [along_z(half[8 * d : 8 * d + 8], d) for d in (1, 2, 3)]
    blocks[3] = after(blocks[3], moved[1], moved[3])
    summed = pair_sum(blocks)
    moved[2] = along_x(after(sends[2], summed), 2)
    w0 = after(jnp.stack(pieces), half)
    over_y = [summed] + [along_y(summed, d) for d in (1, 2, 3)]
    their0 = other_core(after(w0, summed))
    over_y[3] = after(over_y[3], moved[2], their0)
    summed = pair_sum(over_y)
    w1, w3 = [along_y(after(w0, summed), d) for d in (-1, 1)]
    far_columns = other_core(after(jnp.stack([m[1] for m in moved]), summed))
    over_x = [summed] + [along_x(summed, d) for d in (1, 2, 3)]
    ctx_all = lax.all_gather(after(ctx, summed, tokens), "fsdp", axis=0, tiled=True)
    turned = turn(place, moved, far_columns)
    over_x[3] = after(over_x[3], turned)
    rows = pair_sum(over_x)
    p_near = [rows] + [along_z(rows, -d) for d in (1, 2, 3)]
    p_far = other_core(jnp.concatenate(p_near, 0))

    p_raw, u = middle(place, p_near, after(p_far, w1, w3), ctx)
    w2 = along_y(after(w0, w1, w3), 2)
    u_near = [u] + [along_x(u, -d) for d in (1, 2, 3)]
    w_term = right(p_raw, error)
    u_far = other_core(jnp.concatenate([u, u_near[1], u_near[2], after(u_near[3], w_term)], 0))
    their1, their3 = other_core(after(w1, u)), other_core(after(w3, u))
    w = collect(place, after(w_term, their1, their3), turned, u_near, u_far)
    w = [w] + [along_z(w, d) for d in (1, 2, 3)]
    inverse, p = solve(p_raw)
    w = pair_sum([w[0], w[1], w[2], after(w[3], p)])
    their2 = other_core(after(w2, w))
    w = [w] + [along_y(w, d) for d in (1, 2, 3)]
    outs = share(place, tokens, [w0, w1, w2, w3], [their0, their1, their2, their3])
    w = pair_sum([w[0], w[1], w[2], after(w[3], outs[0])])
    outs = [outs[0]] + [along_z(outs[d], d) for d in (1, 2, 3)]
    q_factor, new_error = last(inverse, w, turned, p, error, ctx_all)
    grad_ctx = join(place, [outs[0], outs[3], outs[2], after(outs[1], q_factor)])
    return (grad_ctx, q_factor.T, new_error[None])


def solution(mesh):
    in_specs = (
        P(("dp", "fsdp"), None),
        P(("dp", "fsdp"), None),
        P(None, "fsdp"),
        P("dp", "fsdp", None),
        P("fsdp", None),
    )
    out_specs = (P(("dp", "fsdp"), None), P("fsdp", None), P("dp", "fsdp", None))
    return jax.shard_map(local, mesh=mesh, in_specs=in_specs, out_specs=out_specs, check_vma=False)
```

time: 524 us -> 182 us (0.35)
  waiting for transfers between devices: 406 us -> 56.3 us
  matrix products: 60.4 us -> 0 us
  starting transfers between devices: 0.56 us -> 57.7 us
  Pallas kernels: 0 us -> 43 us
  blocking collectives: 23.5 us -> 0 us
  other arithmetic: 13 us -> 0.58 us
    psum x2 -> x0, waiting for transfers between devices: 227 us -> none  [the longest x1 148 us: reduce_left(): return lax.psum(p_part, ('dp', 'fsdp'))]
    all_gather x2, waiting for transfers between devices: 179 us -> 0.04 us  [the longest x1 0.02 us: local(): lax.all_gather(after(ctx, summed, tokens), 'fsdp', axis=0, tiled=True)]
    dot_general x6 -> x0, matrix products: 58.1 us -> none  [the longest x1 16.9 us: local(): lax.dot_general(picked, lax.all_gather(weight, 'fsdp', axis=1, tiled=True...]
    ppermute x0 -> x45, starting transfers between devices: none -> 57.6 us  [the longest x12 16.7 us: along_z(): lax.ppermute(value, 'dp', [(i, i // 4 * 4 + (i % 4 + d) % 4) for i in ran...]
    ppermute x0 -> x45, waiting for transfers between devices: none -> 55.6 us  [the longest x15 21.5 us: along_x(): lax.ppermute(value, 'fsdp', [(i, (i // 2 + d) % 4 * 2 + i % 2) for i in r...]
    pallas_call x0 -> x11, Pallas kernels: none -> 43 us  [the longest x1 11.4 us: last(): pallas(last_body, [shaped((64, 512)), shaped((512, 4096))], flops=2 * 512...]
    all_to_all x1 -> x0, blocking collectives: 23.5 us -> none  [local(): lax.all_to_all(grad_out, 'fsdp', split_axis=1, concat_axis=0, tiled=True)]
    another operation x5 -> x3, other arithmetic: 12.1 us -> 0.28 us  [the longest x1 0.13 us: local(): w0 = after(jnp.stack(pieces), half)]
  transfers between devices with their start and end apart: 4 -> 47, of which waited for: 4 -> 16; matrix products, arithmetic and copies ran while one was open for 3% -> 1% of each run, Pallas kernels for 0% -> 23%
where the time goes in v1:
time: 182 us
  starting transfers between devices  57.7 us (32%)
  waiting for transfers between devices  56.3 us (31%)
  Pallas kernels  43 us (24%)
  between operations  14.5 us (8%)
  local copies, waits for them, and re-layouts  9.69 us (5%)
    ppermute x15, waiting for transfers between devices, along_x(): lax.ppermute(value, 'fsdp', [(i, (i // 2 + d) % 4 * 2 + i % 2) for i in r...  21.5 us
    ppermute x9, waiting for transfers between devices, along_y(): lax.ppermute(value, 'dp', [(i, (i // 4 + d) % 4 * 4 + i % 4) for i in ran...  17.6 us
    ppermute x12, starting transfers between devices, along_z(): lax.ppermute(value, 'dp', [(i, i // 4 * 4 + (i % 4 + d) % 4) for i in ran...  16.7 us
    ppermute x15, starting transfers between devices, along_x(): lax.ppermute(value, 'fsdp', [(i, (i // 2 + d) % 4 * 2 + i % 2) for i in r...  16.5 us
    ppermute x12, waiting for transfers between devices, along_z(): lax.ppermute(value, 'dp', [(i, i // 4 * 4 + (i % 4 + d) % 4) for i in ran...  15.5 us
    ppermute x9, starting transfers between devices, other_core(): return lax.ppermute(value, 'fsdp', [(i, i ^ 1) for i in range(8)])  13.9 us
    pallas_call x1, Pallas kernels, last(): pallas(last_body, [shaped((64, 512)), shaped((512, 4096))], flops=2 * 512...  11.4 us
    ppermute x9, starting transfers between devices, along_y(): lax.ppermute(value, 'dp', [(i, (i // 4 + d) % 4 * 4 + i % 4) for i in ran...  10.5 us
  transfers between devices with their start and end apart: 47, of which 16 were waited for; matrix products, arithmetic and copies ran while one was open for 1% of the time, Pallas kernels for 23%

profile of v1, /device:TPU:1, one launch (start us, length us, event | category | flops | bytes accessed | tf_op | source)
XLA Modules:
  0.0 181.7 jit_solution(13529360345455869448)
XLA Ops:
  8.9 3.4 %collective-permute-start.3 = (bf16[256,512]{1,0:T(8,128)(2,1)S(1)}, bf16[256,512]{1,0:T(8,128)(2,1)S(1)}, u32[]{:S(2)}, u32[]{:S(2)}) collective-permute-start(bf16[256,512]{1,0:T(8,128)(2,1)S(1)} %constant_dynamic-slice_fusion), channel_id=1, source_target_pairs={{0,6},{1,7},{2,0},{3,1},{4,2},{5,3},{6,4},{7,5},{8,14},{9,15},{10,... | collective-permute-start | bytes 786440 | tf_op jit(solution)/shard_map/ppermute | solution.py:36
  12.3 2.7 %collective-permute-start.1 = (f32[64,512]{1,0:T(8,128)}, f32[64,512]{1,0:T(8,128)S(1)}, u32[]{:S(2)}, u32[]{:S(2)}) collective-permute-start(f32[64,512]{1,0:T(8,128)} %bitcast.14), channel_id=1, source_target_pairs={{0,6},{1,7},{2,0},{3,1},{4,2},{5,3},{6,4},{7,5},{8,14},{9,15},{10,... | collective-permute-start | bytes 393224 | tf_op jit(solution)/shard_map/ppermute | solution.py:36
  16.6 4.4 %shard_map.76.term = f32[64,4096]{1,0:T(8,128)S(1)} custom-call(s32[4]{0:T(128)S(1)} %pad_add_fusion.place, f32[64,512]{1,0:T(8,128)S(1)} %bitcast.17, f32[512,4096]{1,0:T(8,128)} %bitcast.21), custom_call_target="tpu_custom_call" | custom-call | flops 805306368 | bytes 9437184 | tf_op jit(solution)/shard_map/pallas_call | solution.py:126
  22.2 3.8 %collective-permute-done.5.q3 = f32[64,512]{1,0:T(8,128)S(1)} collective-permute-done((f32[64,512]{1,0:T(8,128)}, f32[64,512]{1,0:T(8,128)S(1)}, u32[]{:S(2)}, u32[]{:S(2)}) %collective-permute-start.5) | collective-permute-done | bytes 131104 | tf_op jit(solution)/shard_map/ppermute | solution.py:36
  26.1 1.9 %collective-permute-start.6 = (f32[256,512]{1,0:T(8,128)S(1)}, f32[256,512]{1,0:T(8,128)S(1)}, u32[]{:S(2)}, u32[]{:S(2)}) collective-permute-start(f32[256,512]{1,0:T(8,128)S(1)} %pad_maximum_fusion.1), channel_id=1, source_target_pairs={{0,1},{1,0},{2,3},{3,2},{4,5},{5,4},{6,7},{7,6},{8,9},{9,8},{10,11... | collective-permute-start | bytes 1572872 | tf_op jit(solution)/shard_map/ppermute | solution.py:48
  28.0 9.4 %collective-permute-done.2 = bf16[256,512]{1,0:T(8,128)(2,1)S(1)} collective-permute-done((bf16[256,512]{1,0:T(8,128)(2,1)S(1)}, bf16[256,512]{1,0:T(8,128)(2,1)S(1)}, u32[]{:S(2)}, u32[]{:S(2)}) %collective-permute-start.2) | collective-permute-done | bytes 262176 | tf_op jit(solution)/shard_map/ppermute | solution.py:36
  37.4 2.4 %shard_map.77 = (f32[32,4096]{1,0:T(8,128)S(1)}, f32[32,4096]{1,0:T(8,128)S(1)}) custom-call(s32[4]{0:T(128)S(1)} %pad_add_fusion.place, f32[64,512]{1,0:T(8,128)S(1)} %bitcast.19, f32[64,512]{1,0:T(8,128)S(1)} %collective-permute-done.1.q1, f32[64,512]{1,0:T(8,128)S(1)} %collective-permute-done.4.q2, f32[64,512]{1,0:T(8,128)S(1)} %collective-permute-done.5.q3, ...), custom_call_target="tpu_custom_call" | custom-call | flops 402653184 | bytes 5242880 | tf_op jit(solution)/shard_map/pallas_call | solution.py:158
  42.5 2.7 %collective-permute-start.12 = (bf16[2,128,512]{2,1,0:T(8,128)(2,1)S(1)}, bf16[2,128,512]{2,1,0:T(8,128)(2,1)S(1)}, u32[]{:S(2)}, u32[]{:S(2)}) collective-permute-start(bf16[2,128,512]{2,1,0:T(8,128)(2,1)S(1)} %get-tuple-element.52), channel_id=1, source_target_pairs={{0,6},{1,7},{2,0},{3,1},{4,2},{5,3},{6,4},{7,5},{8,14},{9,15},{10,... | collective-permute-start | bytes 786440 | tf_op jit(solution)/shard_map/ppermute | solution.py:36
  45.2 3.7 %collective-permute-start.8 = (f32[8,4096]{1,0:T(8,128)S(1)}, f32[8,4096]{1,0:T(8,128)S(1)}, u32[]{:S(2)}, u32[]{:S(2)}) collective-permute-start(f32[8,4096]{1,0:T(8,128)S(1)} %get-tuple-element.85), channel_id=1, source_target_pairs={{0,16},{8,24},{16,0},{24,8},{32,48},{40,56},{48,32},{56,40},{64,80... | collective-permute-start | bytes 393224 | tf_op jit(solution)/shard_map/ppermute | solution.py:44
  49.7 1.9 %collective-permute-start.10 = (f32[8,4096]{1,0:T(8,128)S(1)}, f32[8,4096]{1,0:T(8,128)S(1)}, u32[]{:S(2)}, u32[]{:S(2)}) collective-permute-start(f32[8,4096]{1,0:T(8,128)S(1)} %get-tuple-element.83), channel_id=1, source_target_pairs={{0,24},{8,0},{16,8},{24,16},{32,56},{40,32},{48,40},{56,48},{64,88... | collective-permute-start | bytes 393224 | tf_op jit(solution)/shard_map/ppermute | solution.py:44
  51.8 10.1 %collective-permute-done.10 = f32[8,4096]{1,0:T(8,128)S(1)} collective-permute-done((f32[8,4096]{1,0:T(8,128)S(1)}, f32[8,4096]{1,0:T(8,128)S(1)}, u32[]{:S(2)}, u32[]{:S(2)}) %collective-permute-start.10) | collective-permute-done | bytes 131104 | tf_op jit(solution)/shard_map/ppermute | solution.py:44
  63.3 2.7 %collective-permute-start.15 = (f32[8,4096]{1,0:T(8,128)S(1)}, f32[8,4096]{1,0:T(8,128)S(1)}, u32[]{:S(2)}, u32[]{:S(2)}) collective-permute-start(f32[8,4096]{1,0:T(8,128)S(1)} %fusion), channel_id=1, source_target_pairs={{0,96},{8,104},{16,112},{24,120},{32,0},{40,8},{48,16},{56,24},{64... | collective-permute-start | bytes 393224 | tf_op jit(solution)/shard_map/ppermute | solution.py:40
  66.1 1.6 collective-permute-start.13
  68.8 3.9 %collective-permute-done.16.c2 = bf16[2,128,512]{2,1,0:T(8,128)(2,1)S(1)} collective-permute-done((bf16[2,128,512]{2,1,0:T(8,128)(2,1)S(1)}, bf16[2,128,512]{2,1,0:T(8,128)(2,1)S(1)}, u32[]{:S(2)}, u32[]{:S(2)}) %collective-permute-start.16) | collective-permute-done | bytes 262176 | tf_op jit(solution)/shard_map/ppermute | solution.py:36
  77.8 3.0 %collective-permute-start.21 = (f32[8,4096]{1,0:T(8,128)S(1)}, f32[8,4096]{1,0:T(8,128)S(1)}, u32[]{:S(2)}, u32[]{:S(2)}) collective-permute-start(f32[8,4096]{1,0:T(8,128)S(1)} %add_add_fusion.3), channel_id=1, source_target_pairs={{0,4},{1,5},{2,6},{3,7},{4,0},{5,1},{6,2},{7,3},{8,12},{9,13},{10,... | collective-permute-start | bytes 393224 | tf_op jit(solution)/shard_map/ppermute | solution.py:36
  84.7 2.2 %collective-permute-done.21 = f32[8,4096]{1,0:T(8,128)S(1)} collective-permute-done((f32[8,4096]{1,0:T(8,128)S(1)}, f32[8,4096]{1,0:T(8,128)S(1)}, u32[]{:S(2)}, u32[]{:S(2)}) %collective-permute-start.21) | collective-permute-done | bytes 131104 | tf_op jit(solution)/shard_map/ppermute | solution.py:36
  87.6 1.8 collective-permute-start.26
  91.2 1.8 %collective-permute-done.26.p2 = f32[8,4096]{1,0:T(8,128)S(1)} collective-permute-done((f32[8,4096]{1,0:T(8,128)S(1)}, f32[8,4096]{1,0:T(8,128)S(1)}, u32[]{:S(2)}, u32[]{:S(2)}) %collective-permute-start.26) | collective-permute-done | bytes 131104 | tf_op jit(solution)/shard_map/ppermute | solution.py:44
  93.0 3.3 %collective-permute-done.27.p3 = f32[8,4096]{1,0:T(8,128)S(1)} collective-permute-done((f32[8,4096]{1,0:T(8,128)S(1)}, f32[8,4096]{1,0:T(8,128)S(1)}, u32[]{:S(2)}, u32[]{:S(2)}) %collective-permute-start.27) | collective-permute-done | bytes 131104 | tf_op jit(solution)/shard_map/ppermute | solution.py:44
  96.3 1.8 collective-permute-start.28
  98.1 14.4 %collective-permute-done.18.refs_1_ = bf16[4,256,512]{2,1,0:T(8,128)(2,1)S(1)} collective-permute-done((bf16[4,256,512]{2,1,0:T(8,128)(2,1)S(1)}, bf16[4,256,512]{2,1,0:T(8,128)(2,1)S(1)}, u32[]{:S(2)}, u32[]{:S(2)}) %collective-permute-start.18) | collective-permute-done | bytes 1048608 | tf_op jit(solution)/shard_map/ppermute | solution.py:40
  114.7 2.9 %collective-permute-start.29 = (bf16[4,256,512]{2,1,0:T(8,128)(2,1)S(1)}, bf16[4,256,512]{2,1,0:T(8,128)(2,1)S(1)}, u32[]{:S(2)}, u32[]{:S(2)}) collective-permute-start(bf16[4,256,512]{2,1,0:T(8,128)(2,1)S(1)} %collective-permute-done.18.refs_1_), channel_id=1, source_target_pairs={{0,1},{1,0},{2,3},{3,2},{4,5},{5,4},{6,7},{7,6},{8,9},{9,8},{10,11... | collective-permute-start | bytes 3145736 | tf_op jit(solution)/shard_map/ppermute | solution.py:48
  118.2 2.7 %collective-permute-start.31 = (f32[64,128]{1,0:T(8,128)S(1)}, f32[64,128]{1,0:T(8,128)S(1)}, u32[]{:S(2)}, u32[]{:S(2)}) collective-permute-start(f32[64,128]{1,0:T(8,128)S(1)} %get-tuple-element.64.u0), channel_id=1, source_target_pairs={{0,6},{1,7},{2,0},{3,1},{4,2},{5,3},{6,4},{7,5},{8,14},{9,15},{10,... | collective-permute-start | bytes 98312 | tf_op jit(solution)/shard_map/ppermute | solution.py:36
  122.2 5.5 %shard_map.81.term = f32[512,64]{1,0:T(8,128)S(1)} custom-call(f32[64,4096]{1,0:T(8,128)S(1)} %get-tuple-element.66.p_raw, f32[512,4096]{1,0:T(8,128)} %bitcast.22), custom_call_target="tpu_custom_call" | custom-call | flops 805306368 | bytes 9437184 | tf_op jit(solution)/shard_map/pallas_call | solution.py:232
  127.7 1.9 %collective-permute-start.34 = (f32[256,128]{1,0:T(8,128)S(1)}, f32[256,128]{1,0:T(8,128)S(1)}, u32[]{:S(2)}, u32[]{:S(2)}) collective-permute-start(f32[256,128]{1,0:T(8,128)S(1)} %pad_maximum_fusion.4), channel_id=1, source_target_pairs={{0,1},{1,0},{2,3},{3,2},{4,5},{5,4},{6,7},{7,6},{8,9},{9,8},{10,11... | collective-permute-start | bytes 393224 | tf_op jit(solution)/shard_map/ppermute | solution.py:48
  131.8 2.7 %collective-permute-start.37 = (f32[64,512]{1,0:T(8,128)S(1)}, f32[64,512]{1,0:T(8,128)S(1)}, u32[]{:S(2)}, u32[]{:S(2)}) collective-permute-start(f32[64,512]{1,0:T(8,128)S(1)} %shard_map.82), channel_id=1, source_target_pairs={{0,24},{8,0},{16,8},{24,16},{32,56},{40,32},{48,40},{56,48},{64,88... | collective-permute-start | bytes 393224 | tf_op jit(solution)/shard_map/ppermute | solution.py:44
  135.8 7.9 %shard_map.83 = (f32[64,64]{1,0:T(8,128)S(1)}, bf16[192,4096]{1,0:T(8,128)(2,1)S(1)}) custom-call(f32[64,4096]{1,0:T(8,128)S(1)} %get-tuple-element.66.p_raw), custom_call_target="tpu_custom_call" | custom-call | flops 8388608 | bytes 26214400 | tf_op jit(solution)/shard_map/pallas_call | solution.py:290
  146.8 2.3 %collective-permute-start.44 = (f32[64,512]{1,0:T(8,128)S(1)}, f32[64,512]{1,0:T(8,128)S(1)}, u32[]{:S(2)}, u32[]{:S(2)}) collective-permute-start(f32[64,512]{1,0:T(8,128)S(1)} %add_add_fusion.1), channel_id=1, source_target_pairs={{0,96},{8,104},{16,112},{24,120},{32,0},{40,8},{48,16},{56,24},{64... | collective-permute-start | bytes 393224 | tf_op jit(solution)/shard_map/ppermute | solution.py:40
  150.7 5.9 %shard_map.84 = (bf16[128,1024]{1,0:T(8,128)(2,1)S(1)}, bf16[128,1024]{1,0:T(8,128)(2,1)}, bf16[128,1024]{1,0:T(8,128)(2,1)S(1)}, bf16[128,1024]{1,0:T(8,128)(2,1)}) custom-call(s32[4]{0:T(128)S(1)} %pad_add_fusion.place, bf16[4,128,4096]{2,1,0:T(8,128)(2,1)S(1)} %bitcast.20, bf16[4,256,512]{2,1,0:T(8,128)(2,1)S(1)} %pad_maximum_fusion.refs_0_, ...), custom_call_target="tpu_custom_call" | custom-call | flops 4294967296 | bytes 12582912 | tf_op jit(solution)/shard_map/pallas_call | solution.py:347
  157.7 2.6 %collective-permute-start.40 = (bf16[128,1024]{1,0:T(8,128)(2,1)S(1)}, bf16[128,1024]{1,0:T(8,128)(2,1)S(1)}, u32[]{:S(2)}, u32[]{:S(2)}) collective-permute-start(bf16[128,1024]{1,0:T(8,128)(2,1)S(1)} %get-tuple-element.75), channel_id=1, source_target_pairs={{0,16},{8,24},{16,0},{24,8},{32,48},{40,56},{48,32},{56,40},{64,80... | collective-permute-start | bytes 786440 | tf_op jit(solution)/shard_map/ppermute | solution.py:44
  161.9 11.4 %shard_map.85 = (f32[64,512]{1,0:T(8,128)}, f32[512,4096]{1,0:T(8,128)}) custom-call(f32[64,64]{1,0:T(8,128)S(1)} %get-tuple-element.77.inverse, f32[64,512]{1,0:T(8,128)S(1)} %add_add_fusion.w, bf16[512,1024]{1,0:T(8,128)(2,1)S(1)} %shard_map.79.turned, bf16[192,4096]{1,0:T(8,128)(2,1)S(1)} %copy-done.4, f32[512,4096]{1,0:T(8,128)} %bitcast.23, ...), custom_call_target="tpu_custom_call" | custom-call | flops 5100273664 | bytes 28311552 | tf_op jit(solution)/shard_map/pallas_call | solution.py:320
  173.3 1.6 shard_map.86
  (132 shorter events, 36.8 us)
Async XLA Ops:
  7.2 67.6 %all-gather.6.cloned.1.call-start = ((), (), s32[]{:S(2)}) async-start(), calls=%async_computation.1 | async-start | bytes 5242880 | tf_op jit(solution)/shard_map/all_gather | solution.py:370
  7.9 152.5 %all-gather.4.cloned.1.call-start = ((), (), s32[]{:S(2)}) async-start(), calls=%async_computation | async-start | bytes 9437184 | tf_op jit(solution)/shard_map/all_gather | solution.py:395
  8.9 12.5 %collective-permute-start.3 = (bf16[256,512]{1,0:T(8,128)(2,1)S(1)}, bf16[256,512]{1,0:T(8,128)(2,1)S(1)}, u32[]{:S(2)}, u32[]{:S(2)}) collective-permute-start(bf16[256,512]{1,0:T(8,128)(2,1)S(1)} %constant_dynamic-slice_fusion), channel_id=1, source_target_pairs={{0,6},{1,7},{2,0},{3,1},{4,2},{5,3},{6,4},{7,5},{8,14},{9,15},{10,... | collective-permute-start | bytes 786440 | tf_op jit(solution)/shard_map/ppermute | solution.py:36
  12.3 9.1 %collective-permute-start = (bf16[256,512]{1,0:T(8,128)(2,1)S(1)}, bf16[256,512]{1,0:T(8,128)(2,1)S(1)}, u32[]{:S(2)}, u32[]{:S(2)}) collective-permute-start(bf16[256,512]{1,0:T(8,128)(2,1)S(1)} %constant_dynamic-slice_fusion), channel_id=1, source_target_pairs={{0,2},{1,3},{2,4},{3,5},{4,6},{5,7},{6,0},{7,1},{8,10},{9,11},{10,... | collective-permute-start | bytes 786440 | tf_op jit(solution)/shard_map/ppermute | solution.py:36
  12.3 9.1 %collective-permute-start.1 = (f32[64,512]{1,0:T(8,128)}, f32[64,512]{1,0:T(8,128)S(1)}, u32[]{:S(2)}, u32[]{:S(2)}) collective-permute-start(f32[64,512]{1,0:T(8,128)} %bitcast.14), channel_id=1, source_target_pairs={{0,6},{1,7},{2,0},{3,1},{4,2},{5,3},{6,4},{7,5},{8,14},{9,15},{10,... | collective-permute-start | bytes 393224 | tf_op jit(solution)/shard_map/ppermute | solution.py:36
  15.0 11.0 %collective-permute-start.5 = (f32[64,512]{1,0:T(8,128)}, f32[64,512]{1,0:T(8,128)S(1)}, u32[]{:S(2)}, u32[]{:S(2)}) collective-permute-start(f32[64,512]{1,0:T(8,128)} %bitcast.16), channel_id=1, source_target_pairs={{0,2},{1,3},{2,4},{3,5},{4,6},{5,7},{6,0},{7,1},{8,10},{9,11},{10,... | collective-permute-start | bytes 393224 | tf_op jit(solution)/shard_map/ppermute | solution.py:36
  26.1 11.3 %collective-permute-start.6 = (f32[256,512]{1,0:T(8,128)S(1)}, f32[256,512]{1,0:T(8,128)S(1)}, u32[]{:S(2)}, u32[]{:S(2)}) collective-permute-start(f32[256,512]{1,0:T(8,128)S(1)} %pad_maximum_fusion.1), channel_id=1, source_target_pairs={{0,1},{1,0},{2,3},{3,2},{4,5},{5,4},{6,7},{7,6},{8,9},{9,8},{10,11... | collective-permute-start | bytes 1572872 | tf_op jit(solution)/shard_map/ppermute | solution.py:48
  28.0 9.4 %collective-permute-start.2 = (bf16[256,512]{1,0:T(8,128)(2,1)S(1)}, bf16[256,512]{1,0:T(8,128)(2,1)S(1)}, u32[]{:S(2)}, u32[]{:S(2)}) collective-permute-start(bf16[256,512]{1,0:T(8,128)(2,1)S(1)} %constant_dynamic-slice_fusion), channel_id=1, source_target_pairs={{0,4},{1,5},{2,6},{3,7},{4,0},{5,1},{6,2},{7,3},{8,12},{9,13},{10,... | collective-permute-start | bytes 786440 | tf_op jit(solution)/shard_map/ppermute | solution.py:36
  42.4 9.3 %collective-permute-start.11 = (bf16[2,128,512]{2,1,0:T(8,128)(2,1)S(1)}, bf16[2,128,512]{2,1,0:T(8,128)(2,1)S(1)}, u32[]{:S(2)}, u32[]{:S(2)}) collective-permute-start(bf16[2,128,512]{2,1,0:T(8,128)(2,1)S(1)} %get-tuple-element.50), channel_id=1, source_target_pairs={{0,2},{1,3},{2,4},{3,5},{4,6},{5,7},{6,0},{7,1},{8,10},{9,11},{10,... | collective-permute-start | bytes 786440 | tf_op jit(solution)/shard_map/ppermute | solution.py:36
  42.5 9.3 %collective-permute-start.12 = (bf16[2,128,512]{2,1,0:T(8,128)(2,1)S(1)}, bf16[2,128,512]{2,1,0:T(8,128)(2,1)S(1)}, u32[]{:S(2)}, u32[]{:S(2)}) collective-permute-start(bf16[2,128,512]{2,1,0:T(8,128)(2,1)S(1)} %get-tuple-element.52), channel_id=1, source_target_pairs={{0,6},{1,7},{2,0},{3,1},{4,2},{5,3},{6,4},{7,5},{8,14},{9,15},{10,... | collective-permute-start | bytes 786440 | tf_op jit(solution)/shard_map/ppermute | solution.py:36
  45.2 16.6 %collective-permute-start.8 = (f32[8,4096]{1,0:T(8,128)S(1)}, f32[8,4096]{1,0:T(8,128)S(1)}, u32[]{:S(2)}, u32[]{:S(2)}) collective-permute-start(f32[8,4096]{1,0:T(8,128)S(1)} %get-tuple-element.85), channel_id=1, source_target_pairs={{0,16},{8,24},{16,0},{24,8},{32,48},{40,56},{48,32},{56,40},{64,80... | collective-permute-start | bytes 393224 | tf_op jit(solution)/shard_map/ppermute | solution.py:44
  48.9 13.0 %collective-permute-start.9 = (f32[8,4096]{1,0:T(8,128)S(1)}, f32[8,4096]{1,0:T(8,128)S(1)}, u32[]{:S(2)}, u32[]{:S(2)}) collective-permute-start(f32[8,4096]{1,0:T(8,128)S(1)} %get-tuple-element.84), channel_id=1, source_target_pairs={{0,8},{8,16},{16,24},{24,0},{32,40},{40,48},{48,56},{56,32},{64,72... | collective-permute-start | bytes 393224 | tf_op jit(solution)/shard_map/ppermute | solution.py:44
  49.7 12.2 %collective-permute-start.10 = (f32[8,4096]{1,0:T(8,128)S(1)}, f32[8,4096]{1,0:T(8,128)S(1)}, u32[]{:S(2)}, u32[]{:S(2)}) collective-permute-start(f32[8,4096]{1,0:T(8,128)S(1)} %get-tuple-element.83), channel_id=1, source_target_pairs={{0,24},{8,0},{16,8},{24,16},{32,56},{40,32},{48,40},{56,48},{64,88... | collective-permute-start | bytes 393224 | tf_op jit(solution)/shard_map/ppermute | solution.py:44
  61.9 10.8 %collective-permute-start.17 = (bf16[4,256,512]{2,1,0:T(8,128)(2,1)S(1)}, bf16[4,256,512]{2,1,0:T(8,128)(2,1)S(1)}, u32[]{:S(2)}, u32[]{:S(2)}) collective-permute-start(bf16[4,256,512]{2,1,0:T(8,128)(2,1)S(1)} %pad_maximum_fusion.refs_0_), channel_id=1, source_target_pairs={{0,1},{1,0},{2,3},{3,2},{4,5},{5,4},{6,7},{7,6},{8,9},{9,8},{10,11... | collective-permute-start | bytes 3145736 | tf_op jit(solution)/shard_map/ppermute | solution.py:48
  63.3 9.4 %collective-permute-start.16 = (bf16[2,128,512]{2,1,0:T(8,128)(2,1)S(1)}, bf16[2,128,512]{2,1,0:T(8,128)(2,1)S(1)}, u32[]{:S(2)}, u32[]{:S(2)}) collective-permute-start(bf16[2,128,512]{2,1,0:T(8,128)(2,1)S(1)} %get-tuple-element.55), channel_id=1, source_target_pairs={{0,4},{1,5},{2,6},{3,7},{4,0},{5,1},{6,2},{7,3},{8,12},{9,13},{10,... | collective-permute-start | bytes 786440 | tf_op jit(solution)/shard_map/ppermute | solution.py:36
  77.8 9.1 %collective-permute-start.21 = (f32[8,4096]{1,0:T(8,128)S(1)}, f32[8,4096]{1,0:T(8,128)S(1)}, u32[]{:S(2)}, u32[]{:S(2)}) collective-permute-start(f32[8,4096]{1,0:T(8,128)S(1)} %add_add_fusion.3), channel_id=1, source_target_pairs={{0,4},{1,5},{2,6},{3,7},{4,0},{5,1},{6,2},{7,3},{8,12},{9,13},{10,... | collective-permute-start | bytes 393224 | tf_op jit(solution)/shard_map/ppermute | solution.py:36
  89.5 23.0 %collective-permute-start.18 = (bf16[4,256,512]{2,1,0:T(8,128)(2,1)S(1)}, bf16[4,256,512]{2,1,0:T(8,128)(2,1)S(1)}, u32[]{:S(2)}, u32[]{:S(2)}) collective-permute-start(bf16[4,256,512]{2,1,0:T(8,128)(2,1)S(1)} %pad_maximum_fusion.refs_0_), channel_id=1, source_target_pairs={{0,96},{8,104},{16,112},{24,120},{32,0},{40,8},{48,16},{56,24},{64... | collective-permute-start | bytes 3145736 | tf_op jit(solution)/shard_map/ppermute | solution.py:40
  89.6 23.9 %collective-permute-start.19 = (bf16[4,256,512]{2,1,0:T(8,128)(2,1)S(1)}, bf16[4,256,512]{2,1,0:T(8,128)(2,1)S(1)}, u32[]{:S(2)}, u32[]{:S(2)}) collective-permute-start(bf16[4,256,512]{2,1,0:T(8,128)(2,1)S(1)} %pad_maximum_fusion.refs_0_), channel_id=1, source_target_pairs={{0,32},{8,40},{16,48},{24,56},{32,64},{40,72},{48,80},{56,88},{64,... | collective-permute-start | bytes 3145736 | tf_op jit(solution)/shard_map/ppermute | solution.py:40
  96.3 17.2 %collective-permute-start.28 = (f32[32,4096]{1,0:T(8,128)S(1)}, f32[32,4096]{1,0:T(8,128)S(1)}, u32[]{:S(2)}, u32[]{:S(2)}) collective-permute-start(f32[32,4096]{1,0:T(8,128)S(1)} %pad_maximum_fusion.3), channel_id=1, source_target_pairs={{0,1},{1,0},{2,3},{3,2},{4,5},{5,4},{6,7},{7,6},{8,9},{9,8},{10,11... | collective-permute-start | bytes 1572872 | tf_op jit(solution)/shard_map/ppermute | solution.py:48
  114.7 14.9 %collective-permute-start.29 = (bf16[4,256,512]{2,1,0:T(8,128)(2,1)S(1)}, bf16[4,256,512]{2,1,0:T(8,128)(2,1)S(1)}, u32[]{:S(2)}, u32[]{:S(2)}) collective-permute-start(bf16[4,256,512]{2,1,0:T(8,128)(2,1)S(1)} %collective-permute-done.18.refs_1_), channel_id=1, source_target_pairs={{0,1},{1,0},{2,3},{3,2},{4,5},{5,4},{6,7},{7,6},{8,9},{9,8},{10,11... | collective-permute-start | bytes 3145736 | tf_op jit(solution)/shard_map/ppermute | solution.py:48
  117.7 12.0 %collective-permute-start.30 = (bf16[4,256,512]{2,1,0:T(8,128)(2,1)S(1)}, bf16[4,256,512]{2,1,0:T(8,128)(2,1)S(1)}, u32[]{:S(2)}, u32[]{:S(2)}) collective-permute-start(bf16[4,256,512]{2,1,0:T(8,128)(2,1)S(1)} %collective-permute-done.19.refs_3_), channel_id=1, source_target_pairs={{0,1},{1,0},{2,3},{3,2},{4,5},{5,4},{6,7},{7,6},{8,9},{9,8},{10,11... | collective-permute-start | bytes 3145736 | tf_op jit(solution)/shard_map/ppermute | solution.py:48
  117.8 27.2 %collective-permute-start.20 = (bf16[4,256,512]{2,1,0:T(8,128)(2,1)S(1)}, bf16[4,256,512]{2,1,0:T(8,128)(2,1)S(1)}, u32[]{:S(2)}, u32[]{:S(2)}) collective-permute-start(bf16[4,256,512]{2,1,0:T(8,128)(2,1)S(1)} %pad_maximum_fusion.refs_0_), channel_id=1, source_target_pairs={{0,64},{8,72},{16,80},{24,88},{32,96},{40,104},{48,112},{56,120},{... | collective-permute-start | bytes 3145736 | tf_op jit(solution)/shard_map/ppermute | solution.py:40
  118.2 9.5 %collective-permute-start.31 = (f32[64,128]{1,0:T(8,128)S(1)}, f32[64,128]{1,0:T(8,128)S(1)}, u32[]{:S(2)}, u32[]{:S(2)}) collective-permute-start(f32[64,128]{1,0:T(8,128)S(1)} %get-tuple-element.64.u0), channel_id=1, source_target_pairs={{0,6},{1,7},{2,0},{3,1},{4,2},{5,3},{6,4},{7,5},{8,14},{9,15},{10,... | collective-permute-start | bytes 98312 | tf_op jit(solution)/shard_map/ppermute | solution.py:36
  131.8 13.1 %collective-permute-start.37 = (f32[64,512]{1,0:T(8,128)S(1)}, f32[64,512]{1,0:T(8,128)S(1)}, u32[]{:S(2)}, u32[]{:S(2)}) collective-permute-start(f32[64,512]{1,0:T(8,128)S(1)} %shard_map.82), channel_id=1, source_target_pairs={{0,24},{8,0},{16,8},{24,16},{32,56},{40,32},{48,40},{56,48},{64,88... | collective-permute-start | bytes 393224 | tf_op jit(solution)/shard_map/ppermute | solution.py:44
  134.5 10.4 %collective-permute-start.36 = (f32[64,512]{1,0:T(8,128)S(1)}, f32[64,512]{1,0:T(8,128)S(1)}, u32[]{:S(2)}, u32[]{:S(2)}) collective-permute-start(f32[64,512]{1,0:T(8,128)S(1)} %shard_map.82), channel_id=1, source_target_pairs={{0,8},{8,16},{16,24},{24,0},{32,40},{40,48},{48,56},{56,32},{64,72... | collective-permute-start | bytes 393224 | tf_op jit(solution)/shard_map/ppermute | solution.py:44
  134.5 10.4 %collective-permute-start.35 = (f32[64,512]{1,0:T(8,128)S(1)}, f32[64,512]{1,0:T(8,128)S(1)}, u32[]{:S(2)}, u32[]{:S(2)}) collective-permute-start(f32[64,512]{1,0:T(8,128)S(1)} %shard_map.82), channel_id=1, source_target_pairs={{0,16},{8,24},{16,0},{24,8},{32,48},{40,56},{48,32},{56,40},{64,80... | collective-permute-start | bytes 393224 | tf_op jit(solution)/shard_map/ppermute | solution.py:44
  146.4 13.9 %collective-permute-start.43 = (f32[64,512]{1,0:T(8,128)S(1)}, f32[64,512]{1,0:T(8,128)S(1)}, u32[]{:S(2)}, u32[]{:S(2)}) collective-permute-start(f32[64,512]{1,0:T(8,128)S(1)} %add_add_fusion.1), channel_id=1, source_target_pairs={{0,32},{8,40},{16,48},{24,56},{32,64},{40,72},{48,80},{56,88},{64,... | collective-permute-start | bytes 393224 | tf_op jit(solution)/shard_map/ppermute | solution.py:40
  146.8 13.5 %collective-permute-start.44 = (f32[64,512]{1,0:T(8,128)S(1)}, f32[64,512]{1,0:T(8,128)S(1)}, u32[]{:S(2)}, u32[]{:S(2)}) collective-permute-start(f32[64,512]{1,0:T(8,128)S(1)} %add_add_fusion.1), channel_id=1, source_target_pairs={{0,96},{8,104},{16,112},{24,120},{32,0},{40,8},{48,16},{56,24},{64... | collective-permute-start | bytes 393224 | tf_op jit(solution)/shard_map/ppermute | solution.py:40
  149.1 11.2 %collective-permute-start.42 = (f32[64,512]{1,0:T(8,128)S(1)}, f32[64,512]{1,0:T(8,128)S(1)}, u32[]{:S(2)}, u32[]{:S(2)}) collective-permute-start(f32[64,512]{1,0:T(8,128)S(1)} %add_add_fusion.1), channel_id=1, source_target_pairs={{0,64},{8,72},{16,80},{24,88},{32,96},{40,104},{48,112},{56,120},{... | collective-permute-start | bytes 393224 | tf_op jit(solution)/shard_map/ppermute | solution.py:40
  156.6 16.6 %collective-permute-start.39 = (bf16[128,1024]{1,0:T(8,128)(2,1)}, bf16[128,1024]{1,0:T(8,128)(2,1)S(1)}, u32[]{:S(2)}, u32[]{:S(2)}) collective-permute-start(bf16[128,1024]{1,0:T(8,128)(2,1)} %get-tuple-element.74), channel_id=1, source_target_pairs={{0,24},{8,0},{16,8},{24,16},{32,56},{40,32},{48,40},{56,48},{64,88... | collective-permute-start | bytes 786440 | tf_op jit(solution)/shard_map/ppermute | solution.py:44
  157.7 15.5 %collective-permute-start.40 = (bf16[128,1024]{1,0:T(8,128)(2,1)S(1)}, bf16[128,1024]{1,0:T(8,128)(2,1)S(1)}, u32[]{:S(2)}, u32[]{:S(2)}) collective-permute-start(bf16[128,1024]{1,0:T(8,128)(2,1)S(1)} %get-tuple-element.75), channel_id=1, source_target_pairs={{0,16},{8,24},{16,0},{24,8},{32,48},{40,56},{48,32},{56,40},{64,80... | collective-permute-start | bytes 786440 | tf_op jit(solution)/shard_map/ppermute | solution.py:44
  160.4 12.9 %collective-permute-start.41 = (bf16[128,1024]{1,0:T(8,128)(2,1)}, bf16[128,1024]{1,0:T(8,128)(2,1)S(1)}, u32[]{:S(2)}, u32[]{:S(2)}) collective-permute-start(bf16[128,1024]{1,0:T(8,128)(2,1)} %get-tuple-element.76), channel_id=1, source_target_pairs={{0,8},{8,16},{16,24},{24,0},{32,40},{40,48},{48,56},{56,32},{64,72... | collective-permute-start | bytes 786440 | tf_op jit(solution)/shard_map/ppermute | solution.py:44
  (34 other events, 367.5 us)
Sparse Core Ops, SparseCore 0:
  9.7 57.3 all-gather.5
  74.9 48.3 all-gather.3

commit v2 on v1

v2 whole, which is shorter than its diff:
```python
import functools

import jax
import jax.numpy as jnp
from jax import lax
from jax.experimental import pallas as pl
from jax.experimental.pallas import tpu as pltpu
from jax.sharding import PartitionSpec as P

F32, BF16 = jnp.float32, jnp.bfloat16
VMEM = pl.BlockSpec(memory_space=pltpu.VMEM)
SMEM = pl.BlockSpec(memory_space=pltpu.SMEM)
HBM = pl.BlockSpec(memory_space=pltpu.HBM)
RELATIVE = [(a, d) for a in range(2) for d in range(4)]
NT = (((1,), (1,)), ((), ()))
NN = (((1,), (0,)), ((), ()))


def mm(lhs, rhs, dims=NN, precision=None):
    return lax.dot_general(lhs, rhs, dims, precision=precision, preferred_element_type=F32)


def halves(value):
    high = value.astype(BF16)
    return high, (value - high.astype(F32)).astype(BF16)


def thirds(value):
    high = value.astype(BF16)
    rest = value - high.astype(F32)
    mid = rest.astype(BF16)
    return high, mid, (rest - mid.astype(F32)).astype(BF16)


def along_x(value, d):
    return lax.ppermute(value, "fsdp", [(i, ((i // 2 + d) % 4) * 2 + i % 2) for i in range(8)])


def along_y(value, d):
    return lax.ppermute(value, "dp", [(i, ((i // 4 + d) % 4) * 4 + i % 4) for i in range(16)])


def along_z(value, d):
    return lax.ppermute(value, "dp", [(i, (i // 4) * 4 + (i % 4 + d) % 4) for i in range(16)])


def other_core(value):
    return lax.ppermute(value, "fsdp", [(i, i ^ 1) for i in range(8)])


def to_relative(value, a, d):
    return lax.ppermute(value, "fsdp", [(i, ((i // 2 + d) % 4) * 2 + (i % 2 ^ a)) for i in range(8)])


def pallas(body, out_shape, mib=16, **kw):
    return pl.pallas_call(
        body,
        out_shape=out_shape,
        compiler_params=pltpu.CompilerParams(vmem_limit_bytes=mib * 2**20),
        cost_estimate=pl.CostEstimate(flops=0, bytes_accessed=0, transcendentals=0),
        **kw,
    )


def in_hbm(value):
    return pltpu.with_memory_space_constraint(value, pltpu.HBM)


def shaped(shape, dtype=F32):
    return jax.ShapeDtypeStruct(shape, dtype)


def after(value, *earlier):
    return lax.optimization_barrier((value, *earlier))[0]


def chunk_of(x, c, a, d):
    return lax.rem(x + d, 4) * 2 + (c ^ a)


def rank_row(y, c, a, d):
    return pl.multiple_of((c ^ a) * 32 + lax.rem(y + d, 4) * 8, 8)


def cut_body(place, grad, *outs):
    x, c = place[0], place[1]
    for d, out in enumerate(outs):
        for a in range(2):
            out[a] = grad[:, pl.ds(pl.multiple_of(chunk_of(x, c, a, d) * 512, 512), 512)]


def cut(place, grad):
    return pallas(cut_body, [shaped((2, 128, 512), BF16)] * 4, in_specs=[SMEM, VMEM], out_specs=[VMEM] * 4)(place, grad)


def sort_body(c0, c1, c2, c3, near, far, done):
    copies = []
    for d, chunk in enumerate((c0, c1, c2, c3)):
        for a, out in enumerate((near, far)):
            copies.append(pltpu.make_async_copy(chunk.at[a], out.at[d], done.at[a, d]))
            copies[-1].start()
    for copy in copies:
        copy.wait()


def sort(chunks):
    return pallas(
        sort_body,
        [shaped((4, 128, 512), BF16)] * 2,
        in_specs=[HBM] * 4,
        out_specs=[VMEM] * 2,
        scratch_shapes=[pltpu.SemaphoreType.DMA((2, 4))],
    )(*[in_hbm(chunk) for chunk in chunks])


def columns(i, blocks=4):
    return slice(4096 // blocks * i, 4096 // blocks * (i + 1))


class Fetch:
    def __init__(self, source, held, arrived, ahead, blocks=4):
        parts = [columns(i, blocks) for i in range(blocks)]
        self.copies = [pltpu.make_async_copy(source.at[:, at], held.at[:, at], arrived.at[i]) for i, at in enumerate(parts)]
        self.ahead = ahead
        for copy in self.copies[:ahead]:
            copy.start()

    def wait(self, i):
        if i + self.ahead < len(self.copies):
            self.copies[i + self.ahead].start()
        self.copies[i].wait()


def error_left_body(place, qt, error, out, held, arrived, pieces):
    c, y = place[1], place[2]
    blocks = Fetch(error, held, arrived, 3)
    for n, (a, d) in enumerate(RELATIVE):
        rows = qt[pl.ds(rank_row(y, c, a, d), 8), :]
        high = rows.astype(BF16).astype(F32)
        pieces[8 * n : 8 * n + 8, :] = high
        pieces[64 + 8 * n : 72 + 8 * n, :] = rows - high
    q = pieces[...].astype(BF16)
    for i in range(4):
        blocks.wait(i)
        high, low = halves(held[:, columns(i)])
        first = mm(q, high)
        out[:, columns(i)] = first[:64] + first[64:] + mm(q[:64], low)


def error_left(place, qt, error):
    return pallas(
        error_left_body,
        shaped((64, 4096)),
        in_specs=[SMEM, VMEM, HBM],
        out_specs=VMEM,
        scratch_shapes=[pltpu.VMEM((512, 4096), F32), pltpu.SemaphoreType.DMA((4,)), pltpu.VMEM((128, 512), F32)],
    )(place, qt, in_hbm(error))


def left_body(place, q0, q1, q2, q3, q_far, grad, ctx, term, near, far, g_abs, g_rel):
    x, c, y = place[0], place[1], place[2]
    total = jnp.zeros((64, 128), F32)
    for a, d in RELATIVE:
        q = (q0, q1, q2, q3)[d][...] if a == 0 else q_far[64 * d : 64 * d + 64, :]
        chunk = grad[:, pl.ds(pl.multiple_of(chunk_of(x, c, a, d) * 512, 512), 512)]
        parts = mm(jnp.concatenate(thirds(q), 0), chunk, NT)
        total += parts[:64] + parts[64:128] + parts[128:]
    g_abs[...] = total
    for n, (a, d) in enumerate(RELATIVE):
        g_rel[8 * n : 8 * n + 8, :] = g_abs[pl.ds(rank_row(y, c, a, d), 8), :]
    g = jnp.concatenate(thirds(g_rel[...]), 0)
    for i in range(4):
        at = slice(1024 * i, 1024 * i + 1024)
        parts = mm(g, ctx[:, at])
        whole = term[:, at] + (parts[:64] + parts[64:128] + parts[128:])
        near[:, at] = whole[:32]
        far[:, at] = whole[32:]


def left(place, q_near, q_far, grad, ctx, term):
    return pallas(
        left_body,
        [shaped((32, 4096))] * 2,
        in_specs=[SMEM] + [VMEM] * 8,
        out_specs=[VMEM] * 2,
        scratch_shapes=[pltpu.VMEM((64, 128), F32)] * 2,
    )(place, *q_near, q_far, grad, ctx, term)


def join_body(place, v0, v1, v2, v3, out, done):
    copies = []
    for d, value in enumerate((v0, v1, v2, v3)):
        at = pl.ds(pl.multiple_of(lax.rem(place[3] + d, 4) * 1024, 1024), 1024)
        copies.append(pltpu.make_async_copy(value, out.at[:, at], done.at[d]))
        copies[-1].start()
    for copy in copies:
        copy.wait()


def join(place, values):
    return pallas(
        join_body,
        shaped((128, 4096), BF16),
        in_specs=[SMEM] + [VMEM] * 4,
        out_specs=HBM,
        scratch_shapes=[pltpu.SemaphoreType.DMA((4,))],
    )(place, *values)


def turn_body(place, near, far, out):
    x, c = place[0], place[1]
    for a, d in RELATIVE:
        chunk = far[d] if a else near[d]
        out[:, pl.ds(pl.multiple_of(chunk_of(x, c, a, 4 - d) * 128, 128), 128)] = chunk.T


def turn(place, near, far):
    return pallas(
        turn_body, shaped((512, 1024), BF16), in_specs=[SMEM, VMEM, VMEM], out_specs=VMEM
    )(place, near, far)


def middle_body(place, p0, p1, p2, p3, p_far, ctx, p_out, u_out):
    c, y = place[1], place[2]
    for a, d in RELATIVE:
        p_out[pl.ds(rank_row(y, c, a, d), 8), :] = (p0, p1, p2, p3)[d][...] if a == 0 else p_far[8 * d : 8 * d + 8, :]
    u = jnp.zeros((64, 128), F32)
    for i in range(4):
        at = slice(1024 * i, 1024 * i + 1024)
        parts = mm(jnp.concatenate(thirds(p_out[:, at]), 0), ctx[:, at], NT)
        u += parts[:64] + parts[64:128] + parts[128:]
    u_out[...] = u


def middle(place, p_near, p_far, ctx):
    return pallas(
        middle_body,
        [shaped((64, 4096)), shaped((64, 128))],
        in_specs=[SMEM] + [VMEM] * 6,
        out_specs=[VMEM] * 2,
    )(place, *p_near, p_far, ctx)


def right_body(p_raw, error, out, held, arrived):
    blocks = Fetch(error, held, arrived, 3)
    for i in range(4):
        high, low = halves(p_raw[:, columns(i)])
        blocks.wait(i)
        e_high, e_low = halves(held[:, columns(i)])
        parts = mm(e_high, jnp.concatenate([high, low], 0), NT)
        part = parts[:, :64] + parts[:, 64:] + mm(e_low, high, NT)
        if i == 0:
            out[...] = part
        else:
            out[...] += part


def right(p_raw, error):
    return pallas(
        right_body,
        shaped((512, 64)),
        in_specs=[VMEM, HBM],
        out_specs=VMEM,
        scratch_shapes=[pltpu.VMEM((512, 4096), F32), pltpu.SemaphoreType.DMA((4,))],
    )(p_raw, in_hbm(error))


def collect_body(place, term, turned, u0, u1, u2, u3, u_far, out, u_all):
    x, c = place[0], place[1]
    for a, d in RELATIVE:
        u = (u0, u1, u2, u3)[d][...] if a == 0 else u_far[64 * d : 64 * d + 64, :]
        first = pl.multiple_of(chunk_of(x, c, a, d) * 128, 128)
        for n, part in enumerate(thirds(u)):
            u_all[64 * n : 64 * n + 64, pl.ds(first, 128)] = part
    parts = mm(u_all[...], turned[...], NT)
    out[...] = term[...].T + (parts[:64] + parts[64:128] + parts[128:])


def collect(place, term, turned, u_near, u_far):
    return pallas(
        collect_body,
        shaped((64, 512)),
        in_specs=[SMEM] + [VMEM] * 7,
        out_specs=VMEM,
        scratch_shapes=[pltpu.VMEM((192, 1024), BF16)],
    )(place, term, turned, *u_near, u_far)


def solve_body(p_raw, inverse, out, p, left_here):
    squares = jnp.zeros((192, 192), F32)
    for i in range(4):
        stack = jnp.concatenate(thirds(p_raw[:, 1024 * i : 1024 * i + 1024]), 0)
        squares += mm(stack, stack, NT)
    gram = squares[:64, :64] + (
        (squares[:64, 64:128] + squares[64:128, :64]) + (squares[:64, 128:] + squares[128:, :64] + squares[64:128, 64:128])
    )
    same = lax.broadcasted_iota(jnp.int32, (64, 64), 0) == lax.broadcasted_iota(jnp.int32, (64, 64), 1)
    row = lax.broadcasted_iota(jnp.int32, (64, 128), 0)
    both = jnp.concatenate([gram, jnp.where(same, 1.0, 0.0).astype(F32)], 1)
    for k in range(64):
        scale = both[:, k : k + 1] / both[k : k + 1, k : k + 1]
        both = both - jnp.where(row > k, scale * both[k : k + 1, :], 0.0)
    diagonal = jnp.sum(jnp.where(same, both[:, :64], 0.0), 1, keepdims=True)
    solved = both[:, 64:] / jnp.sqrt(diagonal)
    inverse[...] = solved
    high, low = halves(solved)
    solved_split = jnp.concatenate([high, high, low], 1)
    for i in range(4):
        at = slice(1024 * i, 1024 * i + 1024)
        high, low = halves(p_raw[:, at])
        high, low = halves(mm(solved_split, jnp.concatenate([high, low, high], 0)))
        p[:, at] = jnp.concatenate([high, low, high], 0)
        pltpu.make_async_copy(p.at[:, at], out.at[:, at], left_here.at[i]).start()
    for i in range(4):
        at = slice(1024 * i, 1024 * i + 1024)
        pltpu.make_async_copy(p.at[:, at], out.at[:, at], left_here.at[i]).wait()


def solve(p_raw):
    return pallas(
        solve_body,
        [shaped((64, 64)), pltpu.HBM((192, 4096), BF16)],
        in_specs=[VMEM],
        out_specs=[VMEM, HBM],
        scratch_shapes=[pltpu.VMEM((192, 4096), BF16), pltpu.SemaphoreType.DMA((4,))],
    )(p_raw)


def last_body(inverse, w, turned, p_far, error, ctx, q_out, out, p, held, held_ctx, arrived, arrived_ctx, left_here, p_here):
    ctx_blocks, blocks = Fetch(ctx, held_ctx, arrived_ctx, 2, 8), Fetch(error, held, arrived, 2, 8)
    p_copy = pltpu.make_async_copy(p_far, p, p_here)
    p_copy.start()
    ctx_blocks.wait(0)
    product = mm(turned[...], held_ctx[:, columns(0, 8)])
    q = mm(inverse[...], w[...], NN, lax.Precision.HIGHEST) * (1.0 / 16)
    q_out[...] = q
    high, low = halves(q)
    q_split = jnp.concatenate([high, high, low], 0).T
    p_copy.wait()
    stores = []
    for i in range(8):
        at = columns(i, 8)
        approx = mm(q_split, p[:, at])
        blocks.wait(i)
        held[:, at] = (held[:, at] + product) - approx
        stores.append(pltpu.make_async_copy(held.at[:, at], out.at[:, at], left_here.at[i]))
        stores[-1].start()
        if i < 7:
            ctx_blocks.wait(i + 1)
            product = mm(turned[...], held_ctx[:, columns(i + 1, 8)])
    for store in stores:
        store.wait()


def last(inverse, w, turned, p, error, ctx):
    return pallas(
        last_body,
        [shaped((64, 512)), shaped((512, 4096))],
        mib=24,
        in_specs=[VMEM] * 3 + [HBM] * 3,
        out_specs=[VMEM, HBM],
        scratch_shapes=[pltpu.VMEM((192, 4096), BF16), pltpu.VMEM((512, 4096), F32), pltpu.VMEM((1024, 4096), BF16)]
        + [pltpu.SemaphoreType.DMA((8,))] * 3
        + [pltpu.SemaphoreType.DMA],
    )(inverse, w, turned, in_hbm(p), in_hbm(error), in_hbm(ctx))


def share_body(place, tokens, *refs):
    slabs, outs, whole = refs[:8], refs[8:12], refs[12]
    x, c, y, z = place[0], place[1], place[2], place[3]
    for e in range(4):
        total = jnp.zeros((512, 256), F32)
        for a in range(2):
            for d in range(4):
                at = pl.ds(pl.multiple_of(chunk_of(x, c, a, 4 - d) * 512, 512), 512)
                total += mm(tokens[:, :, at].reshape(512, 512), slabs[4 * a + e][d], NT)
        whole[:, pl.ds(pl.multiple_of(lax.rem(y + e, 4) * 256, 256), 256)] = total.astype(BF16)
    for d, out in enumerate(outs):
        out[...] = whole[pl.ds(pl.multiple_of(lax.rem(z + d, 4) * 128, 128), 128), :]


def share(place, tokens, mine, theirs):
    return pallas(
        share_body,
        [shaped((128, 1024), BF16)] * 4,
        mib=24,
        in_specs=[SMEM] + [VMEM] * 9,
        out_specs=[VMEM] * 4,
        scratch_shapes=[pltpu.VMEM((512, 1024), BF16)],
    )(place, tokens, *mine, *theirs)


def pair_sum(values):
    return (values[0] + values[2]) + (values[1] + values[3])


def local(ctx, grad_out, weight, error, q_init):
    j, k = lax.axis_index("fsdp"), lax.axis_index("dp")
    x, c, y, z = j // 2, j % 2, k // 4, k % 4
    place = jnp.stack([x, c, y, z]).astype(jnp.int32)
    error = error[0]

    groups = [[e * 4 + f for f in range(4)] for e in range(4)]
    tokens = lax.all_gather(grad_out, "dp", axis_index_groups=groups)

    qt = q_init.T
    q_near = [qt] + [along_x(qt, -d) for d in (1, 2, 3)]
    piece = lax.dynamic_slice_in_dim(weight, z * 1024 + y * 256, 256, 0)
    pieces = [piece, along_x(piece, 1), along_x(after(piece, q_near[1]), 2), along_x(piece, 3)]
    term = error_left(place, qt, error)
    q_far = other_core(jnp.concatenate([qt, after(q_near[1], term, pieces[1], pieces[3]), *q_near[2:]], 0))
    sends = cut(place, grad_out)
    near, far = left(place, q_near, q_far, grad_out, ctx, term)
    chunks = [sends[0]] + [along_x(after(sends[d], *q_near), d) if d != 2 else None for d in (1, 2, 3)]
    half = near + other_core(far)

    chunks[2] = along_x(after(sends[2], half), 2)
    blocks = [half[:8]] + [along_y(half[8 * d : 8 * d + 8], d) for d in (1, 2, 3)]
    blocks[3] = after(blocks[3], pieces[2], chunks[1], chunks[3])
    summed = pair_sum(blocks)
    w0 = after(jnp.stack(pieces), summed)
    w1, w3 = [along_y(w0, d) for d in (-1, 1)]
    over_x = [summed] + [along_x(summed, d) for d in (1, 2, 3)]
    over_x[3] = after(over_x[3], chunks[2])
    summed = pair_sum(over_x)
    near_columns, far_columns = sort([*chunks[:3], after(chunks[3], summed)])
    far_columns = other_core(far_columns)
    turned = turn(place, near_columns, far_columns)
    over_z = [summed] + [along_z(summed, d) for d in (1, 2, 3)]
    over_z[3] = after(over_z[3], w1, w3, turned)
    rows = pair_sum(over_z)
    ctx_all = lax.all_gather(after(ctx, rows, tokens), "fsdp", axis=0, tiled=True)
    p_near = [rows] + [along_y(rows, -d) for d in (1, 2, 3)]
    their1, their3 = other_core(after(w1, rows)), other_core(after(w3, rows))
    p_far = other_core(jnp.concatenate([rows, after(p_near[1], their1, their3), *p_near[2:]], 0))
    w2 = along_y(after(w0, *p_near), 2)

    p_raw, u = middle(place, p_near, p_far, ctx)
    u_near = [u] + [along_x(u, -d) for d in (1, 2, 3)]
    w_term = right(p_raw, error)
    their0 = other_core(after(w0, u))
    u_far = other_core(jnp.concatenate([u, u_near[1], u_near[2], after(u_near[3], w_term, their0)], 0))
    w = collect(place, w_term, turned, u_near, u_far)
    w = [w] + [along_z(w, d) for d in (1, 2, 3)]
    inverse, p = solve(p_raw)
    w = pair_sum([w[0], w[1], w[2], after(w[3], p, w2)])
    their2 = other_core(after(w2, w))
    w = [w] + [along_y(w, d) for d in (1, 2, 3)]
    outs = share(place, tokens, [w0, w1, w2, w3], [their0, their1, their2, their3])
    w = pair_sum([w[0], w[1], w[2], after(w[3], outs[0])])
    outs = [outs[0]] + [along_z(outs[d], d) for d in (1, 2, 3)]
    q_factor, new_error = last(inverse, w, turned, p, error, ctx_all)
    grad_ctx = join(place, [outs[0], outs[3], outs[2], after(outs[1], q_factor)])
    return (grad_ctx, q_factor.T, new_error[None])


def solution(mesh):
    in_specs = (
        P(("dp", "fsdp"), None),
        P(("dp", "fsdp"), None),
        P(None, "fsdp"),
        P("dp", "fsdp", None),
        P("fsdp", None),
    )
    out_specs = (P(("dp", "fsdp"), None), P("fsdp", None), P("dp", "fsdp", None))
    return jax.shard_map(local, mesh=mesh, in_specs=in_specs, out_specs=out_specs, check_vma=False)
```

time: 182 us -> 164 us (0.901)
  waiting for transfers between devices: 56.3 us -> 41 us
  local copies, waits for them, and re-layouts: 9.69 us -> 3.87 us
  starting transfers between devices: 57.7 us -> 59.9 us
    ppermute x12 -> x9, waiting for transfers between devices: 15.5 us -> 0.71 us  [along_z(): lax.ppermute(value, 'dp', [(i, i // 4 * 4 + (i % 4 + d) % 4) for i in ran...]
    unnamed x38 -> x26, local copies, waits for them, and re-layouts: 7.67 us -> 1.9 us
    ppermute x9 -> x12, starting transfers between devices: 10.5 us -> 16.2 us  [along_y(): lax.ppermute(value, 'dp', [(i, (i // 4 + d) % 4 * 4 + i % 4) for i in ran...]
    ppermute x15, waiting for transfers between devices: 21.5 us -> 16.7 us  [along_x(): lax.ppermute(value, 'fsdp', [(i, (i // 2 + d) % 4 * 2 + i % 2) for i in r...]
    ppermute x9, starting transfers between devices: 13.9 us -> 10.4 us  [other_core(): return lax.ppermute(value, 'fsdp', [(i, i ^ 1) for i in range(8)])]
    ppermute x9, waiting for transfers between devices: 1 us -> 4.1 us  [other_core(): return lax.ppermute(value, 'fsdp', [(i, i ^ 1) for i in range(8)])]
    ppermute x12 -> x9, starting transfers between devices: 16.7 us -> 13.7 us  [along_z(): lax.ppermute(value, 'dp', [(i, i // 4 * 4 + (i % 4 + d) % 4) for i in ran...]
    ppermute x15, starting transfers between devices: 16.5 us -> 19.5 us  [along_x(): lax.ppermute(value, 'fsdp', [(i, (i // 2 + d) % 4 * 2 + i % 2) for i in r...]
  transfers between devices with their start and end apart: 47 -> 47, of which waited for: 16 -> 17; matrix products, arithmetic and copies ran while one was open for 1% -> 2% of each run, Pallas kernels for 23% -> 26%
where the time goes in v2:
time: 164 us; the launch traced here: 163 us
  starting transfers between devices  59.9 us (37%)
  Pallas kernels  43.6 us (27%)
  waiting for transfers between devices  41 us (25%)
  between operations  14.5 us (9%)
  local copies, waits for them, and re-layouts  3.87 us (2%)
    ppermute x15, starting transfers between devices, along_x(): lax.ppermute(value, 'fsdp', [(i, (i // 2 + d) % 4 * 2 + i % 2) for i in r...  19.5 us
    ppermute x12, waiting for transfers between devices, along_y(): lax.ppermute(value, 'dp', [(i, (i // 4 + d) % 4 * 4 + i % 4) for i in ran...  18.7 us
    ppermute x15, waiting for transfers between devices, along_x(): lax.ppermute(value, 'fsdp', [(i, (i // 2 + d) % 4 * 2 + i % 2) for i in r...  16.7 us
    ppermute x12, starting transfers between devices, along_y(): lax.ppermute(value, 'dp', [(i, (i // 4 + d) % 4 * 4 + i % 4) for i in ran...  16.2 us
    ppermute x9, starting transfers between devices, along_z(): lax.ppermute(value, 'dp', [(i, i // 4 * 4 + (i % 4 + d) % 4) for i in ran...  13.7 us
    pallas_call x1, Pallas kernels, last(): pallas(last_body, [shaped((64, 512)), shaped((512, 4096))], mib=24, in_sp...  12 us
    ppermute x9, starting transfers between devices, other_core(): return lax.ppermute(value, 'fsdp', [(i, i ^ 1) for i in range(8)])  10.4 us
    pallas_call x1, Pallas kernels, solve(): pallas(solve_body, [shaped((64, 64)), pltpu.HBM((192, 4096), BF16)], in_s...  7.73 us
  transfers between devices with their start and end apart: 47, of which 17 were waited for; matrix products, arithmetic and copies ran while one was open for 2% of the time, Pallas kernels for 26%

profile of v2, /device:TPU:1, one launch (start us, length us, event | category | flops | bytes accessed | tf_op | source)
XLA Modules:
  0.0 163.3 jit_solution(4149991325473243725)
XLA Ops:
  8.9 3.4 %collective-permute-start.3 = (bf16[256,512]{1,0:T(8,128)(2,1)S(1)}, bf16[256,512]{1,0:T(8,128)(2,1)S(1)}, u32[]{:S(2)}, u32[]{:S(2)}) collective-permute-start(bf16[256,512]{1,0:T(8,128)(2,1)S(1)} %constant_dynamic-slice_fusion), channel_id=1, source_target_pairs={{0,6},{1,7},{2,0},{3,1},{4,2},{5,3},{6,4},{7,5},{8,14},{9,15},{10,... | collective-permute-start | bytes 786440 | tf_op jit(solution)/shard_map/ppermute | solution.py:36
  12.3 2.7 %collective-permute-start.1 = (f32[64,512]{1,0:T(8,128)}, f32[64,512]{1,0:T(8,128)S(1)}, u32[]{:S(2)}, u32[]{:S(2)}) collective-permute-start(f32[64,512]{1,0:T(8,128)} %bitcast.15), channel_id=1, source_target_pairs={{0,6},{1,7},{2,0},{3,1},{4,2},{5,3},{6,4},{7,5},{8,14},{9,15},{10,... | collective-permute-start | bytes 393224 | tf_op jit(solution)/shard_map/ppermute | solution.py:36
  16.6 4.6 %shard_map.76.term = f32[64,4096]{1,0:T(8,128)S(1)} custom-call(s32[4]{0:T(128)S(1)} %pad_add_fusion.place, f32[64,512]{1,0:T(8,128)S(1)} %bitcast.18, f32[512,4096]{1,0:T(8,128)} %bitcast.21), custom_call_target="tpu_custom_call" | custom-call | tf_op jit(solution)/shard_map/pallas_call | solution.py:151
  22.0 4.0 %collective-permute-done.5.q3 = f32[64,512]{1,0:T(8,128)S(1)} collective-permute-done((f32[64,512]{1,0:T(8,128)}, f32[64,512]{1,0:T(8,128)S(1)}, u32[]{:S(2)}, u32[]{:S(2)}) %collective-permute-start.5) | collective-permute-done | bytes 131104 | tf_op jit(solution)/shard_map/ppermute | solution.py:36
  26.0 1.9 %collective-permute-start.6 = (f32[256,512]{1,0:T(8,128)S(1)}, f32[256,512]{1,0:T(8,128)S(1)}, u32[]{:S(2)}, u32[]{:S(2)}) collective-permute-start(f32[256,512]{1,0:T(8,128)S(1)} %pad_maximum_fusion.1), channel_id=1, source_target_pairs={{0,1},{1,0},{2,3},{3,2},{4,5},{5,4},{6,7},{7,6},{8,9},{9,8},{10,11... | collective-permute-start | bytes 1572872 | tf_op jit(solution)/shard_map/ppermute | solution.py:48
  29.5 2.4 %shard_map.77 = (f32[32,4096]{1,0:T(8,128)S(1)}, f32[32,4096]{1,0:T(8,128)S(1)}) custom-call(s32[4]{0:T(128)S(1)} %pad_add_fusion.place, f32[64,512]{1,0:T(8,128)S(1)} %bitcast.20, f32[64,512]{1,0:T(8,128)S(1)} %collective-permute-done.1.q1, f32[64,512]{1,0:T(8,128)S(1)} %collective-permute-done.4.q2, f32[64,512]{1,0:T(8,128)S(1)} %collective-permute-done.5.q3, ...), custom_call_target="tpu_custom_call" | custom-call | tf_op jit(solution)/shard_map/pallas_call | solution.py:181
  33.8 2.2 %collective-permute-start.12 = (bf16[2,128,512]{2,1,0:T(8,128)(2,1)S(1)}, bf16[2,128,512]{2,1,0:T(8,128)(2,1)S(1)}, u32[]{:S(2)}, u32[]{:S(2)}) collective-permute-start(bf16[2,128,512]{2,1,0:T(8,128)(2,1)S(1)} %get-tuple-element.49), channel_id=1, source_target_pairs={{0,6},{1,7},{2,0},{3,1},{4,2},{5,3},{6,4},{7,5},{8,14},{9,15},{10,... | collective-permute-start | bytes 786440 | tf_op jit(solution)/shard_map/ppermute | solution.py:36
  36.0 2.8 %collective-permute-start.10 = (f32[8,4096]{1,0:T(8,128)S(1)}, f32[8,4096]{1,0:T(8,128)S(1)}, u32[]{:S(2)}, u32[]{:S(2)}) collective-permute-start(f32[8,4096]{1,0:T(8,128)S(1)} %get-tuple-element.81), channel_id=1, source_target_pairs={{0,96},{8,104},{16,112},{24,120},{32,0},{40,8},{48,16},{56,24},{64... | collective-permute-start | bytes 393224 | tf_op jit(solution)/shard_map/ppermute | solution.py:40
  39.2 3.3 %collective-permute-done.2 = bf16[256,512]{1,0:T(8,128)(2,1)S(1)} collective-permute-done((bf16[256,512]{1,0:T(8,128)(2,1)S(1)}, bf16[256,512]{1,0:T(8,128)(2,1)S(1)}, u32[]{:S(2)}, u32[]{:S(2)}) %collective-permute-start.2) | collective-permute-done | bytes 262176 | tf_op jit(solution)/shard_map/ppermute | solution.py:36
  44.7 3.5 %collective-permute-done.11.c1 = bf16[2,128,512]{2,1,0:T(8,128)(2,1)S(1)} collective-permute-done((bf16[2,128,512]{2,1,0:T(8,128)(2,1)S(1)}, bf16[2,128,512]{2,1,0:T(8,128)(2,1)S(1)}, u32[]{:S(2)}, u32[]{:S(2)}) %collective-permute-start.11) | collective-permute-done | bytes 262176 | tf_op jit(solution)/shard_map/ppermute | solution.py:36
  49.2 2.2 %collective-permute-start.16 = (f32[8,4096]{1,0:T(8,128)S(1)}, f32[8,4096]{1,0:T(8,128)S(1)}, u32[]{:S(2)}, u32[]{:S(2)}) collective-permute-start(f32[8,4096]{1,0:T(8,128)S(1)} %fusion), channel_id=1, source_target_pairs={{0,6},{1,7},{2,0},{3,1},{4,2},{5,3},{6,4},{7,5},{8,14},{9,15},{10,... | collective-permute-start | bytes 393224 | tf_op jit(solution)/shard_map/ppermute | solution.py:36
  52.9 2.8 %collective-permute-start.13 = (bf16[4,256,512]{2,1,0:T(8,128)(2,1)S(1)}, bf16[4,256,512]{2,1,0:T(8,128)(2,1)S(1)}, u32[]{:S(2)}, u32[]{:S(2)}) collective-permute-start(bf16[4,256,512]{2,1,0:T(8,128)(2,1)S(1)} %pad_maximum_fusion.refs_0_), channel_id=1, source_target_pairs={{0,96},{8,104},{16,112},{24,120},{32,0},{40,8},{48,16},{56,24},{64... | collective-permute-start | bytes 3145736 | tf_op jit(solution)/shard_map/ppermute | solution.py:40
  55.7 2.2 %collective-permute-done.16 = f32[8,4096]{1,0:T(8,128)S(1)} collective-permute-done((f32[8,4096]{1,0:T(8,128)S(1)}, f32[8,4096]{1,0:T(8,128)S(1)}, u32[]{:S(2)}, u32[]{:S(2)}) %collective-permute-start.16) | collective-permute-done | bytes 131104 | tf_op jit(solution)/shard_map/ppermute | solution.py:36
  57.9 1.8 %collective-permute-start.21 = (bf16[4,256,512]{2,1,0:T(8,128)(2,1)S(1)}, bf16[4,256,512]{2,1,0:T(8,128)(2,1)S(1)}, u32[]{:S(2)}, u32[]{:S(2)}) collective-permute-start(bf16[4,256,512]{2,1,0:T(8,128)(2,1)S(1)} %pad_maximum_fusion.refs_0_), channel_id=1, source_target_pairs={{0,32},{8,40},{16,48},{24,56},{32,64},{40,72},{48,80},{56,88},{64,... | collective-permute-start | bytes 3145736 | tf_op jit(solution)/shard_map/ppermute | solution.py:40
  59.7 2.0 %collective-permute-done.15 = f32[8,4096]{1,0:T(8,128)S(1)} collective-permute-done((f32[8,4096]{1,0:T(8,128)S(1)}, f32[8,4096]{1,0:T(8,128)S(1)}, u32[]{:S(2)}, u32[]{:S(2)}) %collective-permute-start.15) | collective-permute-done | bytes 131104 | tf_op jit(solution)/shard_map/ppermute | solution.py:36
  64.0 1.5 collective-permute-start.22
  65.6 3.8 %collective-permute-start.20 = (f32[8,4096]{1,0:T(8,128)S(1)}, f32[8,4096]{1,0:T(8,128)S(1)}, u32[]{:S(2)}, u32[]{:S(2)}) collective-permute-start(f32[8,4096]{1,0:T(8,128)S(1)} %add_add_fusion.3), channel_id=1, source_target_pairs={{0,24},{8,0},{16,8},{24,16},{32,56},{40,32},{48,40},{56,48},{64,88... | collective-permute-start | bytes 393224 | tf_op jit(solution)/shard_map/ppermute | solution.py:44
  72.2 4.2 %collective-permute-done.13.refs_1_ = bf16[4,256,512]{2,1,0:T(8,128)(2,1)S(1)} collective-permute-done((bf16[4,256,512]{2,1,0:T(8,128)(2,1)S(1)}, bf16[4,256,512]{2,1,0:T(8,128)(2,1)S(1)}, u32[]{:S(2)}, u32[]{:S(2)}) %collective-permute-start.13) | collective-permute-done | bytes 1048608 | tf_op jit(solution)/shard_map/ppermute | solution.py:40
  76.4 5.8 %collective-permute-done.21.refs_3_ = bf16[4,256,512]{2,1,0:T(8,128)(2,1)S(1)} collective-permute-done((bf16[4,256,512]{2,1,0:T(8,128)(2,1)S(1)}, bf16[4,256,512]{2,1,0:T(8,128)(2,1)S(1)}, u32[]{:S(2)}, u32[]{:S(2)}) %collective-permute-start.21) | collective-permute-done | bytes 1048608 | tf_op jit(solution)/shard_map/ppermute | solution.py:40
  83.3 3.2 %collective-permute-start.27 = (bf16[4,256,512]{2,1,0:T(8,128)(2,1)}, bf16[4,256,512]{2,1,0:T(8,128)(2,1)S(1)}, u32[]{:S(2)}, u32[]{:S(2)}) collective-permute-start(bf16[4,256,512]{2,1,0:T(8,128)(2,1)} %copy-done.5), channel_id=1, source_target_pairs={{0,1},{1,0},{2,3},{3,2},{4,5},{5,4},{6,7},{7,6},{8,9},{9,8},{10,11... | collective-permute-start | bytes 3145736 | tf_op jit(solution)/shard_map/ppermute | solution.py:48
  89.1 2.1 %collective-permute-done.23.p1 = f32[8,4096]{1,0:T(8,128)S(1)} collective-permute-done((f32[8,4096]{1,0:T(8,128)S(1)}, f32[8,4096]{1,0:T(8,128)S(1)}, u32[]{:S(2)}, u32[]{:S(2)}) %collective-permute-start.23) | collective-permute-done | bytes 131104 | tf_op jit(solution)/shard_map/ppermute | solution.py:40
  91.3 2.6 %collective-permute-done.24.p2 = f32[8,4096]{1,0:T(8,128)S(1)} collective-permute-done((f32[8,4096]{1,0:T(8,128)S(1)}, f32[8,4096]{1,0:T(8,128)S(1)}, u32[]{:S(2)}, u32[]{:S(2)}) %collective-permute-start.24) | collective-permute-done | bytes 131104 | tf_op jit(solution)/shard_map/ppermute | solution.py:40
  93.9 3.9 %collective-permute-done.25.p3 = f32[8,4096]{1,0:T(8,128)S(1)} collective-permute-done((f32[8,4096]{1,0:T(8,128)S(1)}, f32[8,4096]{1,0:T(8,128)S(1)}, u32[]{:S(2)}, u32[]{:S(2)}) %collective-permute-start.25) | collective-permute-done | bytes 131104 | tf_op jit(solution)/shard_map/ppermute | solution.py:40
  101.9 2.6 %collective-permute-start.33 = (f32[64,128]{1,0:T(8,128)S(1)}, f32[64,128]{1,0:T(8,128)S(1)}, u32[]{:S(2)}, u32[]{:S(2)}) collective-permute-start(f32[64,128]{1,0:T(8,128)S(1)} %get-tuple-element.64.u0), channel_id=1, source_target_pairs={{0,2},{1,3},{2,4},{3,5},{4,6},{5,7},{6,0},{7,1},{8,10},{9,11},{10,... | collective-permute-start | bytes 98312 | tf_op jit(solution)/shard_map/ppermute | solution.py:36
  104.5 1.8 %collective-permute-start.31 = (f32[64,128]{1,0:T(8,128)S(1)}, f32[64,128]{1,0:T(8,128)S(1)}, u32[]{:S(2)}, u32[]{:S(2)}) collective-permute-start(f32[64,128]{1,0:T(8,128)S(1)} %get-tuple-element.64.u0), channel_id=1, source_target_pairs={{0,6},{1,7},{2,0},{3,1},{4,2},{5,3},{6,4},{7,5},{8,14},{9,15},{10,... | collective-permute-start | bytes 98312 | tf_op jit(solution)/shard_map/ppermute | solution.py:36
  107.5 5.0 %shard_map.82.term = f32[512,64]{1,0:T(8,128)S(1)} custom-call(f32[64,4096]{1,0:T(8,128)S(1)} %get-tuple-element.66.p_raw, f32[512,4096]{1,0:T(8,128)} %bitcast.22), custom_call_target="tpu_custom_call" | custom-call | tf_op jit(solution)/shard_map/pallas_call | solution.py:259
  115.5 3.7 %collective-permute-start.37 = (f32[64,512]{1,0:T(8,128)S(1)}, f32[64,512]{1,0:T(8,128)S(1)}, u32[]{:S(2)}, u32[]{:S(2)}) collective-permute-start(f32[64,512]{1,0:T(8,128)S(1)} %shard_map.83), channel_id=1, source_target_pairs={{0,24},{8,0},{16,8},{24,16},{32,56},{40,32},{48,40},{56,48},{64,88... | collective-permute-start | bytes 393224 | tf_op jit(solution)/shard_map/ppermute | solution.py:44
  120.5 7.7 %shard_map.84 = (f32[64,64]{1,0:T(8,128)S(1)}, bf16[192,4096]{1,0:T(8,128)(2,1)}) custom-call(f32[64,4096]{1,0:T(8,128)S(1)} %get-tuple-element.66.p_raw), custom_call_target="tpu_custom_call" | custom-call | tf_op jit(solution)/shard_map/pallas_call | solution.py:320
  131.1 2.9 %collective-permute-start.42 = (f32[64,512]{1,0:T(8,128)S(1)}, f32[64,512]{1,0:T(8,128)S(1)}, u32[]{:S(2)}, u32[]{:S(2)}) collective-permute-start(f32[64,512]{1,0:T(8,128)S(1)} %add_add_fusion.1), channel_id=1, source_target_pairs={{0,64},{8,72},{16,80},{24,88},{32,96},{40,104},{48,112},{56,120},{... | collective-permute-start | bytes 393224 | tf_op jit(solution)/shard_map/ppermute | solution.py:40
  134.0 5.1 %shard_map.85 = (bf16[128,1024]{1,0:T(8,128)(2,1)S(1)}, bf16[128,1024]{1,0:T(8,128)(2,1)S(1)}, bf16[128,1024]{1,0:T(8,128)(2,1)S(1)}, bf16[128,1024]{1,0:T(8,128)(2,1)S(1)}) custom-call(s32[4]{0:T(128)S(1)} %pad_add_fusion.place, bf16[4,128,4096]{2,1,0:T(8,128)(2,1)S(1)} %bitcast.14, bf16[4,256,512]{2,1,0:T(8,128)(2,1)S(1)} %pad_maximum_fusion.refs_0_, ...), custom_call_target="tpu_custom_call" | custom-call | tf_op jit(solution)/shard_map/pallas_call | solution.py:383
  139.1 1.8 %collective-permute-start.41 = (bf16[128,1024]{1,0:T(8,128)(2,1)S(1)}, bf16[128,1024]{1,0:T(8,128)(2,1)S(1)}, u32[]{:S(2)}, u32[]{:S(2)}) collective-permute-start(bf16[128,1024]{1,0:T(8,128)(2,1)S(1)} %get-tuple-element.74), channel_id=1, source_target_pairs={{0,8},{8,16},{16,24},{24,0},{32,40},{40,48},{48,56},{56,32},{64,72... | collective-permute-start | bytes 786440 | tf_op jit(solution)/shard_map/ppermute | solution.py:44
  142.9 12.0 %shard_map.86 = (f32[64,512]{1,0:T(8,128)}, f32[512,4096]{1,0:T(8,128)}) custom-call(f32[64,64]{1,0:T(8,128)S(1)} %get-tuple-element.75.inverse, f32[64,512]{1,0:T(8,128)S(1)} %add_add_fusion.w, bf16[512,1024]{1,0:T(8,128)(2,1)S(1)} %shard_map.80.turned, bf16[192,4096]{1,0:T(8,128)(2,1)} %get-tuple-element.68.p_far, f32[512,4096]{1,0:T(8,128)} %bitcast.23, ...), custom_call_target="tpu_custom_call" | custom-call | tf_op jit(solution)/shard_map/pallas_call | solution.py:356
  (116 shorter events, 37.3 us)
Async XLA Ops:
  7.2 76.1 %all-gather.6.cloned.1.call-start = ((), (), s32[]{:S(2)}) async-start(), calls=%async_computation.1 | async-start | bytes 5242880 | tf_op jit(solution)/shard_map/all_gather | solution.py:404
  7.9 135.0 %all-gather.4.cloned.1.call-start = ((), (), s32[]{:S(2)}) async-start(), calls=%async_computation | async-start | bytes 9437184 | tf_op jit(solution)/shard_map/all_gather | solution.py:432
  8.9 12.5 %collective-permute-start.3 = (bf16[256,512]{1,0:T(8,128)(2,1)S(1)}, bf16[256,512]{1,0:T(8,128)(2,1)S(1)}, u32[]{:S(2)}, u32[]{:S(2)}) collective-permute-start(bf16[256,512]{1,0:T(8,128)(2,1)S(1)} %constant_dynamic-slice_fusion), channel_id=1, source_target_pairs={{0,6},{1,7},{2,0},{3,1},{4,2},{5,3},{6,4},{7,5},{8,14},{9,15},{10,... | collective-permute-start | bytes 786440 | tf_op jit(solution)/shard_map/ppermute | solution.py:36
  12.3 9.1 %collective-permute-start = (bf16[256,512]{1,0:T(8,128)(2,1)S(1)}, bf16[256,512]{1,0:T(8,128)(2,1)S(1)}, u32[]{:S(2)}, u32[]{:S(2)}) collective-permute-start(bf16[256,512]{1,0:T(8,128)(2,1)S(1)} %constant_dynamic-slice_fusion), channel_id=1, source_target_pairs={{0,2},{1,3},{2,4},{3,5},{4,6},{5,7},{6,0},{7,1},{8,10},{9,11},{10,... | collective-permute-start | bytes 786440 | tf_op jit(solution)/shard_map/ppermute | solution.py:36
  12.3 9.1 %collective-permute-start.1 = (f32[64,512]{1,0:T(8,128)}, f32[64,512]{1,0:T(8,128)S(1)}, u32[]{:S(2)}, u32[]{:S(2)}) collective-permute-start(f32[64,512]{1,0:T(8,128)} %bitcast.15), channel_id=1, source_target_pairs={{0,6},{1,7},{2,0},{3,1},{4,2},{5,3},{6,4},{7,5},{8,14},{9,15},{10,... | collective-permute-start | bytes 393224 | tf_op jit(solution)/shard_map/ppermute | solution.py:36
  15.0 11.0 %collective-permute-start.5 = (f32[64,512]{1,0:T(8,128)}, f32[64,512]{1,0:T(8,128)S(1)}, u32[]{:S(2)}, u32[]{:S(2)}) collective-permute-start(f32[64,512]{1,0:T(8,128)} %bitcast.17), channel_id=1, source_target_pairs={{0,2},{1,3},{2,4},{3,5},{4,6},{5,7},{6,0},{7,1},{8,10},{9,11},{10,... | collective-permute-start | bytes 393224 | tf_op jit(solution)/shard_map/ppermute | solution.py:36
  33.1 9.4 %collective-permute-start.2 = (bf16[256,512]{1,0:T(8,128)(2,1)S(1)}, bf16[256,512]{1,0:T(8,128)(2,1)S(1)}, u32[]{:S(2)}, u32[]{:S(2)}) collective-permute-start(bf16[256,512]{1,0:T(8,128)(2,1)S(1)} %constant_dynamic-slice_fusion), channel_id=1, source_target_pairs={{0,4},{1,5},{2,6},{3,7},{4,0},{5,1},{6,2},{7,3},{8,12},{9,13},{10,... | collective-permute-start | bytes 786440 | tf_op jit(solution)/shard_map/ppermute | solution.py:36
  33.2 15.0 %collective-permute-start.11 = (bf16[2,128,512]{2,1,0:T(8,128)(2,1)S(1)}, bf16[2,128,512]{2,1,0:T(8,128)(2,1)S(1)}, u32[]{:S(2)}, u32[]{:S(2)}) collective-permute-start(bf16[2,128,512]{2,1,0:T(8,128)(2,1)S(1)} %get-tuple-element.47), channel_id=1, source_target_pairs={{0,2},{1,3},{2,4},{3,5},{4,6},{5,7},{6,0},{7,1},{8,10},{9,11},{10,... | collective-permute-start | bytes 786440 | tf_op jit(solution)/shard_map/ppermute | solution.py:36
  33.8 14.9 %collective-permute-start.12 = (bf16[2,128,512]{2,1,0:T(8,128)(2,1)S(1)}, bf16[2,128,512]{2,1,0:T(8,128)(2,1)S(1)}, u32[]{:S(2)}, u32[]{:S(2)}) collective-permute-start(bf16[2,128,512]{2,1,0:T(8,128)(2,1)S(1)} %get-tuple-element.49), channel_id=1, source_target_pairs={{0,6},{1,7},{2,0},{3,1},{4,2},{5,3},{6,4},{7,5},{8,14},{9,15},{10,... | collective-permute-start | bytes 786440 | tf_op jit(solution)/shard_map/ppermute | solution.py:36
  36.0 12.6 %collective-permute-start.10 = (f32[8,4096]{1,0:T(8,128)S(1)}, f32[8,4096]{1,0:T(8,128)S(1)}, u32[]{:S(2)}, u32[]{:S(2)}) collective-permute-start(f32[8,4096]{1,0:T(8,128)S(1)} %get-tuple-element.81), channel_id=1, source_target_pairs={{0,96},{8,104},{16,112},{24,120},{32,0},{40,8},{48,16},{56,24},{64... | collective-permute-start | bytes 393224 | tf_op jit(solution)/shard_map/ppermute | solution.py:40
  38.8 9.8 %collective-permute-start.8 = (f32[8,4096]{1,0:T(8,128)S(1)}, f32[8,4096]{1,0:T(8,128)S(1)}, u32[]{:S(2)}, u32[]{:S(2)}) collective-permute-start(f32[8,4096]{1,0:T(8,128)S(1)} %get-tuple-element.83), channel_id=1, source_target_pairs={{0,64},{8,72},{16,80},{24,88},{32,96},{40,104},{48,112},{56,120},{... | collective-permute-start | bytes 393224 | tf_op jit(solution)/shard_map/ppermute | solution.py:40
  48.2 11.5 %collective-permute-start.17 = (bf16[2,128,512]{2,1,0:T(8,128)(2,1)S(1)}, bf16[2,128,512]{2,1,0:T(8,128)(2,1)S(1)}, u32[]{:S(2)}, u32[]{:S(2)}) collective-permute-start(bf16[2,128,512]{2,1,0:T(8,128)(2,1)S(1)} %get-tuple-element.53), channel_id=1, source_target_pairs={{0,4},{1,5},{2,6},{3,7},{4,0},{5,1},{6,2},{7,3},{8,12},{9,13},{10,... | collective-permute-start | bytes 786440 | tf_op jit(solution)/shard_map/ppermute | solution.py:36
  48.7 13.0 %collective-permute-start.15 = (f32[8,4096]{1,0:T(8,128)S(1)}, f32[8,4096]{1,0:T(8,128)S(1)}, u32[]{:S(2)}, u32[]{:S(2)}) collective-permute-start(f32[8,4096]{1,0:T(8,128)S(1)} %fusion), channel_id=1, source_target_pairs={{0,2},{1,3},{2,4},{3,5},{4,6},{5,7},{6,0},{7,1},{8,10},{9,11},{10,... | collective-permute-start | bytes 393224 | tf_op jit(solution)/shard_map/ppermute | solution.py:36
  49.2 8.7 %collective-permute-start.16 = (f32[8,4096]{1,0:T(8,128)S(1)}, f32[8,4096]{1,0:T(8,128)S(1)}, u32[]{:S(2)}, u32[]{:S(2)}) collective-permute-start(f32[8,4096]{1,0:T(8,128)S(1)} %fusion), channel_id=1, source_target_pairs={{0,6},{1,7},{2,0},{3,1},{4,2},{5,3},{6,4},{7,5},{8,14},{9,15},{10,... | collective-permute-start | bytes 393224 | tf_op jit(solution)/shard_map/ppermute | solution.py:36
  51.4 11.2 %collective-permute-start.14 = (f32[8,4096]{1,0:T(8,128)S(1)}, f32[8,4096]{1,0:T(8,128)S(1)}, u32[]{:S(2)}, u32[]{:S(2)}) collective-permute-start(f32[8,4096]{1,0:T(8,128)S(1)} %fusion), channel_id=1, source_target_pairs={{0,4},{1,5},{2,6},{3,7},{4,0},{5,1},{6,2},{7,3},{8,12},{9,13},{10,... | collective-permute-start | bytes 393224 | tf_op jit(solution)/shard_map/ppermute | solution.py:36
  52.9 23.5 %collective-permute-start.13 = (bf16[4,256,512]{2,1,0:T(8,128)(2,1)S(1)}, bf16[4,256,512]{2,1,0:T(8,128)(2,1)S(1)}, u32[]{:S(2)}, u32[]{:S(2)}) collective-permute-start(bf16[4,256,512]{2,1,0:T(8,128)(2,1)S(1)} %pad_maximum_fusion.refs_0_), channel_id=1, source_target_pairs={{0,96},{8,104},{16,112},{24,120},{32,0},{40,8},{48,16},{56,24},{64... | collective-permute-start | bytes 3145736 | tf_op jit(solution)/shard_map/ppermute | solution.py:40
  57.9 24.3 %collective-permute-start.21 = (bf16[4,256,512]{2,1,0:T(8,128)(2,1)S(1)}, bf16[4,256,512]{2,1,0:T(8,128)(2,1)S(1)}, u32[]{:S(2)}, u32[]{:S(2)}) collective-permute-start(bf16[4,256,512]{2,1,0:T(8,128)(2,1)S(1)} %pad_maximum_fusion.refs_0_), channel_id=1, source_target_pairs={{0,32},{8,40},{16,48},{24,56},{32,64},{40,72},{48,80},{56,88},{64,... | collective-permute-start | bytes 3145736 | tf_op jit(solution)/shard_map/ppermute | solution.py:40
  69.4 12.9 %collective-permute-start.19 = (f32[8,4096]{1,0:T(8,128)S(1)}, f32[8,4096]{1,0:T(8,128)S(1)}, u32[]{:S(2)}, u32[]{:S(2)}) collective-permute-start(f32[8,4096]{1,0:T(8,128)S(1)} %add_add_fusion.3), channel_id=1, source_target_pairs={{0,8},{8,16},{16,24},{24,0},{32,40},{40,48},{48,56},{56,32},{64,72... | collective-permute-start | bytes 393224 | tf_op jit(solution)/shard_map/ppermute | solution.py:44
  69.4 12.9 %collective-permute-start.18 = (f32[8,4096]{1,0:T(8,128)S(1)}, f32[8,4096]{1,0:T(8,128)S(1)}, u32[]{:S(2)}, u32[]{:S(2)}) collective-permute-start(f32[8,4096]{1,0:T(8,128)S(1)} %add_add_fusion.3), channel_id=1, source_target_pairs={{0,16},{8,24},{16,0},{24,8},{32,48},{40,56},{48,32},{56,40},{64,80... | collective-permute-start | bytes 393224 | tf_op jit(solution)/shard_map/ppermute | solution.py:44
  88.4 9.4 %collective-permute-start.25 = (f32[8,4096]{1,0:T(8,128)S(1)}, f32[8,4096]{1,0:T(8,128)S(1)}, u32[]{:S(2)}, u32[]{:S(2)}) collective-permute-start(f32[8,4096]{1,0:T(8,128)S(1)} %add_add_fusion.2.p0), channel_id=1, source_target_pairs={{0,32},{8,40},{16,48},{24,56},{32,64},{40,72},{48,80},{56,88},{64,... | collective-permute-start | bytes 393224 | tf_op jit(solution)/shard_map/ppermute | solution.py:40
  101.1 11.4 %collective-permute-start.30 = (bf16[4,256,512]{2,1,0:T(8,128)(2,1)S(1)}, bf16[4,256,512]{2,1,0:T(8,128)(2,1)S(1)}, u32[]{:S(2)}, u32[]{:S(2)}) collective-permute-start(bf16[4,256,512]{2,1,0:T(8,128)(2,1)S(1)} %pad_maximum_fusion.refs_0_), channel_id=1, source_target_pairs={{0,1},{1,0},{2,3},{3,2},{4,5},{5,4},{6,7},{7,6},{8,9},{9,8},{10,11... | collective-permute-start | bytes 3145736 | tf_op jit(solution)/shard_map/ppermute | solution.py:48
  101.6 26.7 %collective-permute-start.26 = (bf16[4,256,512]{2,1,0:T(8,128)(2,1)S(1)}, bf16[4,256,512]{2,1,0:T(8,128)(2,1)S(1)}, u32[]{:S(2)}, u32[]{:S(2)}) collective-permute-start(bf16[4,256,512]{2,1,0:T(8,128)(2,1)S(1)} %pad_maximum_fusion.refs_0_), channel_id=1, source_target_pairs={{0,64},{8,72},{16,80},{24,88},{32,96},{40,104},{48,112},{56,120},{... | collective-permute-start | bytes 3145736 | tf_op jit(solution)/shard_map/ppermute | solution.py:40
  101.9 10.5 %collective-permute-start.33 = (f32[64,128]{1,0:T(8,128)S(1)}, f32[64,128]{1,0:T(8,128)S(1)}, u32[]{:S(2)}, u32[]{:S(2)}) collective-permute-start(f32[64,128]{1,0:T(8,128)S(1)} %get-tuple-element.64.u0), channel_id=1, source_target_pairs={{0,2},{1,3},{2,4},{3,5},{4,6},{5,7},{6,0},{7,1},{8,10},{9,11},{10,... | collective-permute-start | bytes 98312 | tf_op jit(solution)/shard_map/ppermute | solution.py:36
  115.5 12.8 %collective-permute-start.37 = (f32[64,512]{1,0:T(8,128)S(1)}, f32[64,512]{1,0:T(8,128)S(1)}, u32[]{:S(2)}, u32[]{:S(2)}) collective-permute-start(f32[64,512]{1,0:T(8,128)S(1)} %shard_map.83), channel_id=1, source_target_pairs={{0,24},{8,0},{16,8},{24,16},{32,56},{40,32},{48,40},{56,48},{64,88... | collective-permute-start | bytes 393224 | tf_op jit(solution)/shard_map/ppermute | solution.py:44
  119.2 9.1 %collective-permute-start.36 = (f32[64,512]{1,0:T(8,128)S(1)}, f32[64,512]{1,0:T(8,128)S(1)}, u32[]{:S(2)}, u32[]{:S(2)}) collective-permute-start(f32[64,512]{1,0:T(8,128)S(1)} %shard_map.83), channel_id=1, source_target_pairs={{0,8},{8,16},{16,24},{24,0},{32,40},{40,48},{48,56},{56,32},{64,72... | collective-permute-start | bytes 393224 | tf_op jit(solution)/shard_map/ppermute | solution.py:44
  119.2 9.1 %collective-permute-start.35 = (f32[64,512]{1,0:T(8,128)S(1)}, f32[64,512]{1,0:T(8,128)S(1)}, u32[]{:S(2)}, u32[]{:S(2)}) collective-permute-start(f32[64,512]{1,0:T(8,128)S(1)} %shard_map.83), channel_id=1, source_target_pairs={{0,16},{8,24},{16,0},{24,8},{32,48},{40,56},{48,32},{56,40},{64,80... | collective-permute-start | bytes 393224 | tf_op jit(solution)/shard_map/ppermute | solution.py:44
  129.6 12.3 %collective-permute-start.44 = (f32[64,512]{1,0:T(8,128)S(1)}, f32[64,512]{1,0:T(8,128)S(1)}, u32[]{:S(2)}, u32[]{:S(2)}) collective-permute-start(f32[64,512]{1,0:T(8,128)S(1)} %add_add_fusion.1), channel_id=1, source_target_pairs={{0,96},{8,104},{16,112},{24,120},{32,0},{40,8},{48,16},{56,24},{64... | collective-permute-start | bytes 393224 | tf_op jit(solution)/shard_map/ppermute | solution.py:40
  130.5 12.3 %collective-permute-start.43 = (f32[64,512]{1,0:T(8,128)S(1)}, f32[64,512]{1,0:T(8,128)S(1)}, u32[]{:S(2)}, u32[]{:S(2)}) collective-permute-start(f32[64,512]{1,0:T(8,128)S(1)} %add_add_fusion.1), channel_id=1, source_target_pairs={{0,32},{8,40},{16,48},{24,56},{32,64},{40,72},{48,80},{56,88},{64,... | collective-permute-start | bytes 393224 | tf_op jit(solution)/shard_map/ppermute | solution.py:40
  131.1 11.7 %collective-permute-start.42 = (f32[64,512]{1,0:T(8,128)S(1)}, f32[64,512]{1,0:T(8,128)S(1)}, u32[]{:S(2)}, u32[]{:S(2)}) collective-permute-start(f32[64,512]{1,0:T(8,128)S(1)} %add_add_fusion.1), channel_id=1, source_target_pairs={{0,64},{8,72},{16,80},{24,88},{32,96},{40,104},{48,112},{56,120},{... | collective-permute-start | bytes 393224 | tf_op jit(solution)/shard_map/ppermute | solution.py:40
  139.1 15.7 %collective-permute-start.41 = (bf16[128,1024]{1,0:T(8,128)(2,1)S(1)}, bf16[128,1024]{1,0:T(8,128)(2,1)S(1)}, u32[]{:S(2)}, u32[]{:S(2)}) collective-permute-start(bf16[128,1024]{1,0:T(8,128)(2,1)S(1)} %get-tuple-element.74), channel_id=1, source_target_pairs={{0,8},{8,16},{16,24},{24,0},{32,40},{40,48},{48,56},{56,32},{64,72... | collective-permute-start | bytes 786440 | tf_op jit(solution)/shard_map/ppermute | solution.py:44
  140.9 14.0 %collective-permute-start.39 = (bf16[128,1024]{1,0:T(8,128)(2,1)S(1)}, bf16[128,1024]{1,0:T(8,128)(2,1)S(1)}, u32[]{:S(2)}, u32[]{:S(2)}) collective-permute-start(bf16[128,1024]{1,0:T(8,128)(2,1)S(1)} %get-tuple-element.72), channel_id=1, source_target_pairs={{0,24},{8,0},{16,8},{24,16},{32,56},{40,32},{48,40},{56,48},{64,88... | collective-permute-start | bytes 786440 | tf_op jit(solution)/shard_map/ppermute | solution.py:44
  141.9 13.0 %collective-permute-start.40 = (bf16[128,1024]{1,0:T(8,128)(2,1)S(1)}, bf16[128,1024]{1,0:T(8,128)(2,1)S(1)}, u32[]{:S(2)}, u32[]{:S(2)}) collective-permute-start(bf16[128,1024]{1,0:T(8,128)(2,1)S(1)} %get-tuple-element.73), channel_id=1, source_target_pairs={{0,16},{8,24},{16,0},{24,8},{32,48},{40,56},{48,32},{56,40},{64,80... | collective-permute-start | bytes 786440 | tf_op jit(solution)/shard_map/ppermute | solution.py:44
  (28 other events, 291.1 us)
Sparse Core Ops, SparseCore 0:
  9.7 51.6 all-gather.5
  83.4 56.0 all-gather.3

commit v3 on v2

--- a/solution.py
+++ b/solution.py
@@ -82,45 +82,32 @@
     return pl.multiple_of((c ^ a) * 32 + lax.rem(y + d, 4) * 8, 8)
 
 
-def cut_body(place, grad, *outs):
-    x, c = place[0], place[1]
+def cut_far_body(place, grad, out):
+    for d in range(4):
+        out[d] = grad[:, pl.ds(pl.multiple_of(chunk_of(place[0], place[1], 1, d) * 512, 512), 512)]
+
+
+def cut_far(place, grad):
+    return pallas(cut_far_body, shaped((4, 128, 512), BF16), in_specs=[SMEM, VMEM], out_specs=VMEM)(place, grad)
+
+
+def cut_body(place, grad, passed, *outs):
     for d, out in enumerate(outs):
-        for a in range(2):
-            out[a] = grad[:, pl.ds(pl.multiple_of(chunk_of(x, c, a, d) * 512, 512), 512)]
-
-
-def cut(place, grad):
-    return pallas(cut_body, [shaped((2, 128, 512), BF16)] * 4, in_specs=[SMEM, VMEM], out_specs=[VMEM] * 4)(place, grad)
-
-
-def sort_body(c0, c1, c2, c3, near, far, done):
-    copies = []
-    for d, chunk in enumerate((c0, c1, c2, c3)):
-        for a, out in enumerate((near, far)):
-            copies.append(pltpu.make_async_copy(chunk.at[a], out.at[d], done.at[a, d]))
-            copies[-1].start()
-    for copy in copies:
-        copy.wait()
-
-
-def sort(chunks):
-    return pallas(
-        sort_body,
-        [shaped((4, 128, 512), BF16)] * 2,
-        in_specs=[HBM] * 4,
-        out_specs=[VMEM] * 2,
-        scratch_shapes=[pltpu.SemaphoreType.DMA((2, 4))],
-    )(*[in_hbm(chunk) for chunk in chunks])
-
-
-def columns(i, blocks=4):
-    return slice(4096 // blocks * i, 4096 // blocks * (i + 1))
+        out[0] = grad[:, pl.ds(pl.multiple_of(chunk_of(place[0], place[1], 0, d) * 512, 512), 512)]
+        out[1] = passed[d]
+
+
+def cut(place, grad, passed):
+    return pallas(cut_body, [shaped((2, 128, 512), BF16)] * 4, in_specs=[SMEM, VMEM, VMEM], out_specs=[VMEM] * 4)(place, grad, passed)
+
+
+def columns(i):
+    return slice(1024 * i, 1024 * i + 1024)
 
 
 class Fetch:
-    def __init__(self, source, held, arrived, ahead, blocks=4):
-        parts = [columns(i, blocks) for i in range(blocks)]
-        self.copies = [pltpu.make_async_copy(source.at[:, at], held.at[:, at], arrived.at[i]) for i, at in enumerate(parts)]
+    def __init__(self, source, held, arrived, ahead):
+        self.copies = [pltpu.make_async_copy(source.at[:, columns(i)], held.at[:, columns(i)], arrived.at[i]) for i in range(4)]
         self.ahead = ahead
         for copy in self.copies[:ahead]:
             copy.start()
@@ -207,17 +194,26 @@
     )(place, *values)
 
 
-def turn_body(place, near, far, out):
+def turn_body(place, c0, c1, c2, c3, out, held, done):
     x, c = place[0], place[1]
-    for a, d in RELATIVE:
-        chunk = far[d] if a else near[d]
-        out[:, pl.ds(pl.multiple_of(chunk_of(x, c, a, 4 - d) * 128, 128), 128)] = chunk.T
-
-
-def turn(place, near, far):
-    return pallas(
-        turn_body, shaped((512, 1024), BF16), in_specs=[SMEM, VMEM, VMEM], out_specs=VMEM
-    )(place, near, far)
+    copies = [pltpu.make_async_copy(chunk, held.at[d], done.at[d]) for d, chunk in enumerate((c0, c1, c2, c3))]
+    for copy in copies:
+        copy.start()
+    for d, copy in enumerate(copies):
+        copy.wait()
+        for a in range(2):
+            first = pl.multiple_of(chunk_of(x, c, a, 4 - d) * 128, 128)
+            out[:, pl.ds(first, 128)] = held[d, a].T
+
+
+def turn(place, chunks):
+    return pallas(
+        turn_body,
+        shaped((512, 1024), BF16),
+        in_specs=[SMEM] + [HBM] * 4,
+        out_specs=VMEM,
+        scratch_shapes=[pltpu.VMEM((4, 2, 128, 512), BF16), pltpu.SemaphoreType.DMA((4,))],
+    )(place, *[in_hbm(chunk) for chunk in chunks])
 
 
 def middle_body(place, p0, p1, p2, p3, p_far, ctx, p_out, u_out):
@@ -327,27 +323,27 @@
 
 
 def last_body(inverse, w, turned, p_far, error, ctx, q_out, out, p, held, held_ctx, arrived, arrived_ctx, left_here, p_here):
-    ctx_blocks, blocks = Fetch(ctx, held_ctx, arrived_ctx, 2, 8), Fetch(error, held, arrived, 2, 8)
+    ctx_blocks, blocks = Fetch(ctx, held_ctx, arrived_ctx, 1), Fetch(error, held, arrived, 1)
     p_copy = pltpu.make_async_copy(p_far, p, p_here)
     p_copy.start()
     ctx_blocks.wait(0)
-    product = mm(turned[...], held_ctx[:, columns(0, 8)])
+    product = mm(turned[...], held_ctx[:, columns(0)])
     q = mm(inverse[...], w[...], NN, lax.Precision.HIGHEST) * (1.0 / 16)
     q_out[...] = q
     high, low = halves(q)
     q_split = jnp.concatenate([high, high, low], 0).T
     p_copy.wait()
     stores = []
-    for i in range(8):
-        at = columns(i, 8)
+    for i in range(4):
+        at = columns(i)
         approx = mm(q_split, p[:, at])
         blocks.wait(i)
         held[:, at] = (held[:, at] + product) - approx
         stores.append(pltpu.make_async_copy(held.at[:, at], out.at[:, at], left_here.at[i]))
         stores[-1].start()
-        if i < 7:
+        if i < 3:
             ctx_blocks.wait(i + 1)
-            product = mm(turned[...], held_ctx[:, columns(i + 1, 8)])
+            product = mm(turned[...], held_ctx[:, columns(i + 1)])
     for store in stores:
         store.wait()
 
@@ -360,15 +356,20 @@
         in_specs=[VMEM] * 3 + [HBM] * 3,
         out_specs=[VMEM, HBM],
         scratch_shapes=[pltpu.VMEM((192, 4096), BF16), pltpu.VMEM((512, 4096), F32), pltpu.VMEM((1024, 4096), BF16)]
-        + [pltpu.SemaphoreType.DMA((8,))] * 3
+        + [pltpu.SemaphoreType.DMA((4,))] * 3
         + [pltpu.SemaphoreType.DMA],
     )(inverse, w, turned, in_hbm(p), in_hbm(error), in_hbm(ctx))
 
 
 def share_body(place, tokens, *refs):
-    slabs, outs, whole = refs[:8], refs[8:12], refs[12]
+    slabs, outs, (whole, held, done) = [*refs[:8]], refs[8:12], refs[12:]
+    copy = pltpu.make_async_copy(slabs[3], held, done)
+    copy.start()
+    slabs[3] = held
     x, c, y, z = place[0], place[1], place[2], place[3]
     for e in range(4):
+        if e == 3:
+            copy.wait()
         total = jnp.zeros((512, 256), F32)
         for a in range(2):
             for d in range(4):
@@ -384,10 +385,10 @@
         share_body,
         [shaped((128, 1024), BF16)] * 4,
         mib=24,
-        in_specs=[SMEM] + [VMEM] * 9,
+        in_specs=[SMEM] + [VMEM] * 4 + [HBM] + [VMEM] * 4,
         out_specs=[VMEM] * 4,
-        scratch_shapes=[pltpu.VMEM((512, 1024), BF16)],
-    )(place, tokens, *mine, *theirs)
+        scratch_shapes=[pltpu.VMEM((512, 1024), BF16), pltpu.VMEM((4, 256, 512), BF16), pltpu.SemaphoreType.DMA],
+    )(place, tokens, *mine[:3], in_hbm(mine[3]), *theirs)
 
 
 def pair_sum(values):
@@ -409,37 +410,34 @@
     pieces = [piece, along_x(piece, 1), along_x(after(piece, q_near[1]), 2), along_x(piece, 3)]
     term = error_left(place, qt, error)
     q_far = other_core(jnp.concatenate([qt, after(q_near[1], term, pieces[1], pieces[3]), *q_near[2:]], 0))
-    sends = cut(place, grad_out)
     near, far = left(place, q_near, q_far, grad_out, ctx, term)
-    chunks = [sends[0]] + [along_x(after(sends[d], *q_near), d) if d != 2 else None for d in (1, 2, 3)]
     half = near + other_core(far)
 
-    chunks[2] = along_x(after(sends[2], half), 2)
+    passed = other_core(after(cut_far(place, grad_out), near))
     blocks = [half[:8]] + [along_y(half[8 * d : 8 * d + 8], d) for d in (1, 2, 3)]
-    blocks[3] = after(blocks[3], pieces[2], chunks[1], chunks[3])
+    blocks[3] = after(blocks[3], pieces[2], passed)
     summed = pair_sum(blocks)
     w0 = after(jnp.stack(pieces), summed)
     w1, w3 = [along_y(w0, d) for d in (-1, 1)]
-    over_x = [summed] + [along_x(summed, d) for d in (1, 2, 3)]
-    over_x[3] = after(over_x[3], chunks[2])
-    summed = pair_sum(over_x)
-    near_columns, far_columns = sort([*chunks[:3], after(chunks[3], summed)])
-    far_columns = other_core(far_columns)
-    turned = turn(place, near_columns, far_columns)
+    summed = pair_sum([summed] + [along_x(summed, d) for d in (1, 2, 3)])
+    sends = cut(place, grad_out, after(passed, summed))
+    chunk1, chunk3 = [along_x(sends[d], d) for d in (1, 3)]
     over_z = [summed] + [along_z(summed, d) for d in (1, 2, 3)]
-    over_z[3] = after(over_z[3], w1, w3, turned)
+    their0 = other_core(after(w0, summed))
+    over_z[3] = after(over_z[3], w1, w3, chunk1, chunk3, their0)
     rows = pair_sum(over_z)
     ctx_all = lax.all_gather(after(ctx, rows, tokens), "fsdp", axis=0, tiled=True)
     p_near = [rows] + [along_y(rows, -d) for d in (1, 2, 3)]
-    their1, their3 = other_core(after(w1, rows)), other_core(after(w3, rows))
-    p_far = other_core(jnp.concatenate([rows, after(p_near[1], their1, their3), *p_near[2:]], 0))
+    chunk2 = along_x(after(sends[2], rows), 2)
+    their1, their3 = [other_core(after(v, rows)) for v in (w1, w3)]
+    p_far = other_core(jnp.concatenate([rows, after(p_near[1], their1, their3, chunk2), *p_near[2:]], 0))
     w2 = along_y(after(w0, *p_near), 2)
 
     p_raw, u = middle(place, p_near, p_far, ctx)
     u_near = [u] + [along_x(u, -d) for d in (1, 2, 3)]
     w_term = right(p_raw, error)
-    their0 = other_core(after(w0, u))
-    u_far = other_core(jnp.concatenate([u, u_near[1], u_near[2], after(u_near[3], w_term, their0)], 0))
+    turned = turn(place, [sends[0], chunk1, chunk2, chunk3])
+    u_far = other_core(jnp.concatenate([u, u_near[1], u_near[2], after(u_near[3], w_term, turned)], 0))
     w = collect(place, w_term, turned, u_near, u_far)
     w = [w] + [along_z(w, d) for d in (1, 2, 3)]
     inverse, p = solve(p_raw)

time: 164 us -> 164 us (level)
  waiting for transfers between devices: 41 us -> 36.2 us
  Pallas kernels: 43.6 us -> 47.3 us
    ppermute x12, waiting for transfers between devices: 18.7 us -> 12.2 us  [along_y(): lax.ppermute(value, 'dp', [(i, (i // 4 + d) % 4 * 4 + i % 4) for i in ran...]
    ppermute x12, starting transfers between devices: 16.2 us -> 11.5 us  [along_y(): lax.ppermute(value, 'dp', [(i, (i // 4 + d) % 4 * 4 + i % 4) for i in ran...]
    ppermute x9, starting transfers between devices: 13.7 us -> 17.6 us  [along_z(): lax.ppermute(value, 'dp', [(i, i // 4 * 4 + (i % 4 + d) % 4) for i in ran...]
    pallas_call x1, Pallas kernels: 5.13 us -> 8.32 us  [share(): pallas(share_body, [shaped((128, 1024), BF16)] * 4, mib=24, in_specs=[SME...]
    ppermute x9, waiting for transfers between devices: 0.71 us -> 3.82 us  [along_z(): lax.ppermute(value, 'dp', [(i, i // 4 * 4 + (i % 4 + d) % 4) for i in ran...]
  transfers between devices with their start and end apart: 47 -> 47, of which waited for: 17 -> 18; matrix products, arithmetic and copies ran while one was open for 2% -> 1% of each run, Pallas kernels for 26% -> 28%
where the time goes in v3:
time: 164 us
  starting transfers between devices  60.5 us (37%)
  Pallas kernels  47.3 us (29%)
  waiting for transfers between devices  36.2 us (22%)
  between operations  14.5 us (9%)
  local copies, waits for them, and re-layouts  4.89 us (3%)
    ppermute x15, starting transfers between devices, along_x(): lax.ppermute(value, 'fsdp', [(i, (i // 2 + d) % 4 * 2 + i % 2) for i in r...  20.3 us
    ppermute x9, starting transfers between devices, along_z(): lax.ppermute(value, 'dp', [(i, i // 4 * 4 + (i % 4 + d) % 4) for i in ran...  17.6 us
    ppermute x15, waiting for transfers between devices, along_x(): lax.ppermute(value, 'fsdp', [(i, (i // 2 + d) % 4 * 2 + i % 2) for i in r...  15.4 us
    ppermute x12, waiting for transfers between devices, along_y(): lax.ppermute(value, 'dp', [(i, (i // 4 + d) % 4 * 4 + i % 4) for i in ran...  12.2 us
    pallas_call x1, Pallas kernels, last(): pallas(last_body, [shaped((64, 512)), shaped((512, 4096))], mib=24, in_sp...  12.2 us
    ppermute x12, starting transfers between devices, along_y(): lax.ppermute(value, 'dp', [(i, (i // 4 + d) % 4 * 4 + i % 4) for i in ran...  11.5 us
    ppermute x9, starting transfers between devices, other_core(): return lax.ppermute(value, 'fsdp', [(i, i ^ 1) for i in range(8)])  11 us
    pallas_call x1, Pallas kernels, share(): pallas(share_body, [shaped((128, 1024), BF16)] * 4, mib=24, in_specs=[SME...  8.32 us
  transfers between devices with their start and end apart: 47, of which 18 were waited for; matrix products, arithmetic and copies ran while one was open for 1% of the time, Pallas kernels for 28%

profile of v3, /device:TPU:1, one launch (start us, length us, event | category | flops | bytes accessed | tf_op | source)
XLA Modules:
  0.0 163.9 jit_solution(8224023074359115663)
XLA Ops:
  8.2 3.4 %collective-permute-start.3 = (bf16[256,512]{1,0:T(8,128)(2,1)S(1)}, bf16[256,512]{1,0:T(8,128)(2,1)S(1)}, u32[]{:S(2)}, u32[]{:S(2)}) collective-permute-start(bf16[256,512]{1,0:T(8,128)(2,1)S(1)} %constant_dynamic-slice_fusion), channel_id=1, source_target_pairs={{0,6},{1,7},{2,0},{3,1},{4,2},{5,3},{6,4},{7,5},{8,14},{9,15},{10,... | collective-permute-start | bytes 786440 | tf_op jit(solution)/shard_map/ppermute | solution.py:36
  11.7 2.7 %collective-permute-start.1 = (f32[64,512]{1,0:T(8,128)}, f32[64,512]{1,0:T(8,128)S(1)}, u32[]{:S(2)}, u32[]{:S(2)}) collective-permute-start(f32[64,512]{1,0:T(8,128)} %bitcast.15), channel_id=1, source_target_pairs={{0,6},{1,7},{2,0},{3,1},{4,2},{5,3},{6,4},{7,5},{8,14},{9,15},{10,... | collective-permute-start | bytes 393224 | tf_op jit(solution)/shard_map/ppermute | solution.py:36
  16.1 4.6 %shard_map.76.term = f32[64,4096]{1,0:T(8,128)S(1)} custom-call(s32[4]{0:T(128)S(1)} %pad_add_fusion.place, f32[64,512]{1,0:T(8,128)S(1)} %bitcast.18, f32[512,4096]{1,0:T(8,128)} %bitcast.21), custom_call_target="tpu_custom_call" | custom-call | tf_op jit(solution)/shard_map/pallas_call | solution.py:138
  21.7 3.6 %collective-permute-done.5.q3 = f32[64,512]{1,0:T(8,128)S(1)} collective-permute-done((f32[64,512]{1,0:T(8,128)}, f32[64,512]{1,0:T(8,128)S(1)}, u32[]{:S(2)}, u32[]{:S(2)}) %collective-permute-start.5) | collective-permute-done | bytes 131104 | tf_op jit(solution)/shard_map/ppermute | solution.py:36
  25.3 1.9 %collective-permute-start.6 = (f32[256,512]{1,0:T(8,128)S(1)}, f32[256,512]{1,0:T(8,128)S(1)}, u32[]{:S(2)}, u32[]{:S(2)}) collective-permute-start(f32[256,512]{1,0:T(8,128)S(1)} %pad_maximum_fusion.1), channel_id=1, source_target_pairs={{0,1},{1,0},{2,3},{3,2},{4,5},{5,4},{6,7},{7,6},{8,9},{9,8},{10,11... | collective-permute-start | bytes 1572872 | tf_op jit(solution)/shard_map/ppermute | solution.py:48
  28.8 2.4 %shard_map.77 = (f32[32,4096]{1,0:T(8,128)S(1)}, f32[32,4096]{1,0:T(8,128)S(1)}) custom-call(s32[4]{0:T(128)S(1)} %pad_add_fusion.place, f32[64,512]{1,0:T(8,128)S(1)} %bitcast.20, f32[64,512]{1,0:T(8,128)S(1)} %collective-permute-done.1.q1, f32[64,512]{1,0:T(8,128)S(1)} %collective-permute-done.4.q2, f32[64,512]{1,0:T(8,128)S(1)} %collective-permute-done.5.q3, ...), custom_call_target="tpu_custom_call" | custom-call | tf_op jit(solution)/shard_map/pallas_call | solution.py:168
  33.3 2.8 %collective-permute-start.10 = (f32[8,4096]{1,0:T(8,128)S(1)}, f32[8,4096]{1,0:T(8,128)S(1)}, u32[]{:S(2)}, u32[]{:S(2)}) collective-permute-start(f32[8,4096]{1,0:T(8,128)S(1)} %get-tuple-element.73), channel_id=1, source_target_pairs={{0,96},{8,104},{16,112},{24,120},{32,0},{40,8},{48,16},{56,24},{64... | collective-permute-start | bytes 393224 | tf_op jit(solution)/shard_map/ppermute | solution.py:40
  38.2 3.5 %collective-permute-done.2 = bf16[256,512]{1,0:T(8,128)(2,1)S(1)} collective-permute-done((bf16[256,512]{1,0:T(8,128)(2,1)S(1)}, bf16[256,512]{1,0:T(8,128)(2,1)S(1)}, u32[]{:S(2)}, u32[]{:S(2)}) %collective-permute-start.2) | collective-permute-done | bytes 262176 | tf_op jit(solution)/shard_map/ppermute | solution.py:36
  42.1 3.9 %collective-permute-done.9 = f32[8,4096]{1,0:T(8,128)S(1)} collective-permute-done((f32[8,4096]{1,0:T(8,128)S(1)}, f32[8,4096]{1,0:T(8,128)S(1)}, u32[]{:S(2)}, u32[]{:S(2)}) %collective-permute-start.9) | collective-permute-done | bytes 131104 | tf_op jit(solution)/shard_map/ppermute | solution.py:40
  46.3 2.5 %collective-permute-start.15 = (f32[8,4096]{1,0:T(8,128)S(1)}, f32[8,4096]{1,0:T(8,128)S(1)}, u32[]{:S(2)}, u32[]{:S(2)}) collective-permute-start(f32[8,4096]{1,0:T(8,128)S(1)} %fusion), channel_id=1, source_target_pairs={{0,6},{1,7},{2,0},{3,1},{4,2},{5,3},{6,4},{7,5},{8,14},{9,15},{10,... | collective-permute-start | bytes 393224 | tf_op jit(solution)/shard_map/ppermute | solution.py:36
  52.1 2.0 %collective-permute-done.13 = f32[8,4096]{1,0:T(8,128)S(1)} collective-permute-done((f32[8,4096]{1,0:T(8,128)S(1)}, f32[8,4096]{1,0:T(8,128)S(1)}, u32[]{:S(2)}, u32[]{:S(2)}) %collective-permute-start.13) | collective-permute-done | bytes 131104 | tf_op jit(solution)/shard_map/ppermute | solution.py:36
  54.2 2.1 %collective-permute-start.22 = (bf16[4,256,512]{2,1,0:T(8,128)(2,1)S(1)}, bf16[4,256,512]{2,1,0:T(8,128)(2,1)S(1)}, u32[]{:S(2)}, u32[]{:S(2)}) collective-permute-start(bf16[4,256,512]{2,1,0:T(8,128)(2,1)S(1)} %pad_maximum_fusion.refs_0_), channel_id=1, source_target_pairs={{0,1},{1,0},{2,3},{3,2},{4,5},{5,4},{6,7},{7,6},{8,9},{9,8},{10,11... | collective-permute-start | bytes 3145736 | tf_op jit(solution)/shard_map/ppermute | solution.py:48
  56.3 3.8 %collective-permute-start.18 = (f32[8,4096]{1,0:T(8,128)S(1)}, f32[8,4096]{1,0:T(8,128)S(1)}, u32[]{:S(2)}, u32[]{:S(2)}) collective-permute-start(f32[8,4096]{1,0:T(8,128)S(1)} %add_add_fusion.3), channel_id=1, source_target_pairs={{0,24},{8,0},{16,8},{24,16},{32,56},{40,32},{48,40},{56,48},{64,88... | collective-permute-start | bytes 393224 | tf_op jit(solution)/shard_map/ppermute | solution.py:44
  62.2 2.5 %collective-permute-done.18 = f32[8,4096]{1,0:T(8,128)S(1)} collective-permute-done((f32[8,4096]{1,0:T(8,128)S(1)}, f32[8,4096]{1,0:T(8,128)S(1)}, u32[]{:S(2)}, u32[]{:S(2)}) %collective-permute-start.18) | collective-permute-done | bytes 131104 | tf_op jit(solution)/shard_map/ppermute | solution.py:44
  64.8 2.4 %collective-permute-start.21 = (bf16[2,128,512]{2,1,0:T(8,128)(2,1)S(1)}, bf16[2,128,512]{2,1,0:T(8,128)(2,1)S(1)}, u32[]{:S(2)}, u32[]{:S(2)}) collective-permute-start(bf16[2,128,512]{2,1,0:T(8,128)(2,1)S(1)} %get-tuple-element.47), channel_id=1, source_target_pairs={{0,6},{1,7},{2,0},{3,1},{4,2},{5,3},{6,4},{7,5},{8,14},{9,15},{10,... | collective-permute-start | bytes 786440 | tf_op jit(solution)/shard_map/ppermute | solution.py:36
  67.1 3.0 %collective-permute-done.20.c1 = bf16[2,128,512]{2,1,0:T(8,128)(2,1)S(1)} collective-permute-done((bf16[2,128,512]{2,1,0:T(8,128)(2,1)S(1)}, bf16[2,128,512]{2,1,0:T(8,128)(2,1)S(1)}, u32[]{:S(2)}, u32[]{:S(2)}) %collective-permute-start.20) | collective-permute-done | bytes 262176 | tf_op jit(solution)/shard_map/ppermute | solution.py:36
  70.1 2.0 %collective-permute-done.21.c3 = bf16[2,128,512]{2,1,0:T(8,128)(2,1)S(1)} collective-permute-done((bf16[2,128,512]{2,1,0:T(8,128)(2,1)S(1)}, bf16[2,128,512]{2,1,0:T(8,128)(2,1)S(1)}, u32[]{:S(2)}, u32[]{:S(2)}) %collective-permute-start.21) | collective-permute-done | bytes 262176 | tf_op jit(solution)/shard_map/ppermute | solution.py:36
  72.1 2.8 %collective-permute-start.16 = (f32[8,4096]{1,0:T(8,128)S(1)}, f32[8,4096]{1,0:T(8,128)S(1)}, u32[]{:S(2)}, u32[]{:S(2)}) collective-permute-start(f32[8,4096]{1,0:T(8,128)S(1)} %add_add_fusion.3), channel_id=1, source_target_pairs={{0,16},{8,24},{16,0},{24,8},{32,48},{40,56},{48,32},{56,40},{64,80... | collective-permute-start | bytes 393224 | tf_op jit(solution)/shard_map/ppermute | solution.py:44
  77.7 2.8 %collective-permute-start.27 = (bf16[4,256,512]{2,1,0:T(8,128)(2,1)S(1)}, bf16[4,256,512]{2,1,0:T(8,128)(2,1)S(1)}, u32[]{:S(2)}, u32[]{:S(2)}) collective-permute-start(bf16[4,256,512]{2,1,0:T(8,128)(2,1)S(1)} %collective-permute-done.12.refs_1_), channel_id=1, source_target_pairs={{0,1},{1,0},{2,3},{3,2},{4,5},{5,4},{6,7},{7,6},{8,9},{9,8},{10,11... | collective-permute-start | bytes 3145736 | tf_op jit(solution)/shard_map/ppermute | solution.py:48
  81.1 2.2 %collective-permute-start.29 = (bf16[2,128,512]{2,1,0:T(8,128)(2,1)S(1)}, bf16[2,128,512]{2,1,0:T(8,128)(2,1)S(1)}, u32[]{:S(2)}, u32[]{:S(2)}) collective-permute-start(bf16[2,128,512]{2,1,0:T(8,128)(2,1)S(1)} %get-tuple-element.54), channel_id=1, source_target_pairs={{0,4},{1,5},{2,6},{3,7},{4,0},{5,1},{6,2},{7,3},{8,12},{9,13},{10,... | collective-permute-start | bytes 786440 | tf_op jit(solution)/shard_map/ppermute | solution.py:36
  83.6 2.0 %collective-permute-done.23.p1 = f32[8,4096]{1,0:T(8,128)S(1)} collective-permute-done((f32[8,4096]{1,0:T(8,128)S(1)}, f32[8,4096]{1,0:T(8,128)S(1)}, u32[]{:S(2)}, u32[]{:S(2)}) %collective-permute-start.23) | collective-permute-done | bytes 131104 | tf_op jit(solution)/shard_map/ppermute | solution.py:40
  85.6 3.4 %collective-permute-done.24.p2 = f32[8,4096]{1,0:T(8,128)S(1)} collective-permute-done((f32[8,4096]{1,0:T(8,128)S(1)}, f32[8,4096]{1,0:T(8,128)S(1)}, u32[]{:S(2)}, u32[]{:S(2)}) %collective-permute-start.24) | collective-permute-done | bytes 131104 | tf_op jit(solution)/shard_map/ppermute | solution.py:40
  89.0 2.4 %collective-permute-done.25.p3 = f32[8,4096]{1,0:T(8,128)S(1)} collective-permute-done((f32[8,4096]{1,0:T(8,128)S(1)}, f32[8,4096]{1,0:T(8,128)S(1)}, u32[]{:S(2)}, u32[]{:S(2)}) %collective-permute-start.25) | collective-permute-done | bytes 131104 | tf_op jit(solution)/shard_map/ppermute | solution.py:40
  97.0 2.1 %collective-permute-start.33 = (f32[64,128]{1,0:T(8,128)S(1)}, f32[64,128]{1,0:T(8,128)S(1)}, u32[]{:S(2)}, u32[]{:S(2)}) collective-permute-start(f32[64,128]{1,0:T(8,128)S(1)} %get-tuple-element.58.u0), channel_id=1, source_target_pairs={{0,2},{1,3},{2,4},{3,5},{4,6},{5,7},{6,0},{7,1},{8,10},{9,11},{10,... | collective-permute-start | bytes 98312 | tf_op jit(solution)/shard_map/ppermute | solution.py:36
  100.9 2.1 %shard_map.82.turned = bf16[512,1024]{1,0:T(8,128)(2,1)S(1)} custom-call(s32[4]{0:T(128)S(1)} %pad_add_fusion.place, bf16[2,128,512]{2,1,0:T(8,128)(2,1)} %copy-done.7, bf16[2,128,512]{2,1,0:T(8,128)(2,1)} %copy-done.9, bf16[2,128,512]{2,1,0:T(8,128)(2,1)} %copy-done.11, bf16[2,128,512]{2,1,0:T(8,128)(2,1)} %copy-done.10), custom_call_target="tpu_custom_call" | custom-call | tf_op jit(solution)/shard_map/pallas_call | solution.py:210
  103.0 5.0 %shard_map.81.term = f32[512,64]{1,0:T(8,128)S(1)} custom-call(f32[64,4096]{1,0:T(8,128)S(1)} %get-tuple-element.56.p_raw, f32[512,4096]{1,0:T(8,128)} %bitcast.22), custom_call_target="tpu_custom_call" | custom-call | tf_op jit(solution)/shard_map/pallas_call | solution.py:255
  111.2 5.6 %collective-permute-start.37 = (f32[64,512]{1,0:T(8,128)S(1)}, f32[64,512]{1,0:T(8,128)S(1)}, u32[]{:S(2)}, u32[]{:S(2)}) collective-permute-start(f32[64,512]{1,0:T(8,128)S(1)} %shard_map.83), channel_id=1, source_target_pairs={{0,24},{8,0},{16,8},{24,16},{32,56},{40,32},{48,40},{56,48},{64,88... | collective-permute-start | bytes 393224 | tf_op jit(solution)/shard_map/ppermute | solution.py:44
  118.0 7.7 %shard_map.84 = (f32[64,64]{1,0:T(8,128)S(1)}, bf16[192,4096]{1,0:T(8,128)(2,1)}) custom-call(f32[64,4096]{1,0:T(8,128)S(1)} %get-tuple-element.56.p_raw), custom_call_target="tpu_custom_call" | custom-call | tf_op jit(solution)/shard_map/pallas_call | solution.py:316
  128.5 2.2 %collective-permute-start.42 = (f32[64,512]{1,0:T(8,128)S(1)}, f32[64,512]{1,0:T(8,128)S(1)}, u32[]{:S(2)}, u32[]{:S(2)}) collective-permute-start(f32[64,512]{1,0:T(8,128)S(1)} %add_add_fusion.1), channel_id=1, source_target_pairs={{0,64},{8,72},{16,80},{24,88},{32,96},{40,104},{48,112},{56,120},{... | collective-permute-start | bytes 393224 | tf_op jit(solution)/shard_map/ppermute | solution.py:40
  130.7 8.3 %shard_map.85 = (bf16[128,1024]{1,0:T(8,128)(2,1)S(1)}, bf16[128,1024]{1,0:T(8,128)(2,1)}, bf16[128,1024]{1,0:T(8,128)(2,1)}, bf16[128,1024]{1,0:T(8,128)(2,1)}) custom-call(s32[4]{0:T(128)S(1)} %pad_add_fusion.place, bf16[4,128,4096]{2,1,0:T(8,128)(2,1)S(1)} %bitcast.14, bf16[4,256,512]{2,1,0:T(8,128)(2,1)S(1)} %pad_maximum_fusion.refs_0_, ...), custom_call_target="tpu_custom_call" | custom-call | tf_op jit(solution)/shard_map/pallas_call | solution.py:384
  139.0 2.3 %collective-permute-start.41 = (bf16[128,1024]{1,0:T(8,128)(2,1)}, bf16[128,1024]{1,0:T(8,128)(2,1)S(1)}, u32[]{:S(2)}, u32[]{:S(2)}) collective-permute-start(bf16[128,1024]{1,0:T(8,128)(2,1)} %get-tuple-element.66), channel_id=1, source_target_pairs={{0,8},{8,16},{16,24},{24,0},{32,40},{40,48},{48,56},{56,32},{64,72... | collective-permute-start | bytes 786440 | tf_op jit(solution)/shard_map/ppermute | solution.py:44
  143.3 12.2 %shard_map.86 = (f32[64,512]{1,0:T(8,128)}, f32[512,4096]{1,0:T(8,128)}) custom-call(f32[64,64]{1,0:T(8,128)S(1)} %get-tuple-element.67.inverse, f32[64,512]{1,0:T(8,128)S(1)} %add_add_fusion.w, bf16[512,1024]{1,0:T(8,128)(2,1)S(1)} %shard_map.82.turned, bf16[192,4096]{1,0:T(8,128)(2,1)} %get-tuple-element.60.p_far, f32[512,4096]{1,0:T(8,128)} %bitcast.23, ...), custom_call_target="tpu_custom_call" | custom-call | tf_op jit(solution)/shard_map/pallas_call | solution.py:352
  (114 shorter events, 37.1 us)
Async XLA Ops:
  7.2 70.5 %all-gather.6.cloned.1.call-start = ((), (), s32[]{:S(2)}) async-start(), calls=%async_computation.1 | async-start | bytes 5242880 | tf_op jit(solution)/shard_map/all_gather | solution.py:405
  8.2 12.5 %collective-permute-start.3 = (bf16[256,512]{1,0:T(8,128)(2,1)S(1)}, bf16[256,512]{1,0:T(8,128)(2,1)S(1)}, u32[]{:S(2)}, u32[]{:S(2)}) collective-permute-start(bf16[256,512]{1,0:T(8,128)(2,1)S(1)} %constant_dynamic-slice_fusion), channel_id=1, source_target_pairs={{0,6},{1,7},{2,0},{3,1},{4,2},{5,3},{6,4},{7,5},{8,14},{9,15},{10,... | collective-permute-start | bytes 786440 | tf_op jit(solution)/shard_map/ppermute | solution.py:36
  11.6 9.1 %collective-permute-start = (bf16[256,512]{1,0:T(8,128)(2,1)S(1)}, bf16[256,512]{1,0:T(8,128)(2,1)S(1)}, u32[]{:S(2)}, u32[]{:S(2)}) collective-permute-start(bf16[256,512]{1,0:T(8,128)(2,1)S(1)} %constant_dynamic-slice_fusion), channel_id=1, source_target_pairs={{0,2},{1,3},{2,4},{3,5},{4,6},{5,7},{6,0},{7,1},{8,10},{9,11},{10,... | collective-permute-start | bytes 786440 | tf_op jit(solution)/shard_map/ppermute | solution.py:36
  11.6 131.7 %all-gather.4.cloned.1.call-start = ((), (), s32[]{:S(2)}) async-start(), calls=%async_computation | async-start | bytes 9437184 | tf_op jit(solution)/shard_map/all_gather | solution.py:429
  11.7 9.0 %collective-permute-start.1 = (f32[64,512]{1,0:T(8,128)}, f32[64,512]{1,0:T(8,128)S(1)}, u32[]{:S(2)}, u32[]{:S(2)}) collective-permute-start(f32[64,512]{1,0:T(8,128)} %bitcast.15), channel_id=1, source_target_pairs={{0,6},{1,7},{2,0},{3,1},{4,2},{5,3},{6,4},{7,5},{8,14},{9,15},{10,... | collective-permute-start | bytes 393224 | tf_op jit(solution)/shard_map/ppermute | solution.py:36
  14.4 10.9 %collective-permute-start.5 = (f32[64,512]{1,0:T(8,128)}, f32[64,512]{1,0:T(8,128)S(1)}, u32[]{:S(2)}, u32[]{:S(2)}) collective-permute-start(f32[64,512]{1,0:T(8,128)} %bitcast.17), channel_id=1, source_target_pairs={{0,2},{1,3},{2,4},{3,5},{4,6},{5,7},{6,0},{7,1},{8,10},{9,11},{10,... | collective-permute-start | bytes 393224 | tf_op jit(solution)/shard_map/ppermute | solution.py:36
  32.3 9.3 %collective-permute-start.2 = (bf16[256,512]{1,0:T(8,128)(2,1)S(1)}, bf16[256,512]{1,0:T(8,128)(2,1)S(1)}, u32[]{:S(2)}, u32[]{:S(2)}) collective-permute-start(bf16[256,512]{1,0:T(8,128)(2,1)S(1)} %constant_dynamic-slice_fusion), channel_id=1, source_target_pairs={{0,4},{1,5},{2,6},{3,7},{4,0},{5,1},{6,2},{7,3},{8,12},{9,13},{10,... | collective-permute-start | bytes 786440 | tf_op jit(solution)/shard_map/ppermute | solution.py:36
  32.4 9.3 %collective-permute-start.11 = (bf16[4,128,512]{2,1,0:T(8,128)(2,1)S(1)}, bf16[4,128,512]{2,1,0:T(8,128)(2,1)S(1)}, u32[]{:S(2)}, u32[]{:S(2)}) collective-permute-start(bf16[4,128,512]{2,1,0:T(8,128)(2,1)S(1)} %shard_map.78), channel_id=1, source_target_pairs={{0,1},{1,0},{2,3},{3,2},{4,5},{5,4},{6,7},{7,6},{8,9},{9,8},{10,11... | collective-permute-start | bytes 1572872 | tf_op jit(solution)/shard_map/ppermute | solution.py:48
  33.3 8.3 %collective-permute-start.10 = (f32[8,4096]{1,0:T(8,128)S(1)}, f32[8,4096]{1,0:T(8,128)S(1)}, u32[]{:S(2)}, u32[]{:S(2)}) collective-permute-start(f32[8,4096]{1,0:T(8,128)S(1)} %get-tuple-element.73), channel_id=1, source_target_pairs={{0,96},{8,104},{16,112},{24,120},{32,0},{40,8},{48,16},{56,24},{64... | collective-permute-start | bytes 393224 | tf_op jit(solution)/shard_map/ppermute | solution.py:40
  36.5 9.5 %collective-permute-start.9 = (f32[8,4096]{1,0:T(8,128)S(1)}, f32[8,4096]{1,0:T(8,128)S(1)}, u32[]{:S(2)}, u32[]{:S(2)}) collective-permute-start(f32[8,4096]{1,0:T(8,128)S(1)} %get-tuple-element.74), channel_id=1, source_target_pairs={{0,32},{8,40},{16,48},{24,56},{32,64},{40,72},{48,80},{56,88},{64,... | collective-permute-start | bytes 393224 | tf_op jit(solution)/shard_map/ppermute | solution.py:40
  50.2 24.7 %collective-permute-start.12 = (bf16[4,256,512]{2,1,0:T(8,128)(2,1)S(1)}, bf16[4,256,512]{2,1,0:T(8,128)(2,1)S(1)}, u32[]{:S(2)}, u32[]{:S(2)}) collective-permute-start(bf16[4,256,512]{2,1,0:T(8,128)(2,1)S(1)} %pad_maximum_fusion.refs_0_), channel_id=1, source_target_pairs={{0,96},{8,104},{16,112},{24,120},{32,0},{40,8},{48,16},{56,24},{64... | collective-permute-start | bytes 3145736 | tf_op jit(solution)/shard_map/ppermute | solution.py:40
  50.3 24.6 %collective-permute-start.19 = (bf16[4,256,512]{2,1,0:T(8,128)(2,1)S(1)}, bf16[4,256,512]{2,1,0:T(8,128)(2,1)S(1)}, u32[]{:S(2)}, u32[]{:S(2)}) collective-permute-start(bf16[4,256,512]{2,1,0:T(8,128)(2,1)S(1)} %pad_maximum_fusion.refs_0_), channel_id=1, source_target_pairs={{0,32},{8,40},{16,48},{24,56},{32,64},{40,72},{48,80},{56,88},{64,... | collective-permute-start | bytes 3145736 | tf_op jit(solution)/shard_map/ppermute | solution.py:40
  54.2 20.8 %collective-permute-start.22 = (bf16[4,256,512]{2,1,0:T(8,128)(2,1)S(1)}, bf16[4,256,512]{2,1,0:T(8,128)(2,1)S(1)}, u32[]{:S(2)}, u32[]{:S(2)}) collective-permute-start(bf16[4,256,512]{2,1,0:T(8,128)(2,1)S(1)} %pad_maximum_fusion.refs_0_), channel_id=1, source_target_pairs={{0,1},{1,0},{2,3},{3,2},{4,5},{5,4},{6,7},{7,6},{8,9},{9,8},{10,11... | collective-permute-start | bytes 3145736 | tf_op jit(solution)/shard_map/ppermute | solution.py:48
  56.3 8.5 %collective-permute-start.18 = (f32[8,4096]{1,0:T(8,128)S(1)}, f32[8,4096]{1,0:T(8,128)S(1)}, u32[]{:S(2)}, u32[]{:S(2)}) collective-permute-start(f32[8,4096]{1,0:T(8,128)S(1)} %add_add_fusion.3), channel_id=1, source_target_pairs={{0,24},{8,0},{16,8},{24,16},{32,56},{40,32},{48,40},{56,48},{64,88... | collective-permute-start | bytes 393224 | tf_op jit(solution)/shard_map/ppermute | solution.py:44
  61.4 8.8 %collective-permute-start.20 = (bf16[2,128,512]{2,1,0:T(8,128)(2,1)S(1)}, bf16[2,128,512]{2,1,0:T(8,128)(2,1)S(1)}, u32[]{:S(2)}, u32[]{:S(2)}) collective-permute-start(bf16[2,128,512]{2,1,0:T(8,128)(2,1)S(1)} %get-tuple-element.46), channel_id=1, source_target_pairs={{0,2},{1,3},{2,4},{3,5},{4,6},{5,7},{6,0},{7,1},{8,10},{9,11},{10,... | collective-permute-start | bytes 786440 | tf_op jit(solution)/shard_map/ppermute | solution.py:36
  64.8 7.4 %collective-permute-start.21 = (bf16[2,128,512]{2,1,0:T(8,128)(2,1)S(1)}, bf16[2,128,512]{2,1,0:T(8,128)(2,1)S(1)}, u32[]{:S(2)}, u32[]{:S(2)}) collective-permute-start(bf16[2,128,512]{2,1,0:T(8,128)(2,1)S(1)} %get-tuple-element.47), channel_id=1, source_target_pairs={{0,6},{1,7},{2,0},{3,1},{4,2},{5,3},{6,4},{7,5},{8,14},{9,15},{10,... | collective-permute-start | bytes 786440 | tf_op jit(solution)/shard_map/ppermute | solution.py:36
  77.7 15.3 %collective-permute-start.27 = (bf16[4,256,512]{2,1,0:T(8,128)(2,1)S(1)}, bf16[4,256,512]{2,1,0:T(8,128)(2,1)S(1)}, u32[]{:S(2)}, u32[]{:S(2)}) collective-permute-start(bf16[4,256,512]{2,1,0:T(8,128)(2,1)S(1)} %collective-permute-done.12.refs_1_), channel_id=1, source_target_pairs={{0,1},{1,0},{2,3},{3,2},{4,5},{5,4},{6,7},{7,6},{8,9},{9,8},{10,11... | collective-permute-start | bytes 3145736 | tf_op jit(solution)/shard_map/ppermute | solution.py:48
  80.5 12.5 %collective-permute-start.28 = (bf16[4,256,512]{2,1,0:T(8,128)(2,1)}, bf16[4,256,512]{2,1,0:T(8,128)(2,1)S(1)}, u32[]{:S(2)}, u32[]{:S(2)}) collective-permute-start(bf16[4,256,512]{2,1,0:T(8,128)(2,1)} %copy-done.8), channel_id=1, source_target_pairs={{0,1},{1,0},{2,3},{3,2},{4,5},{5,4},{6,7},{7,6},{8,9},{9,8},{10,11... | collective-permute-start | bytes 3145736 | tf_op jit(solution)/shard_map/ppermute | solution.py:48
  81.1 11.9 %collective-permute-start.29 = (bf16[2,128,512]{2,1,0:T(8,128)(2,1)S(1)}, bf16[2,128,512]{2,1,0:T(8,128)(2,1)S(1)}, u32[]{:S(2)}, u32[]{:S(2)}) collective-permute-start(bf16[2,128,512]{2,1,0:T(8,128)(2,1)S(1)} %get-tuple-element.54), channel_id=1, source_target_pairs={{0,4},{1,5},{2,6},{3,7},{4,0},{5,1},{6,2},{7,3},{8,12},{9,13},{10,... | collective-permute-start | bytes 786440 | tf_op jit(solution)/shard_map/ppermute | solution.py:36
  91.4 34.3 %collective-permute-start.26 = (bf16[4,256,512]{2,1,0:T(8,128)(2,1)S(1)}, bf16[4,256,512]{2,1,0:T(8,128)(2,1)S(1)}, u32[]{:S(2)}, u32[]{:S(2)}) collective-permute-start(bf16[4,256,512]{2,1,0:T(8,128)(2,1)S(1)} %pad_maximum_fusion.refs_0_), channel_id=1, source_target_pairs={{0,64},{8,72},{16,80},{24,88},{32,96},{40,104},{48,112},{56,120},{... | collective-permute-start | bytes 3145736 | tf_op jit(solution)/shard_map/ppermute | solution.py:40
  97.0 11.0 %collective-permute-start.33 = (f32[64,128]{1,0:T(8,128)S(1)}, f32[64,128]{1,0:T(8,128)S(1)}, u32[]{:S(2)}, u32[]{:S(2)}) collective-permute-start(f32[64,128]{1,0:T(8,128)S(1)} %get-tuple-element.58.u0), channel_id=1, source_target_pairs={{0,2},{1,3},{2,4},{3,5},{4,6},{5,7},{6,0},{7,1},{8,10},{9,11},{10,... | collective-permute-start | bytes 98312 | tf_op jit(solution)/shard_map/ppermute | solution.py:36
  99.0 9.0 %collective-permute-start.31 = (f32[64,128]{1,0:T(8,128)S(1)}, f32[64,128]{1,0:T(8,128)S(1)}, u32[]{:S(2)}, u32[]{:S(2)}) collective-permute-start(f32[64,128]{1,0:T(8,128)S(1)} %get-tuple-element.58.u0), channel_id=1, source_target_pairs={{0,6},{1,7},{2,0},{3,1},{4,2},{5,3},{6,4},{7,5},{8,14},{9,15},{10,... | collective-permute-start | bytes 98312 | tf_op jit(solution)/shard_map/ppermute | solution.py:36
  99.8 8.2 %collective-permute-start.32 = (f32[64,128]{1,0:T(8,128)S(1)}, f32[64,128]{1,0:T(8,128)S(1)}, u32[]{:S(2)}, u32[]{:S(2)}) collective-permute-start(f32[64,128]{1,0:T(8,128)S(1)} %get-tuple-element.58.u0), channel_id=1, source_target_pairs={{0,4},{1,5},{2,6},{3,7},{4,0},{5,1},{6,2},{7,3},{8,12},{9,13},{10,... | collective-permute-start | bytes 98312 | tf_op jit(solution)/shard_map/ppermute | solution.py:36
  111.2 14.6 %collective-permute-start.37 = (f32[64,512]{1,0:T(8,128)S(1)}, f32[64,512]{1,0:T(8,128)S(1)}, u32[]{:S(2)}, u32[]{:S(2)}) collective-permute-start(f32[64,512]{1,0:T(8,128)S(1)} %shard_map.83), channel_id=1, source_target_pairs={{0,24},{8,0},{16,8},{24,16},{32,56},{40,32},{48,40},{56,48},{64,88... | collective-permute-start | bytes 393224 | tf_op jit(solution)/shard_map/ppermute | solution.py:44
  116.7 9.0 %collective-permute-start.36 = (f32[64,512]{1,0:T(8,128)S(1)}, f32[64,512]{1,0:T(8,128)S(1)}, u32[]{:S(2)}, u32[]{:S(2)}) collective-permute-start(f32[64,512]{1,0:T(8,128)S(1)} %shard_map.83), channel_id=1, source_target_pairs={{0,8},{8,16},{16,24},{24,0},{32,40},{40,48},{48,56},{56,32},{64,72... | collective-permute-start | bytes 393224 | tf_op jit(solution)/shard_map/ppermute | solution.py:44
  116.7 9.0 %collective-permute-start.35 = (f32[64,512]{1,0:T(8,128)S(1)}, f32[64,512]{1,0:T(8,128)S(1)}, u32[]{:S(2)}, u32[]{:S(2)}) collective-permute-start(f32[64,512]{1,0:T(8,128)S(1)} %shard_map.83), channel_id=1, source_target_pairs={{0,16},{8,24},{16,0},{24,8},{32,48},{40,56},{48,32},{56,40},{64,80... | collective-permute-start | bytes 393224 | tf_op jit(solution)/shard_map/ppermute | solution.py:44
  126.8 15.0 %collective-permute-start.44 = (f32[64,512]{1,0:T(8,128)S(1)}, f32[64,512]{1,0:T(8,128)S(1)}, u32[]{:S(2)}, u32[]{:S(2)}) collective-permute-start(f32[64,512]{1,0:T(8,128)S(1)} %add_add_fusion.1), channel_id=1, source_target_pairs={{0,96},{8,104},{16,112},{24,120},{32,0},{40,8},{48,16},{56,24},{64... | collective-permute-start | bytes 393224 | tf_op jit(solution)/shard_map/ppermute | solution.py:40
  127.6 15.6 %collective-permute-start.43 = (f32[64,512]{1,0:T(8,128)S(1)}, f32[64,512]{1,0:T(8,128)S(1)}, u32[]{:S(2)}, u32[]{:S(2)}) collective-permute-start(f32[64,512]{1,0:T(8,128)S(1)} %add_add_fusion.1), channel_id=1, source_target_pairs={{0,32},{8,40},{16,48},{24,56},{32,64},{40,72},{48,80},{56,88},{64,... | collective-permute-start | bytes 393224 | tf_op jit(solution)/shard_map/ppermute | solution.py:40
  128.5 14.8 %collective-permute-start.42 = (f32[64,512]{1,0:T(8,128)S(1)}, f32[64,512]{1,0:T(8,128)S(1)}, u32[]{:S(2)}, u32[]{:S(2)}) collective-permute-start(f32[64,512]{1,0:T(8,128)S(1)} %add_add_fusion.1), channel_id=1, source_target_pairs={{0,64},{8,72},{16,80},{24,88},{32,96},{40,104},{48,112},{56,120},{... | collective-permute-start | bytes 393224 | tf_op jit(solution)/shard_map/ppermute | solution.py:40
  139.0 16.4 %collective-permute-start.41 = (bf16[128,1024]{1,0:T(8,128)(2,1)}, bf16[128,1024]{1,0:T(8,128)(2,1)S(1)}, u32[]{:S(2)}, u32[]{:S(2)}) collective-permute-start(bf16[128,1024]{1,0:T(8,128)(2,1)} %get-tuple-element.66), channel_id=1, source_target_pairs={{0,8},{8,16},{16,24},{24,0},{32,40},{40,48},{48,56},{56,32},{64,72... | collective-permute-start | bytes 786440 | tf_op jit(solution)/shard_map/ppermute | solution.py:44
  141.3 14.1 %collective-permute-start.39 = (bf16[128,1024]{1,0:T(8,128)(2,1)}, bf16[128,1024]{1,0:T(8,128)(2,1)S(1)}, u32[]{:S(2)}, u32[]{:S(2)}) collective-permute-start(bf16[128,1024]{1,0:T(8,128)(2,1)} %get-tuple-element.64), channel_id=1, source_target_pairs={{0,24},{8,0},{16,8},{24,16},{32,56},{40,32},{48,40},{56,48},{64,88... | collective-permute-start | bytes 786440 | tf_op jit(solution)/shard_map/ppermute | solution.py:44
  141.8 13.7 %collective-permute-start.40 = (bf16[128,1024]{1,0:T(8,128)(2,1)}, bf16[128,1024]{1,0:T(8,128)(2,1)S(1)}, u32[]{:S(2)}, u32[]{:S(2)}) collective-permute-start(bf16[128,1024]{1,0:T(8,128)(2,1)} %get-tuple-element.65), channel_id=1, source_target_pairs={{0,16},{8,24},{16,0},{24,8},{32,48},{40,56},{48,32},{56,40},{64,80... | collective-permute-start | bytes 786440 | tf_op jit(solution)/shard_map/ppermute | solution.py:44
  (27 other events, 234.6 us)
Sparse Core Ops, SparseCore 0:
  11.7 53.2 all-gather.5
  77.8 54.0 all-gather.3

commit v4 on v3

--- a/solution.py
+++ b/solution.py
@@ -105,9 +105,13 @@
     return slice(1024 * i, 1024 * i + 1024)
 
 
+EVEN = [columns(i) for i in range(4)]
+ENDS_SMALL = [slice(0, 512), slice(512, 1536), slice(1536, 2560), slice(2560, 3584), slice(3584, 4096)]
+
+
 class Fetch:
-    def __init__(self, source, held, arrived, ahead):
-        self.copies = [pltpu.make_async_copy(source.at[:, columns(i)], held.at[:, columns(i)], arrived.at[i]) for i in range(4)]
+    def __init__(self, source, held, arrived, ahead, parts=EVEN):
+        self.copies = [pltpu.make_async_copy(source.at[:, at], held.at[:, at], arrived.at[i]) for i, at in enumerate(parts)]
         self.ahead = ahead
         for copy in self.copies[:ahead]:
             copy.start()
@@ -323,27 +327,26 @@
 
 
 def last_body(inverse, w, turned, p_far, error, ctx, q_out, out, p, held, held_ctx, arrived, arrived_ctx, left_here, p_here):
-    ctx_blocks, blocks = Fetch(ctx, held_ctx, arrived_ctx, 1), Fetch(error, held, arrived, 1)
+    ctx_blocks, blocks = Fetch(ctx, held_ctx, arrived_ctx, 1, ENDS_SMALL), Fetch(error, held, arrived, 1, ENDS_SMALL)
     p_copy = pltpu.make_async_copy(p_far, p, p_here)
     p_copy.start()
     ctx_blocks.wait(0)
-    product = mm(turned[...], held_ctx[:, columns(0)])
+    product = mm(turned[...], held_ctx[:, ENDS_SMALL[0]])
     q = mm(inverse[...], w[...], NN, lax.Precision.HIGHEST) * (1.0 / 16)
     q_out[...] = q
     high, low = halves(q)
     q_split = jnp.concatenate([high, high, low], 0).T
     p_copy.wait()
     stores = []
-    for i in range(4):
-        at = columns(i)
+    for i, at in enumerate(ENDS_SMALL):
         approx = mm(q_split, p[:, at])
         blocks.wait(i)
         held[:, at] = (held[:, at] + product) - approx
         stores.append(pltpu.make_async_copy(held.at[:, at], out.at[:, at], left_here.at[i]))
         stores[-1].start()
-        if i < 3:
+        if i < 4:
             ctx_blocks.wait(i + 1)
-            product = mm(turned[...], held_ctx[:, columns(i + 1)])
+            product = mm(turned[...], held_ctx[:, ENDS_SMALL[i + 1]])
     for store in stores:
         store.wait()
 
@@ -356,20 +359,15 @@
         in_specs=[VMEM] * 3 + [HBM] * 3,
         out_specs=[VMEM, HBM],
         scratch_shapes=[pltpu.VMEM((192, 4096), BF16), pltpu.VMEM((512, 4096), F32), pltpu.VMEM((1024, 4096), BF16)]
-        + [pltpu.SemaphoreType.DMA((4,))] * 3
+        + [pltpu.SemaphoreType.DMA((5,))] * 3
         + [pltpu.SemaphoreType.DMA],
     )(inverse, w, turned, in_hbm(p), in_hbm(error), in_hbm(ctx))
 
 
 def share_body(place, tokens, *refs):
-    slabs, outs, (whole, held, done) = [*refs[:8]], refs[8:12], refs[12:]
-    copy = pltpu.make_async_copy(slabs[3], held, done)
-    copy.start()
-    slabs[3] = held
+    slabs, outs, whole = refs[:8], refs[8:12], refs[12]
     x, c, y, z = place[0], place[1], place[2], place[3]
     for e in range(4):
-        if e == 3:
-            copy.wait()
         total = jnp.zeros((512, 256), F32)
         for a in range(2):
             for d in range(4):
@@ -385,10 +383,10 @@
         share_body,
         [shaped((128, 1024), BF16)] * 4,
         mib=24,
-        in_specs=[SMEM] + [VMEM] * 4 + [HBM] + [VMEM] * 4,
+        in_specs=[SMEM] + [VMEM] * 9,
         out_specs=[VMEM] * 4,
-        scratch_shapes=[pltpu.VMEM((512, 1024), BF16), pltpu.VMEM((4, 256, 512), BF16), pltpu.SemaphoreType.DMA],
-    )(place, tokens, *mine[:3], in_hbm(mine[3]), *theirs)
+        scratch_shapes=[pltpu.VMEM((512, 1024), BF16)],
+    )(place, tokens, *mine, *theirs)
 
 
 def pair_sum(values):
@@ -423,21 +421,21 @@
     sends = cut(place, grad_out, after(passed, summed))
     chunk1, chunk3 = [along_x(sends[d], d) for d in (1, 3)]
     over_z = [summed] + [along_z(summed, d) for d in (1, 2, 3)]
-    their0 = other_core(after(w0, summed))
-    over_z[3] = after(over_z[3], w1, w3, chunk1, chunk3, their0)
+    over_z[3] = after(over_z[3], w1, w3, chunk1, chunk3)
     rows = pair_sum(over_z)
     ctx_all = lax.all_gather(after(ctx, rows, tokens), "fsdp", axis=0, tiled=True)
     p_near = [rows] + [along_y(rows, -d) for d in (1, 2, 3)]
     chunk2 = along_x(after(sends[2], rows), 2)
-    their1, their3 = [other_core(after(v, rows)) for v in (w1, w3)]
-    p_far = other_core(jnp.concatenate([rows, after(p_near[1], their1, their3, chunk2), *p_near[2:]], 0))
+    their1 = other_core(after(w1, rows))
+    p_far = other_core(jnp.concatenate([rows, after(p_near[1], their1, chunk2), *p_near[2:]], 0))
     w2 = along_y(after(w0, *p_near), 2)
 
-    p_raw, u = middle(place, p_near, p_far, ctx)
+    turned = turn(place, [sends[0], chunk1, chunk2, chunk3])
+    p_raw, u = middle(place, p_near, after(p_far, turned), ctx)
     u_near = [u] + [along_x(u, -d) for d in (1, 2, 3)]
     w_term = right(p_raw, error)
-    turned = turn(place, [sends[0], chunk1, chunk2, chunk3])
-    u_far = other_core(jnp.concatenate([u, u_near[1], u_near[2], after(u_near[3], w_term, turned)], 0))
+    their0, their3 = other_core(after(w0, u)), other_core(after(w3, u))
+    u_far = other_core(jnp.concatenate([u, u_near[1], u_near[2], after(u_near[3], w_term, their0, their3)], 0))
     w = collect(place, w_term, turned, u_near, u_far)
     w = [w] + [along_z(w, d) for d in (1, 2, 3)]
     inverse, p = solve(p_raw)

time: 164 us -> 158 us (0.963)
  Pallas kernels: 47.3 us -> 43.6 us
  starting transfers between devices: 60.5 us -> 57.5 us
    pallas_call x1, Pallas kernels: 8.32 us -> 5.13 us  [share(): pallas(share_body, [shaped((128, 1024), BF16)] * 4, mib=24, in_specs=[SME...]
    ppermute x12, waiting for transfers between devices: 12.2 us -> 15 us  [along_y(): lax.ppermute(value, 'dp', [(i, (i // 4 + d) % 4 * 4 + i % 4) for i in ran...]
    ppermute x15, starting transfers between devices: 20.3 us -> 18 us  [along_x(): lax.ppermute(value, 'fsdp', [(i, (i // 2 + d) % 4 * 2 + i % 2) for i in r...]
    ppermute x9, waiting for transfers between devices: 3.82 us -> 1.97 us  [along_z(): lax.ppermute(value, 'dp', [(i, i // 4 * 4 + (i % 4 + d) % 4) for i in ran...]
  transfers between devices with their start and end apart: 47 -> 47, of which waited for: 18 -> 18; matrix products, arithmetic and copies ran while one was open for 1% -> 2% of each run, Pallas kernels for 28% -> 27%
where the time goes in v4:
time: 158 us
  starting transfers between devices  57.5 us (36%)
  Pallas kernels  43.6 us (28%)
  waiting for transfers between devices  36.7 us (23%)
  between operations  14.5 us (9%)
  local copies, waits for them, and re-layouts  4.83 us (3%)
    ppermute x15, starting transfers between devices, along_x(): lax.ppermute(value, 'fsdp', [(i, (i // 2 + d) % 4 * 2 + i % 2) for i in r...  18 us
    ppermute x9, starting transfers between devices, along_z(): lax.ppermute(value, 'dp', [(i, i // 4 * 4 + (i % 4 + d) % 4) for i in ran...  17.5 us
    ppermute x15, waiting for transfers between devices, along_x(): lax.ppermute(value, 'fsdp', [(i, (i // 2 + d) % 4 * 2 + i % 2) for i in r...  15.8 us
    ppermute x12, waiting for transfers between devices, along_y(): lax.ppermute(value, 'dp', [(i, (i // 4 + d) % 4 * 4 + i % 4) for i in ran...  15 us
    ppermute x12, starting transfers between devices, along_y(): lax.ppermute(value, 'dp', [(i, (i // 4 + d) % 4 * 4 + i % 4) for i in ran...  11.8 us
    pallas_call x1, Pallas kernels, last(): pallas(last_body, [shaped((64, 512)), shaped((512, 4096))], mib=24, in_sp...  11.6 us
    ppermute x9, starting transfers between devices, other_core(): return lax.ppermute(value, 'fsdp', [(i, i ^ 1) for i in range(8)])  10 us
    pallas_call x1, Pallas kernels, solve(): pallas(solve_body, [shaped((64, 64)), pltpu.HBM((192, 4096), BF16)], in_s...  7.75 us
  transfers between devices with their start and end apart: 47, of which 18 were waited for; matrix products, arithmetic and copies ran while one was open for 2% of the time, Pallas kernels for 27%

profile of v4, /device:TPU:1, one launch (start us, length us, event | category | flops | bytes accessed | tf_op | source)
XLA Modules:
  0.0 157.6 jit_solution(9210937734405043110)
XLA Ops:
  8.9 3.4 %collective-permute-start.3 = (bf16[256,512]{1,0:T(8,128)(2,1)S(1)}, bf16[256,512]{1,0:T(8,128)(2,1)S(1)}, u32[]{:S(2)}, u32[]{:S(2)}) collective-permute-start(bf16[256,512]{1,0:T(8,128)(2,1)S(1)} %constant_dynamic-slice_fusion), channel_id=1, source_target_pairs={{0,6},{1,7},{2,0},{3,1},{4,2},{5,3},{6,4},{7,5},{8,14},{9,15},{10,... | collective-permute-start | bytes 786440 | tf_op jit(solution)/shard_map/ppermute | solution.py:36
  12.3 2.7 %collective-permute-start.1 = (f32[64,512]{1,0:T(8,128)}, f32[64,512]{1,0:T(8,128)S(1)}, u32[]{:S(2)}, u32[]{:S(2)}) collective-permute-start(f32[64,512]{1,0:T(8,128)} %bitcast.15), channel_id=1, source_target_pairs={{0,6},{1,7},{2,0},{3,1},{4,2},{5,3},{6,4},{7,5},{8,14},{9,15},{10,... | collective-permute-start | bytes 393224 | tf_op jit(solution)/shard_map/ppermute | solution.py:36
  16.6 4.6 %shard_map.76.term = f32[64,4096]{1,0:T(8,128)S(1)} custom-call(s32[4]{0:T(128)S(1)} %pad_add_fusion.place, f32[64,512]{1,0:T(8,128)S(1)} %bitcast.18, f32[512,4096]{1,0:T(8,128)} %bitcast.21), custom_call_target="tpu_custom_call" | custom-call | tf_op jit(solution)/shard_map/pallas_call | solution.py:142
  22.2 3.8 %collective-permute-done.5.q3 = f32[64,512]{1,0:T(8,128)S(1)} collective-permute-done((f32[64,512]{1,0:T(8,128)}, f32[64,512]{1,0:T(8,128)S(1)}, u32[]{:S(2)}, u32[]{:S(2)}) %collective-permute-start.5) | collective-permute-done | bytes 131104 | tf_op jit(solution)/shard_map/ppermute | solution.py:36
  26.1 1.9 %collective-permute-start.6 = (f32[256,512]{1,0:T(8,128)S(1)}, f32[256,512]{1,0:T(8,128)S(1)}, u32[]{:S(2)}, u32[]{:S(2)}) collective-permute-start(f32[256,512]{1,0:T(8,128)S(1)} %pad_maximum_fusion.1), channel_id=1, source_target_pairs={{0,1},{1,0},{2,3},{3,2},{4,5},{5,4},{6,7},{7,6},{8,9},{9,8},{10,11... | collective-permute-start | bytes 1572872 | tf_op jit(solution)/shard_map/ppermute | solution.py:48
  29.6 2.4 %shard_map.77 = (f32[32,4096]{1,0:T(8,128)S(1)}, f32[32,4096]{1,0:T(8,128)S(1)}) custom-call(s32[4]{0:T(128)S(1)} %pad_add_fusion.place, f32[64,512]{1,0:T(8,128)S(1)} %bitcast.20, f32[64,512]{1,0:T(8,128)S(1)} %collective-permute-done.1.q1, f32[64,512]{1,0:T(8,128)S(1)} %collective-permute-done.4.q2, f32[64,512]{1,0:T(8,128)S(1)} %collective-permute-done.5.q3, ...), custom_call_target="tpu_custom_call" | custom-call | tf_op jit(solution)/shard_map/pallas_call | solution.py:172
  34.1 2.8 %collective-permute-start.10 = (f32[8,4096]{1,0:T(8,128)S(1)}, f32[8,4096]{1,0:T(8,128)S(1)}, u32[]{:S(2)}, u32[]{:S(2)}) collective-permute-start(f32[8,4096]{1,0:T(8,128)S(1)} %get-tuple-element.75), channel_id=1, source_target_pairs={{0,96},{8,104},{16,112},{24,120},{32,0},{40,8},{48,16},{56,24},{64... | collective-permute-start | bytes 393224 | tf_op jit(solution)/shard_map/ppermute | solution.py:40
  38.9 3.5 %collective-permute-done.2 = bf16[256,512]{1,0:T(8,128)(2,1)S(1)} collective-permute-done((bf16[256,512]{1,0:T(8,128)(2,1)S(1)}, bf16[256,512]{1,0:T(8,128)(2,1)S(1)}, u32[]{:S(2)}, u32[]{:S(2)}) %collective-permute-start.2) | collective-permute-done | bytes 262176 | tf_op jit(solution)/shard_map/ppermute | solution.py:36
  42.8 3.9 %collective-permute-done.9 = f32[8,4096]{1,0:T(8,128)S(1)} collective-permute-done((f32[8,4096]{1,0:T(8,128)S(1)}, f32[8,4096]{1,0:T(8,128)S(1)}, u32[]{:S(2)}, u32[]{:S(2)}) %collective-permute-start.9) | collective-permute-done | bytes 131104 | tf_op jit(solution)/shard_map/ppermute | solution.py:40
  47.8 1.7 %collective-permute-start.15 = (f32[8,4096]{1,0:T(8,128)S(1)}, f32[8,4096]{1,0:T(8,128)S(1)}, u32[]{:S(2)}, u32[]{:S(2)}) collective-permute-start(f32[8,4096]{1,0:T(8,128)S(1)} %fusion), channel_id=1, source_target_pairs={{0,6},{1,7},{2,0},{3,1},{4,2},{5,3},{6,4},{7,5},{8,14},{9,15},{10,... | collective-permute-start | bytes 393224 | tf_op jit(solution)/shard_map/ppermute | solution.py:36
  52.8 2.0 %collective-permute-done.13 = f32[8,4096]{1,0:T(8,128)S(1)} collective-permute-done((f32[8,4096]{1,0:T(8,128)S(1)}, f32[8,4096]{1,0:T(8,128)S(1)}, u32[]{:S(2)}, u32[]{:S(2)}) %collective-permute-start.13) | collective-permute-done | bytes 131104 | tf_op jit(solution)/shard_map/ppermute | solution.py:36
  56.2 1.6 %collective-permute-start.20 = (bf16[2,128,512]{2,1,0:T(8,128)(2,1)S(1)}, bf16[2,128,512]{2,1,0:T(8,128)(2,1)S(1)}, u32[]{:S(2)}, u32[]{:S(2)}) collective-permute-start(bf16[2,128,512]{2,1,0:T(8,128)(2,1)S(1)} %get-tuple-element.47), channel_id=1, source_target_pairs={{0,2},{1,3},{2,4},{3,5},{4,6},{5,7},{6,0},{7,1},{8,10},{9,11},{10,... | collective-permute-start | bytes 786440 | tf_op jit(solution)/shard_map/ppermute | solution.py:36
  58.9 3.8 %collective-permute-start.18 = (f32[8,4096]{1,0:T(8,128)S(1)}, f32[8,4096]{1,0:T(8,128)S(1)}, u32[]{:S(2)}, u32[]{:S(2)}) collective-permute-start(f32[8,4096]{1,0:T(8,128)S(1)} %add_add_fusion.3), channel_id=1, source_target_pairs={{0,24},{8,0},{16,8},{24,16},{32,56},{40,32},{48,40},{56,48},{64,88... | collective-permute-start | bytes 393224 | tf_op jit(solution)/shard_map/ppermute | solution.py:44
  62.7 1.9 %collective-permute-done.18 = f32[8,4096]{1,0:T(8,128)S(1)} collective-permute-done((f32[8,4096]{1,0:T(8,128)S(1)}, f32[8,4096]{1,0:T(8,128)S(1)}, u32[]{:S(2)}, u32[]{:S(2)}) %collective-permute-start.18) | collective-permute-done | bytes 131104 | tf_op jit(solution)/shard_map/ppermute | solution.py:44
  64.7 4.5 %collective-permute-start.16 = (f32[8,4096]{1,0:T(8,128)S(1)}, f32[8,4096]{1,0:T(8,128)S(1)}, u32[]{:S(2)}, u32[]{:S(2)}) collective-permute-start(f32[8,4096]{1,0:T(8,128)S(1)} %add_add_fusion.3), channel_id=1, source_target_pairs={{0,16},{8,24},{16,0},{24,8},{32,48},{40,56},{48,32},{56,40},{64,80... | collective-permute-start | bytes 393224 | tf_op jit(solution)/shard_map/ppermute | solution.py:44
  69.2 5.3 %collective-permute-done.12.refs_1_ = bf16[4,256,512]{2,1,0:T(8,128)(2,1)S(1)} collective-permute-done((bf16[4,256,512]{2,1,0:T(8,128)(2,1)S(1)}, bf16[4,256,512]{2,1,0:T(8,128)(2,1)S(1)}, u32[]{:S(2)}, u32[]{:S(2)}) %collective-permute-start.12) | collective-permute-done | bytes 1048608 | tf_op jit(solution)/shard_map/ppermute | solution.py:40
  76.3 2.8 %collective-permute-start.26 = (bf16[4,256,512]{2,1,0:T(8,128)(2,1)}, bf16[4,256,512]{2,1,0:T(8,128)(2,1)S(1)}, u32[]{:S(2)}, u32[]{:S(2)}) collective-permute-start(bf16[4,256,512]{2,1,0:T(8,128)(2,1)} %copy-done.5), channel_id=1, source_target_pairs={{0,1},{1,0},{2,3},{3,2},{4,5},{5,4},{6,7},{7,6},{8,9},{9,8},{10,11... | collective-permute-start | bytes 3145736 | tf_op jit(solution)/shard_map/ppermute | solution.py:48
  79.1 1.6 %collective-permute-start.27 = (bf16[2,128,512]{2,1,0:T(8,128)(2,1)S(1)}, bf16[2,128,512]{2,1,0:T(8,128)(2,1)S(1)}, u32[]{:S(2)}, u32[]{:S(2)}) collective-permute-start(bf16[2,128,512]{2,1,0:T(8,128)(2,1)S(1)} %get-tuple-element.53), channel_id=1, source_target_pairs={{0,4},{1,5},{2,6},{3,7},{4,0},{5,1},{6,2},{7,3},{8,12},{9,13},{10,... | collective-permute-start | bytes 786440 | tf_op jit(solution)/shard_map/ppermute | solution.py:36
  81.0 1.7 %collective-permute-start.23 = (f32[8,4096]{1,0:T(8,128)S(1)}, f32[8,4096]{1,0:T(8,128)S(1)}, u32[]{:S(2)}, u32[]{:S(2)}) collective-permute-start(f32[8,4096]{1,0:T(8,128)S(1)} %add_add_fusion.2.p0), channel_id=1, source_target_pairs={{0,64},{8,72},{16,80},{24,88},{32,96},{40,104},{48,112},{56,120},{... | collective-permute-start | bytes 393224 | tf_op jit(solution)/shard_map/ppermute | solution.py:40
  82.7 2.8 %collective-permute-done.22.p1 = f32[8,4096]{1,0:T(8,128)S(1)} collective-permute-done((f32[8,4096]{1,0:T(8,128)S(1)}, f32[8,4096]{1,0:T(8,128)S(1)}, u32[]{:S(2)}, u32[]{:S(2)}) %collective-permute-start.22) | collective-permute-done | bytes 131104 | tf_op jit(solution)/shard_map/ppermute | solution.py:40
  85.4 3.0 %collective-permute-done.27.c2 = bf16[2,128,512]{2,1,0:T(8,128)(2,1)S(1)} collective-permute-done((bf16[2,128,512]{2,1,0:T(8,128)(2,1)S(1)}, bf16[2,128,512]{2,1,0:T(8,128)(2,1)S(1)}, u32[]{:S(2)}, u32[]{:S(2)}) %collective-permute-start.27) | collective-permute-done | bytes 262176 | tf_op jit(solution)/shard_map/ppermute | solution.py:36
  88.5 1.8 %collective-permute-done.24.p3 = f32[8,4096]{1,0:T(8,128)S(1)} collective-permute-done((f32[8,4096]{1,0:T(8,128)S(1)}, f32[8,4096]{1,0:T(8,128)S(1)}, u32[]{:S(2)}, u32[]{:S(2)}) %collective-permute-start.24) | collective-permute-done | bytes 131104 | tf_op jit(solution)/shard_map/ppermute | solution.py:40
  91.3 2.1 %shard_map.80.turned = bf16[512,1024]{1,0:T(8,128)(2,1)S(1)} custom-call(s32[4]{0:T(128)S(1)} %pad_add_fusion.place, bf16[2,128,512]{2,1,0:T(8,128)(2,1)} %copy-done.9, bf16[2,128,512]{2,1,0:T(8,128)(2,1)} %copy-done.10, bf16[2,128,512]{2,1,0:T(8,128)(2,1)} %copy-done.12, bf16[2,128,512]{2,1,0:T(8,128)(2,1)} %copy-done.11), custom_call_target="tpu_custom_call" | custom-call | tf_op jit(solution)/shard_map/pallas_call | solution.py:214
  96.7 2.7 %collective-permute-start.30 = (f32[64,128]{1,0:T(8,128)S(1)}, f32[64,128]{1,0:T(8,128)S(1)}, u32[]{:S(2)}, u32[]{:S(2)}) collective-permute-start(f32[64,128]{1,0:T(8,128)S(1)} %get-tuple-element.57.u0), channel_id=1, source_target_pairs={{0,6},{1,7},{2,0},{3,1},{4,2},{5,3},{6,4},{7,5},{8,14},{9,15},{10,... | collective-permute-start | bytes 98312 | tf_op jit(solution)/shard_map/ppermute | solution.py:36
  99.4 2.4 %collective-permute-done.32.u3 = f32[64,128]{1,0:T(8,128)S(1)} collective-permute-done((f32[64,128]{1,0:T(8,128)S(1)}, f32[64,128]{1,0:T(8,128)S(1)}, u32[]{:S(2)}, u32[]{:S(2)}) %collective-permute-start.32) | collective-permute-done | bytes 32800 | tf_op jit(solution)/shard_map/ppermute | solution.py:36
  102.0 5.0 %shard_map.82.term = f32[512,64]{1,0:T(8,128)S(1)} custom-call(f32[64,4096]{1,0:T(8,128)S(1)} %get-tuple-element.59.p_raw, f32[512,4096]{1,0:T(8,128)} %bitcast.22), custom_call_target="tpu_custom_call" | custom-call | tf_op jit(solution)/shard_map/pallas_call | solution.py:259
  107.1 2.0 %collective-permute-start.34 = (f32[256,128]{1,0:T(8,128)S(1)}, f32[256,128]{1,0:T(8,128)S(1)}, u32[]{:S(2)}, u32[]{:S(2)}) collective-permute-start(f32[256,128]{1,0:T(8,128)S(1)} %pad_maximum_fusion.3), channel_id=1, source_target_pairs={{0,1},{1,0},{2,3},{3,2},{4,5},{5,4},{6,7},{7,6},{8,9},{9,8},{10,11... | collective-permute-start | bytes 393224 | tf_op jit(solution)/shard_map/ppermute | solution.py:48
  111.2 4.0 %collective-permute-start.37 = (f32[64,512]{1,0:T(8,128)S(1)}, f32[64,512]{1,0:T(8,128)S(1)}, u32[]{:S(2)}, u32[]{:S(2)}) collective-permute-start(f32[64,512]{1,0:T(8,128)S(1)} %shard_map.83), channel_id=1, source_target_pairs={{0,24},{8,0},{16,8},{24,16},{32,56},{40,32},{48,40},{56,48},{64,88... | collective-permute-start | bytes 393224 | tf_op jit(solution)/shard_map/ppermute | solution.py:44
  116.5 7.8 %shard_map.84 = (f32[64,64]{1,0:T(8,128)S(1)}, bf16[192,4096]{1,0:T(8,128)(2,1)}) custom-call(f32[64,4096]{1,0:T(8,128)S(1)} %get-tuple-element.59.p_raw), custom_call_target="tpu_custom_call" | custom-call | tf_op jit(solution)/shard_map/pallas_call | solution.py:320
  128.4 5.1 %shard_map.85 = (bf16[128,1024]{1,0:T(8,128)(2,1)S(1)}, bf16[128,1024]{1,0:T(8,128)(2,1)S(1)}, bf16[128,1024]{1,0:T(8,128)(2,1)S(1)}, bf16[128,1024]{1,0:T(8,128)(2,1)S(1)}) custom-call(s32[4]{0:T(128)S(1)} %pad_add_fusion.place, bf16[4,128,4096]{2,1,0:T(8,128)(2,1)S(1)} %bitcast.14, bf16[4,256,512]{2,1,0:T(8,128)(2,1)S(1)} %pad_maximum_fusion.refs_0_, ...), custom_call_target="tpu_custom_call" | custom-call | tf_op jit(solution)/shard_map/pallas_call | solution.py:382
  133.5 2.1 %collective-permute-start.41 = (bf16[128,1024]{1,0:T(8,128)(2,1)S(1)}, bf16[128,1024]{1,0:T(8,128)(2,1)S(1)}, u32[]{:S(2)}, u32[]{:S(2)}) collective-permute-start(bf16[128,1024]{1,0:T(8,128)(2,1)S(1)} %get-tuple-element.68), channel_id=1, source_target_pairs={{0,8},{8,16},{16,24},{24,0},{32,40},{40,48},{48,56},{56,32},{64,72... | collective-permute-start | bytes 786440 | tf_op jit(solution)/shard_map/ppermute | solution.py:44
  137.6 11.6 %shard_map.86 = (f32[64,512]{1,0:T(8,128)}, f32[512,4096]{1,0:T(8,128)}) custom-call(f32[64,64]{1,0:T(8,128)S(1)} %get-tuple-element.69.inverse, f32[64,512]{1,0:T(8,128)S(1)} %add_add_fusion.w, bf16[512,1024]{1,0:T(8,128)(2,1)S(1)} %shard_map.80.turned, bf16[192,4096]{1,0:T(8,128)(2,1)} %get-tuple-element.62.p_far, f32[512,4096]{1,0:T(8,128)} %bitcast.23, ...), custom_call_target="tpu_custom_call" | custom-call | tf_op jit(solution)/shard_map/pallas_call | solution.py:355
  (124 shorter events, 34.8 us)
Async XLA Ops:
  7.2 69.1 %all-gather.6.cloned.1.call-start = ((), (), s32[]{:S(2)}) async-start(), calls=%async_computation.1 | async-start | bytes 5242880 | tf_op jit(solution)/shard_map/all_gather | solution.py:403
  7.9 129.7 %all-gather.4.cloned.1.call-start = ((), (), s32[]{:S(2)}) async-start(), calls=%async_computation | async-start | bytes 9437184 | tf_op jit(solution)/shard_map/all_gather | solution.py:426
  8.9 12.5 %collective-permute-start.3 = (bf16[256,512]{1,0:T(8,128)(2,1)S(1)}, bf16[256,512]{1,0:T(8,128)(2,1)S(1)}, u32[]{:S(2)}, u32[]{:S(2)}) collective-permute-start(bf16[256,512]{1,0:T(8,128)(2,1)S(1)} %constant_dynamic-slice_fusion), channel_id=1, source_target_pairs={{0,6},{1,7},{2,0},{3,1},{4,2},{5,3},{6,4},{7,5},{8,14},{9,15},{10,... | collective-permute-start | bytes 786440 | tf_op jit(solution)/shard_map/ppermute | solution.py:36
  12.3 9.1 %collective-permute-start = (bf16[256,512]{1,0:T(8,128)(2,1)S(1)}, bf16[256,512]{1,0:T(8,128)(2,1)S(1)}, u32[]{:S(2)}, u32[]{:S(2)}) collective-permute-start(bf16[256,512]{1,0:T(8,128)(2,1)S(1)} %constant_dynamic-slice_fusion), channel_id=1, source_target_pairs={{0,2},{1,3},{2,4},{3,5},{4,6},{5,7},{6,0},{7,1},{8,10},{9,11},{10,... | collective-permute-start | bytes 786440 | tf_op jit(solution)/shard_map/ppermute | solution.py:36
  12.3 9.1 %collective-permute-start.1 = (f32[64,512]{1,0:T(8,128)}, f32[64,512]{1,0:T(8,128)S(1)}, u32[]{:S(2)}, u32[]{:S(2)}) collective-permute-start(f32[64,512]{1,0:T(8,128)} %bitcast.15), channel_id=1, source_target_pairs={{0,6},{1,7},{2,0},{3,1},{4,2},{5,3},{6,4},{7,5},{8,14},{9,15},{10,... | collective-permute-start | bytes 393224 | tf_op jit(solution)/shard_map/ppermute | solution.py:36
  15.0 11.0 %collective-permute-start.5 = (f32[64,512]{1,0:T(8,128)}, f32[64,512]{1,0:T(8,128)S(1)}, u32[]{:S(2)}, u32[]{:S(2)}) collective-permute-start(f32[64,512]{1,0:T(8,128)} %bitcast.17), channel_id=1, source_target_pairs={{0,2},{1,3},{2,4},{3,5},{4,6},{5,7},{6,0},{7,1},{8,10},{9,11},{10,... | collective-permute-start | bytes 393224 | tf_op jit(solution)/shard_map/ppermute | solution.py:36
  33.1 9.3 %collective-permute-start.2 = (bf16[256,512]{1,0:T(8,128)(2,1)S(1)}, bf16[256,512]{1,0:T(8,128)(2,1)S(1)}, u32[]{:S(2)}, u32[]{:S(2)}) collective-permute-start(bf16[256,512]{1,0:T(8,128)(2,1)S(1)} %constant_dynamic-slice_fusion), channel_id=1, source_target_pairs={{0,4},{1,5},{2,6},{3,7},{4,0},{5,1},{6,2},{7,3},{8,12},{9,13},{10,... | collective-permute-start | bytes 786440 | tf_op jit(solution)/shard_map/ppermute | solution.py:36
  33.1 9.3 %collective-permute-start.11 = (bf16[4,128,512]{2,1,0:T(8,128)(2,1)S(1)}, bf16[4,128,512]{2,1,0:T(8,128)(2,1)S(1)}, u32[]{:S(2)}, u32[]{:S(2)}) collective-permute-start(bf16[4,128,512]{2,1,0:T(8,128)(2,1)S(1)} %shard_map.78), channel_id=1, source_target_pairs={{0,1},{1,0},{2,3},{3,2},{4,5},{5,4},{6,7},{7,6},{8,9},{9,8},{10,11... | collective-permute-start | bytes 1572872 | tf_op jit(solution)/shard_map/ppermute | solution.py:48
  34.1 8.3 %collective-permute-start.10 = (f32[8,4096]{1,0:T(8,128)S(1)}, f32[8,4096]{1,0:T(8,128)S(1)}, u32[]{:S(2)}, u32[]{:S(2)}) collective-permute-start(f32[8,4096]{1,0:T(8,128)S(1)} %get-tuple-element.75), channel_id=1, source_target_pairs={{0,96},{8,104},{16,112},{24,120},{32,0},{40,8},{48,16},{56,24},{64... | collective-permute-start | bytes 393224 | tf_op jit(solution)/shard_map/ppermute | solution.py:40
  37.2 9.5 %collective-permute-start.9 = (f32[8,4096]{1,0:T(8,128)S(1)}, f32[8,4096]{1,0:T(8,128)S(1)}, u32[]{:S(2)}, u32[]{:S(2)}) collective-permute-start(f32[8,4096]{1,0:T(8,128)S(1)} %get-tuple-element.76), channel_id=1, source_target_pairs={{0,32},{8,40},{16,48},{24,56},{32,64},{40,72},{48,80},{56,88},{64,... | collective-permute-start | bytes 393224 | tf_op jit(solution)/shard_map/ppermute | solution.py:40
  51.0 23.5 %collective-permute-start.12 = (bf16[4,256,512]{2,1,0:T(8,128)(2,1)S(1)}, bf16[4,256,512]{2,1,0:T(8,128)(2,1)S(1)}, u32[]{:S(2)}, u32[]{:S(2)}) collective-permute-start(bf16[4,256,512]{2,1,0:T(8,128)(2,1)S(1)} %pad_maximum_fusion.refs_0_), channel_id=1, source_target_pairs={{0,96},{8,104},{16,112},{24,120},{32,0},{40,8},{48,16},{56,24},{64... | collective-permute-start | bytes 3145736 | tf_op jit(solution)/shard_map/ppermute | solution.py:40
  51.1 24.2 %collective-permute-start.19 = (bf16[4,256,512]{2,1,0:T(8,128)(2,1)S(1)}, bf16[4,256,512]{2,1,0:T(8,128)(2,1)S(1)}, u32[]{:S(2)}, u32[]{:S(2)}) collective-permute-start(bf16[4,256,512]{2,1,0:T(8,128)(2,1)S(1)} %pad_maximum_fusion.refs_0_), channel_id=1, source_target_pairs={{0,32},{8,40},{16,48},{24,56},{32,64},{40,72},{48,80},{56,88},{64,... | collective-permute-start | bytes 3145736 | tf_op jit(solution)/shard_map/ppermute | solution.py:40
  56.2 8.5 %collective-permute-start.20 = (bf16[2,128,512]{2,1,0:T(8,128)(2,1)S(1)}, bf16[2,128,512]{2,1,0:T(8,128)(2,1)S(1)}, u32[]{:S(2)}, u32[]{:S(2)}) collective-permute-start(bf16[2,128,512]{2,1,0:T(8,128)(2,1)S(1)} %get-tuple-element.47), channel_id=1, source_target_pairs={{0,2},{1,3},{2,4},{3,5},{4,6},{5,7},{6,0},{7,1},{8,10},{9,11},{10,... | collective-permute-start | bytes 786440 | tf_op jit(solution)/shard_map/ppermute | solution.py:36
  57.9 11.3 %collective-permute-start.21 = (bf16[2,128,512]{2,1,0:T(8,128)(2,1)S(1)}, bf16[2,128,512]{2,1,0:T(8,128)(2,1)S(1)}, u32[]{:S(2)}, u32[]{:S(2)}) collective-permute-start(bf16[2,128,512]{2,1,0:T(8,128)(2,1)S(1)} %get-tuple-element.48), channel_id=1, source_target_pairs={{0,6},{1,7},{2,0},{3,1},{4,2},{5,3},{6,4},{7,5},{8,14},{9,15},{10,... | collective-permute-start | bytes 786440 | tf_op jit(solution)/shard_map/ppermute | solution.py:36
  64.6 10.6 %collective-permute-start.17 = (f32[8,4096]{1,0:T(8,128)S(1)}, f32[8,4096]{1,0:T(8,128)S(1)}, u32[]{:S(2)}, u32[]{:S(2)}) collective-permute-start(f32[8,4096]{1,0:T(8,128)S(1)} %add_add_fusion.3), channel_id=1, source_target_pairs={{0,8},{8,16},{16,24},{24,0},{32,40},{40,48},{48,56},{56,32},{64,72... | collective-permute-start | bytes 393224 | tf_op jit(solution)/shard_map/ppermute | solution.py:44
  64.7 10.8 %collective-permute-start.16 = (f32[8,4096]{1,0:T(8,128)S(1)}, f32[8,4096]{1,0:T(8,128)S(1)}, u32[]{:S(2)}, u32[]{:S(2)}) collective-permute-start(f32[8,4096]{1,0:T(8,128)S(1)} %add_add_fusion.3), channel_id=1, source_target_pairs={{0,16},{8,24},{16,0},{24,8},{32,48},{40,56},{48,32},{56,40},{64,80... | collective-permute-start | bytes 393224 | tf_op jit(solution)/shard_map/ppermute | solution.py:44
  76.3 12.1 %collective-permute-start.26 = (bf16[4,256,512]{2,1,0:T(8,128)(2,1)}, bf16[4,256,512]{2,1,0:T(8,128)(2,1)S(1)}, u32[]{:S(2)}, u32[]{:S(2)}) collective-permute-start(bf16[4,256,512]{2,1,0:T(8,128)(2,1)} %copy-done.5), channel_id=1, source_target_pairs={{0,1},{1,0},{2,3},{3,2},{4,5},{5,4},{6,7},{7,6},{8,9},{9,8},{10,11... | collective-permute-start | bytes 3145736 | tf_op jit(solution)/shard_map/ppermute | solution.py:48
  79.1 9.4 %collective-permute-start.27 = (bf16[2,128,512]{2,1,0:T(8,128)(2,1)S(1)}, bf16[2,128,512]{2,1,0:T(8,128)(2,1)S(1)}, u32[]{:S(2)}, u32[]{:S(2)}) collective-permute-start(bf16[2,128,512]{2,1,0:T(8,128)(2,1)S(1)} %get-tuple-element.53), channel_id=1, source_target_pairs={{0,4},{1,5},{2,6},{3,7},{4,0},{5,1},{6,2},{7,3},{8,12},{9,13},{10,... | collective-permute-start | bytes 786440 | tf_op jit(solution)/shard_map/ppermute | solution.py:36
  82.7 7.6 %collective-permute-start.24 = (f32[8,4096]{1,0:T(8,128)S(1)}, f32[8,4096]{1,0:T(8,128)S(1)}, u32[]{:S(2)}, u32[]{:S(2)}) collective-permute-start(f32[8,4096]{1,0:T(8,128)S(1)} %add_add_fusion.2.p0), channel_id=1, source_target_pairs={{0,32},{8,40},{16,48},{24,56},{32,64},{40,72},{48,80},{56,88},{64,... | collective-permute-start | bytes 393224 | tf_op jit(solution)/shard_map/ppermute | solution.py:40
  94.6 12.4 %collective-permute-start.29 = (bf16[4,256,512]{2,1,0:T(8,128)(2,1)S(1)}, bf16[4,256,512]{2,1,0:T(8,128)(2,1)S(1)}, u32[]{:S(2)}, u32[]{:S(2)}) collective-permute-start(bf16[4,256,512]{2,1,0:T(8,128)(2,1)S(1)} %pad_maximum_fusion.refs_0_), channel_id=1, source_target_pairs={{0,1},{1,0},{2,3},{3,2},{4,5},{5,4},{6,7},{7,6},{8,9},{9,8},{10,11... | collective-permute-start | bytes 3145736 | tf_op jit(solution)/shard_map/ppermute | solution.py:48
  94.7 12.3 %collective-permute-start.33 = (bf16[4,256,512]{2,1,0:T(8,128)(2,1)S(1)}, bf16[4,256,512]{2,1,0:T(8,128)(2,1)S(1)}, u32[]{:S(2)}, u32[]{:S(2)}) collective-permute-start(bf16[4,256,512]{2,1,0:T(8,128)(2,1)S(1)} %copy-done.8), channel_id=1, source_target_pairs={{0,1},{1,0},{2,3},{3,2},{4,5},{5,4},{6,7},{7,6},{8,9},{9,8},{10,11... | collective-permute-start | bytes 3145736 | tf_op jit(solution)/shard_map/ppermute | solution.py:48
  95.2 29.0 %collective-permute-start.25 = (bf16[4,256,512]{2,1,0:T(8,128)(2,1)S(1)}, bf16[4,256,512]{2,1,0:T(8,128)(2,1)S(1)}, u32[]{:S(2)}, u32[]{:S(2)}) collective-permute-start(bf16[4,256,512]{2,1,0:T(8,128)(2,1)S(1)} %pad_maximum_fusion.refs_0_), channel_id=1, source_target_pairs={{0,64},{8,72},{16,80},{24,88},{32,96},{40,104},{48,112},{56,120},{... | collective-permute-start | bytes 3145736 | tf_op jit(solution)/shard_map/ppermute | solution.py:40
  96.7 10.4 %collective-permute-start.30 = (f32[64,128]{1,0:T(8,128)S(1)}, f32[64,128]{1,0:T(8,128)S(1)}, u32[]{:S(2)}, u32[]{:S(2)}) collective-permute-start(f32[64,128]{1,0:T(8,128)S(1)} %get-tuple-element.57.u0), channel_id=1, source_target_pairs={{0,6},{1,7},{2,0},{3,1},{4,2},{5,3},{6,4},{7,5},{8,14},{9,15},{10,... | collective-permute-start | bytes 98312 | tf_op jit(solution)/shard_map/ppermute | solution.py:36
  111.2 13.0 %collective-permute-start.37 = (f32[64,512]{1,0:T(8,128)S(1)}, f32[64,512]{1,0:T(8,128)S(1)}, u32[]{:S(2)}, u32[]{:S(2)}) collective-permute-start(f32[64,512]{1,0:T(8,128)S(1)} %shard_map.83), channel_id=1, source_target_pairs={{0,24},{8,0},{16,8},{24,16},{32,56},{40,32},{48,40},{56,48},{64,88... | collective-permute-start | bytes 393224 | tf_op jit(solution)/shard_map/ppermute | solution.py:44
  115.2 9.0 %collective-permute-start.36 = (f32[64,512]{1,0:T(8,128)S(1)}, f32[64,512]{1,0:T(8,128)S(1)}, u32[]{:S(2)}, u32[]{:S(2)}) collective-permute-start(f32[64,512]{1,0:T(8,128)S(1)} %shard_map.83), channel_id=1, source_target_pairs={{0,8},{8,16},{16,24},{24,0},{32,40},{40,48},{48,56},{56,32},{64,72... | collective-permute-start | bytes 393224 | tf_op jit(solution)/shard_map/ppermute | solution.py:44
  115.2 9.1 %collective-permute-start.35 = (f32[64,512]{1,0:T(8,128)S(1)}, f32[64,512]{1,0:T(8,128)S(1)}, u32[]{:S(2)}, u32[]{:S(2)}) collective-permute-start(f32[64,512]{1,0:T(8,128)S(1)} %shard_map.83), channel_id=1, source_target_pairs={{0,16},{8,24},{16,0},{24,8},{32,48},{40,56},{48,32},{56,40},{64,80... | collective-permute-start | bytes 393224 | tf_op jit(solution)/shard_map/ppermute | solution.py:44
  125.4 10.9 %collective-permute-start.44 = (f32[64,512]{1,0:T(8,128)S(1)}, f32[64,512]{1,0:T(8,128)S(1)}, u32[]{:S(2)}, u32[]{:S(2)}) collective-permute-start(f32[64,512]{1,0:T(8,128)S(1)} %add_add_fusion.1), channel_id=1, source_target_pairs={{0,96},{8,104},{16,112},{24,120},{32,0},{40,8},{48,16},{56,24},{64... | collective-permute-start | bytes 393224 | tf_op jit(solution)/shard_map/ppermute | solution.py:40
  126.6 10.9 %collective-permute-start.43 = (f32[64,512]{1,0:T(8,128)S(1)}, f32[64,512]{1,0:T(8,128)S(1)}, u32[]{:S(2)}, u32[]{:S(2)}) collective-permute-start(f32[64,512]{1,0:T(8,128)S(1)} %add_add_fusion.1), channel_id=1, source_target_pairs={{0,32},{8,40},{16,48},{24,56},{32,64},{40,72},{48,80},{56,88},{64,... | collective-permute-start | bytes 393224 | tf_op jit(solution)/shard_map/ppermute | solution.py:40
  126.9 10.6 %collective-permute-start.42 = (f32[64,512]{1,0:T(8,128)S(1)}, f32[64,512]{1,0:T(8,128)S(1)}, u32[]{:S(2)}, u32[]{:S(2)}) collective-permute-start(f32[64,512]{1,0:T(8,128)S(1)} %add_add_fusion.1), channel_id=1, source_target_pairs={{0,64},{8,72},{16,80},{24,88},{32,96},{40,104},{48,112},{56,120},{... | collective-permute-start | bytes 393224 | tf_op jit(solution)/shard_map/ppermute | solution.py:40
  133.5 15.7 %collective-permute-start.41 = (bf16[128,1024]{1,0:T(8,128)(2,1)S(1)}, bf16[128,1024]{1,0:T(8,128)(2,1)S(1)}, u32[]{:S(2)}, u32[]{:S(2)}) collective-permute-start(bf16[128,1024]{1,0:T(8,128)(2,1)S(1)} %get-tuple-element.68), channel_id=1, source_target_pairs={{0,8},{8,16},{16,24},{24,0},{32,40},{40,48},{48,56},{56,32},{64,72... | collective-permute-start | bytes 786440 | tf_op jit(solution)/shard_map/ppermute | solution.py:44
  135.6 13.6 %collective-permute-start.39 = (bf16[128,1024]{1,0:T(8,128)(2,1)S(1)}, bf16[128,1024]{1,0:T(8,128)(2,1)S(1)}, u32[]{:S(2)}, u32[]{:S(2)}) collective-permute-start(bf16[128,1024]{1,0:T(8,128)(2,1)S(1)} %get-tuple-element.66), channel_id=1, source_target_pairs={{0,24},{8,0},{16,8},{24,16},{32,56},{40,32},{48,40},{56,48},{64,88... | collective-permute-start | bytes 786440 | tf_op jit(solution)/shard_map/ppermute | solution.py:44
  136.3 12.9 %collective-permute-start.40 = (bf16[128,1024]{1,0:T(8,128)(2,1)S(1)}, bf16[128,1024]{1,0:T(8,128)(2,1)S(1)}, u32[]{:S(2)}, u32[]{:S(2)}) collective-permute-start(bf16[128,1024]{1,0:T(8,128)(2,1)S(1)} %get-tuple-element.67), channel_id=1, source_target_pairs={{0,16},{8,24},{16,0},{24,8},{32,48},{40,56},{48,32},{56,40},{64,80... | collective-permute-start | bytes 786440 | tf_op jit(solution)/shard_map/ppermute | solution.py:44
  (32 other events, 282.5 us)
Sparse Core Ops, SparseCore 0:
  9.7 51.6 all-gather.5
  76.4 52.3 all-gather.3

commit v5 on v4

--- a/solution.py
+++ b/solution.py
@@ -242,11 +242,11 @@
 
 
 def right_body(p_raw, error, out, held, arrived):
-    blocks = Fetch(error, held, arrived, 3)
-    for i in range(4):
-        high, low = halves(p_raw[:, columns(i)])
+    blocks = Fetch(error, held, arrived, 2, ENDS_SMALL)
+    for i, at in enumerate(ENDS_SMALL):
+        high, low = halves(p_raw[:, at])
         blocks.wait(i)
-        e_high, e_low = halves(held[:, columns(i)])
+        e_high, e_low = halves(held[:, at])
         parts = mm(e_high, jnp.concatenate([high, low], 0), NT)
         part = parts[:, :64] + parts[:, 64:] + mm(e_low, high, NT)
         if i == 0:
@@ -261,7 +261,7 @@
         shaped((512, 64)),
         in_specs=[VMEM, HBM],
         out_specs=VMEM,
-        scratch_shapes=[pltpu.VMEM((512, 4096), F32), pltpu.SemaphoreType.DMA((4,))],
+        scratch_shapes=[pltpu.VMEM((512, 4096), F32), pltpu.SemaphoreType.DMA((5,))],
     )(p_raw, in_hbm(error))
 
 
@@ -297,9 +297,17 @@
     same = lax.broadcasted_iota(jnp.int32, (64, 64), 0) == lax.broadcasted_iota(jnp.int32, (64, 64), 1)
     row = lax.broadcasted_iota(jnp.int32, (64, 128), 0)
     both = jnp.concatenate([gram, jnp.where(same, 1.0, 0.0).astype(F32)], 1)
-    for k in range(64):
-        scale = both[:, k : k + 1] / both[k : k + 1, k : k + 1]
-        both = both - jnp.where(row > k, scale * both[k : k + 1, :], 0.0)
+    for k in range(0, 64, 2):
+        first, second = both[k : k + 1, :], both[k + 1 : k + 2, :]
+        column, next_column = both[:, k : k + 1], both[:, k + 1 : k + 2]
+        scale = 1.0 / first[:, k : k + 1]
+        ratio = second[:, k : k + 1] * scale
+        second = second - ratio * first
+        next_column = next_column - ratio * column
+        next_scale = 1.0 / second[:, k + 1 : k + 2]
+        both = both - (
+            jnp.where(row > k, (column * scale) * first, 0.0) + jnp.where(row > k + 1, (next_column * next_scale) * second, 0.0)
+        )
     diagonal = jnp.sum(jnp.where(same, both[:, :64], 0.0), 1, keepdims=True)
     solved = both[:, 64:] / jnp.sqrt(diagonal)
     inverse[...] = solved
@@ -426,16 +434,16 @@
     ctx_all = lax.all_gather(after(ctx, rows, tokens), "fsdp", axis=0, tiled=True)
     p_near = [rows] + [along_y(rows, -d) for d in (1, 2, 3)]
     chunk2 = along_x(after(sends[2], rows), 2)
-    their1 = other_core(after(w1, rows))
-    p_far = other_core(jnp.concatenate([rows, after(p_near[1], their1, chunk2), *p_near[2:]], 0))
+    their1, their3 = [other_core(after(v, rows)) for v in (w1, w3)]
+    p_far = other_core(jnp.concatenate([rows, after(p_near[1], their1, their3, chunk2), *p_near[2:]], 0))
     w2 = along_y(after(w0, *p_near), 2)
 
     turned = turn(place, [sends[0], chunk1, chunk2, chunk3])
     p_raw, u = middle(place, p_near, after(p_far, turned), ctx)
     u_near = [u] + [along_x(u, -d) for d in (1, 2, 3)]
     w_term = right(p_raw, error)
-    their0, their3 = other_core(after(w0, u)), other_core(after(w3, u))
-    u_far = other_core(jnp.concatenate([u, u_near[1], u_near[2], after(u_near[3], w_term, their0, their3)], 0))
+    their0 = other_core(after(w0, u))
+    u_far = other_core(jnp.concatenate([u, u_near[1], u_near[2], after(u_near[3], w_term, their0)], 0))
     w = collect(place, w_term, turned, u_near, u_far)
     w = [w] + [along_z(w, d) for d in (1, 2, 3)]
     inverse, p = solve(p_raw)

time: 158 us -> 159 us (level)
    ppermute x9, starting transfers between devices: 10 us -> 12.7 us  [other_core(): return lax.ppermute(value, 'fsdp', [(i, i ^ 1) for i in range(8)])]
    ppermute x15, waiting for transfers between devices: 15.8 us -> 13.5 us  [along_x(): lax.ppermute(value, 'fsdp', [(i, (i // 2 + d) % 4 * 2 + i % 2) for i in r...]
where the time goes in v5:
time: 159 us; the launch traced here: 158 us
  starting transfers between devices  59 us (37%)
  Pallas kernels  44.7 us (28%)
  waiting for transfers between devices  35.3 us (22%)
  between operations  14.4 us (9%)
  local copies, waits for them, and re-layouts  4.57 us (3%)
    ppermute x15, starting transfers between devices, along_x(): lax.ppermute(value, 'fsdp', [(i, (i // 2 + d) % 4 * 2 + i % 2) for i in r...  17.9 us
    ppermute x9, starting transfers between devices, along_z(): lax.ppermute(value, 'dp', [(i, i // 4 * 4 + (i % 4 + d) % 4) for i in ran...  17.1 us
    ppermute x12, waiting for transfers between devices, along_y(): lax.ppermute(value, 'dp', [(i, (i // 4 + d) % 4 * 4 + i % 4) for i in ran...  15.8 us
    ppermute x15, waiting for transfers between devices, along_x(): lax.ppermute(value, 'fsdp', [(i, (i // 2 + d) % 4 * 2 + i % 2) for i in r...  13.5 us
    ppermute x9, starting transfers between devices, other_core(): return lax.ppermute(value, 'fsdp', [(i, i ^ 1) for i in range(8)])  12.7 us
    pallas_call x1, Pallas kernels, last(): pallas(last_body, [shaped((64, 512)), shaped((512, 4096))], mib=24, in_sp...  11.6 us
    ppermute x12, starting transfers between devices, along_y(): lax.ppermute(value, 'dp', [(i, (i // 4 + d) % 4 * 4 + i % 4) for i in ran...  11.2 us
    pallas_call x1, Pallas kernels, solve(): pallas(solve_body, [shaped((64, 64)), pltpu.HBM((192, 4096), BF16)], in_s...  7.78 us
  transfers between devices with their start and end apart: 47, of which 18 were waited for; matrix products, arithmetic and copies ran while one was open for 2% of the time, Pallas kernels for 27%

profile of v5, /device:TPU:1, one launch (start us, length us, event | category | flops | bytes accessed | tf_op | source)
XLA Modules:
  0.0 158.5 jit_solution(2449680751691055592)
XLA Ops:
  8.9 3.4 %collective-permute-start.3 = (bf16[256,512]{1,0:T(8,128)(2,1)S(1)}, bf16[256,512]{1,0:T(8,128)(2,1)S(1)}, u32[]{:S(2)}, u32[]{:S(2)}) collective-permute-start(bf16[256,512]{1,0:T(8,128)(2,1)S(1)} %constant_dynamic-slice_fusion), channel_id=1, source_target_pairs={{0,6},{1,7},{2,0},{3,1},{4,2},{5,3},{6,4},{7,5},{8,14},{9,15},{10,... | collective-permute-start | bytes 786440 | tf_op jit(solution)/shard_map/ppermute | solution.py:36
  12.3 2.7 %collective-permute-start.1 = (f32[64,512]{1,0:T(8,128)}, f32[64,512]{1,0:T(8,128)S(1)}, u32[]{:S(2)}, u32[]{:S(2)}) collective-permute-start(f32[64,512]{1,0:T(8,128)} %bitcast.15), channel_id=1, source_target_pairs={{0,6},{1,7},{2,0},{3,1},{4,2},{5,3},{6,4},{7,5},{8,14},{9,15},{10,... | collective-permute-start | bytes 393224 | tf_op jit(solution)/shard_map/ppermute | solution.py:36
  16.6 4.6 %shard_map.76.term = f32[64,4096]{1,0:T(8,128)S(1)} custom-call(s32[4]{0:T(128)S(1)} %pad_add_fusion.place, f32[64,512]{1,0:T(8,128)S(1)} %bitcast.18, f32[512,4096]{1,0:T(8,128)} %bitcast.21), custom_call_target="tpu_custom_call" | custom-call | tf_op jit(solution)/shard_map/pallas_call | solution.py:142
  22.0 4.0 %collective-permute-done.5.q3 = f32[64,512]{1,0:T(8,128)S(1)} collective-permute-done((f32[64,512]{1,0:T(8,128)}, f32[64,512]{1,0:T(8,128)S(1)}, u32[]{:S(2)}, u32[]{:S(2)}) %collective-permute-start.5) | collective-permute-done | bytes 131104 | tf_op jit(solution)/shard_map/ppermute | solution.py:36
  26.0 1.9 %collective-permute-start.6 = (f32[256,512]{1,0:T(8,128)S(1)}, f32[256,512]{1,0:T(8,128)S(1)}, u32[]{:S(2)}, u32[]{:S(2)}) collective-permute-start(f32[256,512]{1,0:T(8,128)S(1)} %pad_maximum_fusion.1), channel_id=1, source_target_pairs={{0,1},{1,0},{2,3},{3,2},{4,5},{5,4},{6,7},{7,6},{8,9},{9,8},{10,11... | collective-permute-start | bytes 1572872 | tf_op jit(solution)/shard_map/ppermute | solution.py:48
  29.5 2.4 %shard_map.77 = (f32[32,4096]{1,0:T(8,128)S(1)}, f32[32,4096]{1,0:T(8,128)S(1)}) custom-call(s32[4]{0:T(128)S(1)} %pad_add_fusion.place, f32[64,512]{1,0:T(8,128)S(1)} %bitcast.20, f32[64,512]{1,0:T(8,128)S(1)} %collective-permute-done.1.q1, f32[64,512]{1,0:T(8,128)S(1)} %collective-permute-done.4.q2, f32[64,512]{1,0:T(8,128)S(1)} %collective-permute-done.5.q3, ...), custom_call_target="tpu_custom_call" | custom-call | tf_op jit(solution)/shard_map/pallas_call | solution.py:172
  34.1 2.8 %collective-permute-start.10 = (f32[8,4096]{1,0:T(8,128)S(1)}, f32[8,4096]{1,0:T(8,128)S(1)}, u32[]{:S(2)}, u32[]{:S(2)}) collective-permute-start(f32[8,4096]{1,0:T(8,128)S(1)} %get-tuple-element.75), channel_id=1, source_target_pairs={{0,96},{8,104},{16,112},{24,120},{32,0},{40,8},{48,16},{56,24},{64... | collective-permute-start | bytes 393224 | tf_op jit(solution)/shard_map/ppermute | solution.py:40
  38.9 3.5 %collective-permute-done.2 = bf16[256,512]{1,0:T(8,128)(2,1)S(1)} collective-permute-done((bf16[256,512]{1,0:T(8,128)(2,1)S(1)}, bf16[256,512]{1,0:T(8,128)(2,1)S(1)}, u32[]{:S(2)}, u32[]{:S(2)}) %collective-permute-start.2) | collective-permute-done | bytes 262176 | tf_op jit(solution)/shard_map/ppermute | solution.py:36
  42.8 3.9 %collective-permute-done.9 = f32[8,4096]{1,0:T(8,128)S(1)} collective-permute-done((f32[8,4096]{1,0:T(8,128)S(1)}, f32[8,4096]{1,0:T(8,128)S(1)}, u32[]{:S(2)}, u32[]{:S(2)}) %collective-permute-start.9) | collective-permute-done | bytes 131104 | tf_op jit(solution)/shard_map/ppermute | solution.py:40
  47.0 2.5 %collective-permute-start.15 = (f32[8,4096]{1,0:T(8,128)S(1)}, f32[8,4096]{1,0:T(8,128)S(1)}, u32[]{:S(2)}, u32[]{:S(2)}) collective-permute-start(f32[8,4096]{1,0:T(8,128)S(1)} %fusion), channel_id=1, source_target_pairs={{0,6},{1,7},{2,0},{3,1},{4,2},{5,3},{6,4},{7,5},{8,14},{9,15},{10,... | collective-permute-start | bytes 393224 | tf_op jit(solution)/shard_map/ppermute | solution.py:36
  52.8 2.0 %collective-permute-done.13 = f32[8,4096]{1,0:T(8,128)S(1)} collective-permute-done((f32[8,4096]{1,0:T(8,128)S(1)}, f32[8,4096]{1,0:T(8,128)S(1)}, u32[]{:S(2)}, u32[]{:S(2)}) %collective-permute-start.13) | collective-permute-done | bytes 131104 | tf_op jit(solution)/shard_map/ppermute | solution.py:36
  56.2 1.6 %collective-permute-start.20 = (bf16[2,128,512]{2,1,0:T(8,128)(2,1)S(1)}, bf16[2,128,512]{2,1,0:T(8,128)(2,1)S(1)}, u32[]{:S(2)}, u32[]{:S(2)}) collective-permute-start(bf16[2,128,512]{2,1,0:T(8,128)(2,1)S(1)} %get-tuple-element.47), channel_id=1, source_target_pairs={{0,2},{1,3},{2,4},{3,5},{4,6},{5,7},{6,0},{7,1},{8,10},{9,11},{10,... | collective-permute-start | bytes 786440 | tf_op jit(solution)/shard_map/ppermute | solution.py:36
  58.9 3.8 %collective-permute-start.18 = (f32[8,4096]{1,0:T(8,128)S(1)}, f32[8,4096]{1,0:T(8,128)S(1)}, u32[]{:S(2)}, u32[]{:S(2)}) collective-permute-start(f32[8,4096]{1,0:T(8,128)S(1)} %add_add_fusion.3), channel_id=1, source_target_pairs={{0,24},{8,0},{16,8},{24,16},{32,56},{40,32},{48,40},{56,48},{64,88... | collective-permute-start | bytes 393224 | tf_op jit(solution)/shard_map/ppermute | solution.py:44
  62.6 1.9 %collective-permute-done.18 = f32[8,4096]{1,0:T(8,128)S(1)} collective-permute-done((f32[8,4096]{1,0:T(8,128)S(1)}, f32[8,4096]{1,0:T(8,128)S(1)}, u32[]{:S(2)}, u32[]{:S(2)}) %collective-permute-start.18) | collective-permute-done | bytes 131104 | tf_op jit(solution)/shard_map/ppermute | solution.py:44
  64.7 4.5 %collective-permute-start.16 = (f32[8,4096]{1,0:T(8,128)S(1)}, f32[8,4096]{1,0:T(8,128)S(1)}, u32[]{:S(2)}, u32[]{:S(2)}) collective-permute-start(f32[8,4096]{1,0:T(8,128)S(1)} %add_add_fusion.3), channel_id=1, source_target_pairs={{0,16},{8,24},{16,0},{24,8},{32,48},{40,56},{48,32},{56,40},{64,80... | collective-permute-start | bytes 393224 | tf_op jit(solution)/shard_map/ppermute | solution.py:44
  69.2 5.3 %collective-permute-done.12.refs_1_ = bf16[4,256,512]{2,1,0:T(8,128)(2,1)S(1)} collective-permute-done((bf16[4,256,512]{2,1,0:T(8,128)(2,1)S(1)}, bf16[4,256,512]{2,1,0:T(8,128)(2,1)S(1)}, u32[]{:S(2)}, u32[]{:S(2)}) %collective-permute-start.12) | collective-permute-done | bytes 1048608 | tf_op jit(solution)/shard_map/ppermute | solution.py:40
  76.3 2.8 %collective-permute-start.26 = (bf16[4,256,512]{2,1,0:T(8,128)(2,1)S(1)}, bf16[4,256,512]{2,1,0:T(8,128)(2,1)S(1)}, u32[]{:S(2)}, u32[]{:S(2)}) collective-permute-start(bf16[4,256,512]{2,1,0:T(8,128)(2,1)S(1)} %collective-permute-done.12.refs_1_), channel_id=1, source_target_pairs={{0,1},{1,0},{2,3},{3,2},{4,5},{5,4},{6,7},{7,6},{8,9},{9,8},{10,11... | collective-permute-start | bytes 3145736 | tf_op jit(solution)/shard_map/ppermute | solution.py:48
  80.8 2.0 %collective-permute-start.23 = (f32[8,4096]{1,0:T(8,128)S(1)}, f32[8,4096]{1,0:T(8,128)S(1)}, u32[]{:S(2)}, u32[]{:S(2)}) collective-permute-start(f32[8,4096]{1,0:T(8,128)S(1)} %add_add_fusion.2.p0), channel_id=1, source_target_pairs={{0,64},{8,72},{16,80},{24,88},{32,96},{40,104},{48,112},{56,120},{... | collective-permute-start | bytes 393224 | tf_op jit(solution)/shard_map/ppermute | solution.py:40
  82.7 2.4 %collective-permute-done.22.p1 = f32[8,4096]{1,0:T(8,128)S(1)} collective-permute-done((f32[8,4096]{1,0:T(8,128)S(1)}, f32[8,4096]{1,0:T(8,128)S(1)}, u32[]{:S(2)}, u32[]{:S(2)}) %collective-permute-start.22) | collective-permute-done | bytes 131104 | tf_op jit(solution)/shard_map/ppermute | solution.py:40
  85.3 2.8 %collective-permute-done.28.c2 = bf16[2,128,512]{2,1,0:T(8,128)(2,1)S(1)} collective-permute-done((bf16[2,128,512]{2,1,0:T(8,128)(2,1)S(1)}, bf16[2,128,512]{2,1,0:T(8,128)(2,1)S(1)}, u32[]{:S(2)}, u32[]{:S(2)}) %collective-permute-start.28) | collective-permute-done | bytes 262176 | tf_op jit(solution)/shard_map/ppermute | solution.py:36
  88.1 2.0 %collective-permute-done.24.p3 = f32[8,4096]{1,0:T(8,128)S(1)} collective-permute-done((f32[8,4096]{1,0:T(8,128)S(1)}, f32[8,4096]{1,0:T(8,128)S(1)}, u32[]{:S(2)}, u32[]{:S(2)}) %collective-permute-start.24) | collective-permute-done | bytes 131104 | tf_op jit(solution)/shard_map/ppermute | solution.py:40
  90.2 4.0 %collective-permute-start.29 = (f32[32,4096]{1,0:T(8,128)S(1)}, f32[32,4096]{1,0:T(8,128)S(1)}, u32[]{:S(2)}, u32[]{:S(2)}) collective-permute-start(f32[32,4096]{1,0:T(8,128)S(1)} %pad_maximum_fusion.2), channel_id=1, source_target_pairs={{0,1},{1,0},{2,3},{3,2},{4,5},{5,4},{6,7},{7,6},{8,9},{9,8},{10,11... | collective-permute-start | bytes 1572872 | tf_op jit(solution)/shard_map/ppermute | solution.py:48
  94.2 2.1 %shard_map.80.turned = bf16[512,1024]{1,0:T(8,128)(2,1)S(1)} custom-call(s32[4]{0:T(128)S(1)} %pad_add_fusion.place, bf16[2,128,512]{2,1,0:T(8,128)(2,1)} %copy-done.9, bf16[2,128,512]{2,1,0:T(8,128)(2,1)} %copy-done.10, bf16[2,128,512]{2,1,0:T(8,128)(2,1)} %copy-done.12, bf16[2,128,512]{2,1,0:T(8,128)(2,1)} %copy-done.11), custom_call_target="tpu_custom_call" | custom-call | tf_op jit(solution)/shard_map/pallas_call | solution.py:214
  97.8 2.7 %collective-permute-start.31 = (f32[64,128]{1,0:T(8,128)S(1)}, f32[64,128]{1,0:T(8,128)S(1)}, u32[]{:S(2)}, u32[]{:S(2)}) collective-permute-start(f32[64,128]{1,0:T(8,128)S(1)} %get-tuple-element.58.u0), channel_id=1, source_target_pairs={{0,6},{1,7},{2,0},{3,1},{4,2},{5,3},{6,4},{7,5},{8,14},{9,15},{10,... | collective-permute-start | bytes 98312 | tf_op jit(solution)/shard_map/ppermute | solution.py:36
  100.5 5.1 %shard_map.82.term = f32[512,64]{1,0:T(8,128)S(1)} custom-call(f32[64,4096]{1,0:T(8,128)S(1)} %get-tuple-element.60.p_raw, f32[512,4096]{1,0:T(8,128)} %bitcast.22), custom_call_target="tpu_custom_call" | custom-call | tf_op jit(solution)/shard_map/pallas_call | solution.py:259
  105.7 1.8 %collective-permute-start.34 = (f32[256,128]{1,0:T(8,128)S(1)}, f32[256,128]{1,0:T(8,128)S(1)}, u32[]{:S(2)}, u32[]{:S(2)}) collective-permute-start(f32[256,128]{1,0:T(8,128)S(1)} %pad_maximum_fusion.3), channel_id=1, source_target_pairs={{0,1},{1,0},{2,3},{3,2},{4,5},{5,4},{6,7},{7,6},{8,9},{9,8},{10,11... | collective-permute-start | bytes 393224 | tf_op jit(solution)/shard_map/ppermute | solution.py:48
  109.7 3.7 %collective-permute-start.37 = (f32[64,512]{1,0:T(8,128)S(1)}, f32[64,512]{1,0:T(8,128)S(1)}, u32[]{:S(2)}, u32[]{:S(2)}) collective-permute-start(f32[64,512]{1,0:T(8,128)S(1)} %shard_map.83), channel_id=1, source_target_pairs={{0,24},{8,0},{16,8},{24,16},{32,56},{40,32},{48,40},{56,48},{64,88... | collective-permute-start | bytes 393224 | tf_op jit(solution)/shard_map/ppermute | solution.py:44
  114.7 7.8 %shard_map.84 = (f32[64,64]{1,0:T(8,128)S(1)}, bf16[192,4096]{1,0:T(8,128)(2,1)}) custom-call(f32[64,4096]{1,0:T(8,128)S(1)} %get-tuple-element.60.p_raw), custom_call_target="tpu_custom_call" | custom-call | tf_op jit(solution)/shard_map/pallas_call | solution.py:328
  126.4 2.1 %collective-permute-start.42 = (f32[64,512]{1,0:T(8,128)S(1)}, f32[64,512]{1,0:T(8,128)S(1)}, u32[]{:S(2)}, u32[]{:S(2)}) collective-permute-start(f32[64,512]{1,0:T(8,128)S(1)} %add_add_fusion.1), channel_id=1, source_target_pairs={{0,64},{8,72},{16,80},{24,88},{32,96},{40,104},{48,112},{56,120},{... | collective-permute-start | bytes 393224 | tf_op jit(solution)/shard_map/ppermute | solution.py:40
  128.5 6.0 %shard_map.85 = (bf16[128,1024]{1,0:T(8,128)(2,1)S(1)}, bf16[128,1024]{1,0:T(8,128)(2,1)}, bf16[128,1024]{1,0:T(8,128)(2,1)}, bf16[128,1024]{1,0:T(8,128)(2,1)}) custom-call(s32[4]{0:T(128)S(1)} %pad_add_fusion.place, bf16[4,128,4096]{2,1,0:T(8,128)(2,1)S(1)} %bitcast.14, bf16[4,256,512]{2,1,0:T(8,128)(2,1)S(1)} %pad_maximum_fusion.refs_0_, ...), custom_call_target="tpu_custom_call" | custom-call | tf_op jit(solution)/shard_map/pallas_call | solution.py:390
  134.5 2.0 %collective-permute-start.41 = (bf16[128,1024]{1,0:T(8,128)(2,1)}, bf16[128,1024]{1,0:T(8,128)(2,1)S(1)}, u32[]{:S(2)}, u32[]{:S(2)}) collective-permute-start(bf16[128,1024]{1,0:T(8,128)(2,1)} %get-tuple-element.68), channel_id=1, source_target_pairs={{0,8},{8,16},{16,24},{24,0},{32,40},{40,48},{48,56},{56,32},{64,72... | collective-permute-start | bytes 786440 | tf_op jit(solution)/shard_map/ppermute | solution.py:44
  138.4 11.6 %shard_map.86 = (f32[64,512]{1,0:T(8,128)}, f32[512,4096]{1,0:T(8,128)}) custom-call(f32[64,64]{1,0:T(8,128)S(1)} %get-tuple-element.69.inverse, f32[64,512]{1,0:T(8,128)S(1)} %add_add_fusion.w, bf16[512,1024]{1,0:T(8,128)(2,1)S(1)} %shard_map.80.turned, bf16[192,4096]{1,0:T(8,128)(2,1)} %get-tuple-element.62.p_far, f32[512,4096]{1,0:T(8,128)} %bitcast.23, ...), custom_call_target="tpu_custom_call" | custom-call | tf_op jit(solution)/shard_map/pallas_call | solution.py:363
  (116 shorter events, 32.2 us)
Async XLA Ops:
  7.2 69.1 %all-gather.6.cloned.1.call-start = ((), (), s32[]{:S(2)}) async-start(), calls=%async_computation.1 | async-start | bytes 5242880 | tf_op jit(solution)/shard_map/all_gather | solution.py:411
  7.9 130.5 %all-gather.4.cloned.1.call-start = ((), (), s32[]{:S(2)}) async-start(), calls=%async_computation | async-start | bytes 9437184 | tf_op jit(solution)/shard_map/all_gather | solution.py:434
  8.9 12.5 %collective-permute-start.3 = (bf16[256,512]{1,0:T(8,128)(2,1)S(1)}, bf16[256,512]{1,0:T(8,128)(2,1)S(1)}, u32[]{:S(2)}, u32[]{:S(2)}) collective-permute-start(bf16[256,512]{1,0:T(8,128)(2,1)S(1)} %constant_dynamic-slice_fusion), channel_id=1, source_target_pairs={{0,6},{1,7},{2,0},{3,1},{4,2},{5,3},{6,4},{7,5},{8,14},{9,15},{10,... | collective-permute-start | bytes 786440 | tf_op jit(solution)/shard_map/ppermute | solution.py:36
  12.3 9.1 %collective-permute-start = (bf16[256,512]{1,0:T(8,128)(2,1)S(1)}, bf16[256,512]{1,0:T(8,128)(2,1)S(1)}, u32[]{:S(2)}, u32[]{:S(2)}) collective-permute-start(bf16[256,512]{1,0:T(8,128)(2,1)S(1)} %constant_dynamic-slice_fusion), channel_id=1, source_target_pairs={{0,2},{1,3},{2,4},{3,5},{4,6},{5,7},{6,0},{7,1},{8,10},{9,11},{10,... | collective-permute-start | bytes 786440 | tf_op jit(solution)/shard_map/ppermute | solution.py:36
  12.3 9.1 %collective-permute-start.1 = (f32[64,512]{1,0:T(8,128)}, f32[64,512]{1,0:T(8,128)S(1)}, u32[]{:S(2)}, u32[]{:S(2)}) collective-permute-start(f32[64,512]{1,0:T(8,128)} %bitcast.15), channel_id=1, source_target_pairs={{0,6},{1,7},{2,0},{3,1},{4,2},{5,3},{6,4},{7,5},{8,14},{9,15},{10,... | collective-permute-start | bytes 393224 | tf_op jit(solution)/shard_map/ppermute | solution.py:36
  15.0 11.0 %collective-permute-start.5 = (f32[64,512]{1,0:T(8,128)}, f32[64,512]{1,0:T(8,128)S(1)}, u32[]{:S(2)}, u32[]{:S(2)}) collective-permute-start(f32[64,512]{1,0:T(8,128)} %bitcast.17), channel_id=1, source_target_pairs={{0,2},{1,3},{2,4},{3,5},{4,6},{5,7},{6,0},{7,1},{8,10},{9,11},{10,... | collective-permute-start | bytes 393224 | tf_op jit(solution)/shard_map/ppermute | solution.py:36
  33.0 9.4 %collective-permute-start.2 = (bf16[256,512]{1,0:T(8,128)(2,1)S(1)}, bf16[256,512]{1,0:T(8,128)(2,1)S(1)}, u32[]{:S(2)}, u32[]{:S(2)}) collective-permute-start(bf16[256,512]{1,0:T(8,128)(2,1)S(1)} %constant_dynamic-slice_fusion), channel_id=1, source_target_pairs={{0,4},{1,5},{2,6},{3,7},{4,0},{5,1},{6,2},{7,3},{8,12},{9,13},{10,... | collective-permute-start | bytes 786440 | tf_op jit(solution)/shard_map/ppermute | solution.py:36
  33.1 9.3 %collective-permute-start.11 = (bf16[4,128,512]{2,1,0:T(8,128)(2,1)S(1)}, bf16[4,128,512]{2,1,0:T(8,128)(2,1)S(1)}, u32[]{:S(2)}, u32[]{:S(2)}) collective-permute-start(bf16[4,128,512]{2,1,0:T(8,128)(2,1)S(1)} %shard_map.78), channel_id=1, source_target_pairs={{0,1},{1,0},{2,3},{3,2},{4,5},{5,4},{6,7},{7,6},{8,9},{9,8},{10,11... | collective-permute-start | bytes 1572872 | tf_op jit(solution)/shard_map/ppermute | solution.py:48
  34.1 8.3 %collective-permute-start.10 = (f32[8,4096]{1,0:T(8,128)S(1)}, f32[8,4096]{1,0:T(8,128)S(1)}, u32[]{:S(2)}, u32[]{:S(2)}) collective-permute-start(f32[8,4096]{1,0:T(8,128)S(1)} %get-tuple-element.75), channel_id=1, source_target_pairs={{0,96},{8,104},{16,112},{24,120},{32,0},{40,8},{48,16},{56,24},{64... | collective-permute-start | bytes 393224 | tf_op jit(solution)/shard_map/ppermute | solution.py:40
  37.2 9.5 %collective-permute-start.9 = (f32[8,4096]{1,0:T(8,128)S(1)}, f32[8,4096]{1,0:T(8,128)S(1)}, u32[]{:S(2)}, u32[]{:S(2)}) collective-permute-start(f32[8,4096]{1,0:T(8,128)S(1)} %get-tuple-element.76), channel_id=1, source_target_pairs={{0,32},{8,40},{16,48},{24,56},{32,64},{40,72},{48,80},{56,88},{64,... | collective-permute-start | bytes 393224 | tf_op jit(solution)/shard_map/ppermute | solution.py:40
  51.0 23.5 %collective-permute-start.12 = (bf16[4,256,512]{2,1,0:T(8,128)(2,1)S(1)}, bf16[4,256,512]{2,1,0:T(8,128)(2,1)S(1)}, u32[]{:S(2)}, u32[]{:S(2)}) collective-permute-start(bf16[4,256,512]{2,1,0:T(8,128)(2,1)S(1)} %pad_maximum_fusion.refs_0_), channel_id=1, source_target_pairs={{0,96},{8,104},{16,112},{24,120},{32,0},{40,8},{48,16},{56,24},{64... | collective-permute-start | bytes 3145736 | tf_op jit(solution)/shard_map/ppermute | solution.py:40
  51.1 24.2 %collective-permute-start.19 = (bf16[4,256,512]{2,1,0:T(8,128)(2,1)S(1)}, bf16[4,256,512]{2,1,0:T(8,128)(2,1)S(1)}, u32[]{:S(2)}, u32[]{:S(2)}) collective-permute-start(bf16[4,256,512]{2,1,0:T(8,128)(2,1)S(1)} %pad_maximum_fusion.refs_0_), channel_id=1, source_target_pairs={{0,32},{8,40},{16,48},{24,56},{32,64},{40,72},{48,80},{56,88},{64,... | collective-permute-start | bytes 3145736 | tf_op jit(solution)/shard_map/ppermute | solution.py:40
  56.2 8.5 %collective-permute-start.20 = (bf16[2,128,512]{2,1,0:T(8,128)(2,1)S(1)}, bf16[2,128,512]{2,1,0:T(8,128)(2,1)S(1)}, u32[]{:S(2)}, u32[]{:S(2)}) collective-permute-start(bf16[2,128,512]{2,1,0:T(8,128)(2,1)S(1)} %get-tuple-element.47), channel_id=1, source_target_pairs={{0,2},{1,3},{2,4},{3,5},{4,6},{5,7},{6,0},{7,1},{8,10},{9,11},{10,... | collective-permute-start | bytes 786440 | tf_op jit(solution)/shard_map/ppermute | solution.py:36
  57.8 11.3 %collective-permute-start.21 = (bf16[2,128,512]{2,1,0:T(8,128)(2,1)S(1)}, bf16[2,128,512]{2,1,0:T(8,128)(2,1)S(1)}, u32[]{:S(2)}, u32[]{:S(2)}) collective-permute-start(bf16[2,128,512]{2,1,0:T(8,128)(2,1)S(1)} %get-tuple-element.48), channel_id=1, source_target_pairs={{0,6},{1,7},{2,0},{3,1},{4,2},{5,3},{6,4},{7,5},{8,14},{9,15},{10,... | collective-permute-start | bytes 786440 | tf_op jit(solution)/shard_map/ppermute | solution.py:36
  64.6 10.6 %collective-permute-start.17 = (f32[8,4096]{1,0:T(8,128)S(1)}, f32[8,4096]{1,0:T(8,128)S(1)}, u32[]{:S(2)}, u32[]{:S(2)}) collective-permute-start(f32[8,4096]{1,0:T(8,128)S(1)} %add_add_fusion.3), channel_id=1, source_target_pairs={{0,8},{8,16},{16,24},{24,0},{32,40},{40,48},{48,56},{56,32},{64,72... | collective-permute-start | bytes 393224 | tf_op jit(solution)/shard_map/ppermute | solution.py:44
  64.7 11.5 %collective-permute-start.16 = (f32[8,4096]{1,0:T(8,128)S(1)}, f32[8,4096]{1,0:T(8,128)S(1)}, u32[]{:S(2)}, u32[]{:S(2)}) collective-permute-start(f32[8,4096]{1,0:T(8,128)S(1)} %add_add_fusion.3), channel_id=1, source_target_pairs={{0,16},{8,24},{16,0},{24,8},{32,48},{40,56},{48,32},{56,40},{64,80... | collective-permute-start | bytes 393224 | tf_op jit(solution)/shard_map/ppermute | solution.py:44
  76.3 11.8 %collective-permute-start.26 = (bf16[4,256,512]{2,1,0:T(8,128)(2,1)S(1)}, bf16[4,256,512]{2,1,0:T(8,128)(2,1)S(1)}, u32[]{:S(2)}, u32[]{:S(2)}) collective-permute-start(bf16[4,256,512]{2,1,0:T(8,128)(2,1)S(1)} %collective-permute-done.12.refs_1_), channel_id=1, source_target_pairs={{0,1},{1,0},{2,3},{3,2},{4,5},{5,4},{6,7},{7,6},{8,9},{9,8},{10,11... | collective-permute-start | bytes 3145736 | tf_op jit(solution)/shard_map/ppermute | solution.py:48
  79.1 9.1 %collective-permute-start.27 = (bf16[4,256,512]{2,1,0:T(8,128)(2,1)}, bf16[4,256,512]{2,1,0:T(8,128)(2,1)S(1)}, u32[]{:S(2)}, u32[]{:S(2)}) collective-permute-start(bf16[4,256,512]{2,1,0:T(8,128)(2,1)} %copy-done.7), channel_id=1, source_target_pairs={{0,1},{1,0},{2,3},{3,2},{4,5},{5,4},{6,7},{7,6},{8,9},{9,8},{10,11... | collective-permute-start | bytes 3145736 | tf_op jit(solution)/shard_map/ppermute | solution.py:48
  79.1 9.0 %collective-permute-start.28 = (bf16[2,128,512]{2,1,0:T(8,128)(2,1)S(1)}, bf16[2,128,512]{2,1,0:T(8,128)(2,1)S(1)}, u32[]{:S(2)}, u32[]{:S(2)}) collective-permute-start(bf16[2,128,512]{2,1,0:T(8,128)(2,1)S(1)} %get-tuple-element.54), channel_id=1, source_target_pairs={{0,4},{1,5},{2,6},{3,7},{4,0},{5,1},{6,2},{7,3},{8,12},{9,13},{10,... | collective-permute-start | bytes 786440 | tf_op jit(solution)/shard_map/ppermute | solution.py:36
  97.5 8.1 %collective-permute-start.30 = (bf16[4,256,512]{2,1,0:T(8,128)(2,1)S(1)}, bf16[4,256,512]{2,1,0:T(8,128)(2,1)S(1)}, u32[]{:S(2)}, u32[]{:S(2)}) collective-permute-start(bf16[4,256,512]{2,1,0:T(8,128)(2,1)S(1)} %pad_maximum_fusion.refs_0_), channel_id=1, source_target_pairs={{0,1},{1,0},{2,3},{3,2},{4,5},{5,4},{6,7},{7,6},{8,9},{9,8},{10,11... | collective-permute-start | bytes 3145736 | tf_op jit(solution)/shard_map/ppermute | solution.py:48
  97.6 25.9 %collective-permute-start.25 = (bf16[4,256,512]{2,1,0:T(8,128)(2,1)S(1)}, bf16[4,256,512]{2,1,0:T(8,128)(2,1)S(1)}, u32[]{:S(2)}, u32[]{:S(2)}) collective-permute-start(bf16[4,256,512]{2,1,0:T(8,128)(2,1)S(1)} %pad_maximum_fusion.refs_0_), channel_id=1, source_target_pairs={{0,64},{8,72},{16,80},{24,88},{32,96},{40,104},{48,112},{56,120},{... | collective-permute-start | bytes 3145736 | tf_op jit(solution)/shard_map/ppermute | solution.py:40
  97.7 7.9 %collective-permute-start.33 = (f32[64,128]{1,0:T(8,128)S(1)}, f32[64,128]{1,0:T(8,128)S(1)}, u32[]{:S(2)}, u32[]{:S(2)}) collective-permute-start(f32[64,128]{1,0:T(8,128)S(1)} %get-tuple-element.58.u0), channel_id=1, source_target_pairs={{0,2},{1,3},{2,4},{3,5},{4,6},{5,7},{6,0},{7,1},{8,10},{9,11},{10,... | collective-permute-start | bytes 98312 | tf_op jit(solution)/shard_map/ppermute | solution.py:36
  97.8 7.9 %collective-permute-start.31 = (f32[64,128]{1,0:T(8,128)S(1)}, f32[64,128]{1,0:T(8,128)S(1)}, u32[]{:S(2)}, u32[]{:S(2)}) collective-permute-start(f32[64,128]{1,0:T(8,128)S(1)} %get-tuple-element.58.u0), channel_id=1, source_target_pairs={{0,6},{1,7},{2,0},{3,1},{4,2},{5,3},{6,4},{7,5},{8,14},{9,15},{10,... | collective-permute-start | bytes 98312 | tf_op jit(solution)/shard_map/ppermute | solution.py:36
  109.7 13.8 %collective-permute-start.37 = (f32[64,512]{1,0:T(8,128)S(1)}, f32[64,512]{1,0:T(8,128)S(1)}, u32[]{:S(2)}, u32[]{:S(2)}) collective-permute-start(f32[64,512]{1,0:T(8,128)S(1)} %shard_map.83), channel_id=1, source_target_pairs={{0,24},{8,0},{16,8},{24,16},{32,56},{40,32},{48,40},{56,48},{64,88... | collective-permute-start | bytes 393224 | tf_op jit(solution)/shard_map/ppermute | solution.py:44
  113.4 10.1 %collective-permute-start.36 = (f32[64,512]{1,0:T(8,128)S(1)}, f32[64,512]{1,0:T(8,128)S(1)}, u32[]{:S(2)}, u32[]{:S(2)}) collective-permute-start(f32[64,512]{1,0:T(8,128)S(1)} %shard_map.83), channel_id=1, source_target_pairs={{0,8},{8,16},{16,24},{24,0},{32,40},{40,48},{48,56},{56,32},{64,72... | collective-permute-start | bytes 393224 | tf_op jit(solution)/shard_map/ppermute | solution.py:44
  113.4 10.1 %collective-permute-start.35 = (f32[64,512]{1,0:T(8,128)S(1)}, f32[64,512]{1,0:T(8,128)S(1)}, u32[]{:S(2)}, u32[]{:S(2)}) collective-permute-start(f32[64,512]{1,0:T(8,128)S(1)} %shard_map.83), channel_id=1, source_target_pairs={{0,16},{8,24},{16,0},{24,8},{32,48},{40,56},{48,32},{56,40},{64,80... | collective-permute-start | bytes 393224 | tf_op jit(solution)/shard_map/ppermute | solution.py:44
  124.9 12.3 %collective-permute-start.44 = (f32[64,512]{1,0:T(8,128)S(1)}, f32[64,512]{1,0:T(8,128)S(1)}, u32[]{:S(2)}, u32[]{:S(2)}) collective-permute-start(f32[64,512]{1,0:T(8,128)S(1)} %add_add_fusion.1), channel_id=1, source_target_pairs={{0,96},{8,104},{16,112},{24,120},{32,0},{40,8},{48,16},{56,24},{64... | collective-permute-start | bytes 393224 | tf_op jit(solution)/shard_map/ppermute | solution.py:40
  125.0 13.4 %collective-permute-start.43 = (f32[64,512]{1,0:T(8,128)S(1)}, f32[64,512]{1,0:T(8,128)S(1)}, u32[]{:S(2)}, u32[]{:S(2)}) collective-permute-start(f32[64,512]{1,0:T(8,128)S(1)} %add_add_fusion.1), channel_id=1, source_target_pairs={{0,32},{8,40},{16,48},{24,56},{32,64},{40,72},{48,80},{56,88},{64,... | collective-permute-start | bytes 393224 | tf_op jit(solution)/shard_map/ppermute | solution.py:40
  126.4 12.0 %collective-permute-start.42 = (f32[64,512]{1,0:T(8,128)S(1)}, f32[64,512]{1,0:T(8,128)S(1)}, u32[]{:S(2)}, u32[]{:S(2)}) collective-permute-start(f32[64,512]{1,0:T(8,128)S(1)} %add_add_fusion.1), channel_id=1, source_target_pairs={{0,64},{8,72},{16,80},{24,88},{32,96},{40,104},{48,112},{56,120},{... | collective-permute-start | bytes 393224 | tf_op jit(solution)/shard_map/ppermute | solution.py:40
  134.5 15.5 %collective-permute-start.41 = (bf16[128,1024]{1,0:T(8,128)(2,1)}, bf16[128,1024]{1,0:T(8,128)(2,1)S(1)}, u32[]{:S(2)}, u32[]{:S(2)}) collective-permute-start(bf16[128,1024]{1,0:T(8,128)(2,1)} %get-tuple-element.68), channel_id=1, source_target_pairs={{0,8},{8,16},{16,24},{24,0},{32,40},{40,48},{48,56},{56,32},{64,72... | collective-permute-start | bytes 786440 | tf_op jit(solution)/shard_map/ppermute | solution.py:44
  136.6 13.5 %collective-permute-start.39 = (bf16[128,1024]{1,0:T(8,128)(2,1)}, bf16[128,1024]{1,0:T(8,128)(2,1)S(1)}, u32[]{:S(2)}, u32[]{:S(2)}) collective-permute-start(bf16[128,1024]{1,0:T(8,128)(2,1)} %get-tuple-element.66), channel_id=1, source_target_pairs={{0,24},{8,0},{16,8},{24,16},{32,56},{40,32},{48,40},{56,48},{64,88... | collective-permute-start | bytes 786440 | tf_op jit(solution)/shard_map/ppermute | solution.py:44
  137.2 12.9 %collective-permute-start.40 = (bf16[128,1024]{1,0:T(8,128)(2,1)}, bf16[128,1024]{1,0:T(8,128)(2,1)S(1)}, u32[]{:S(2)}, u32[]{:S(2)}) collective-permute-start(bf16[128,1024]{1,0:T(8,128)(2,1)} %get-tuple-element.67), channel_id=1, source_target_pairs={{0,16},{8,24},{16,0},{24,8},{32,48},{40,56},{48,32},{56,40},{64,80... | collective-permute-start | bytes 786440 | tf_op jit(solution)/shard_map/ppermute | solution.py:44
  (28 other events, 268.4 us)
Sparse Core Ops, SparseCore 0:
  9.7 51.6 all-gather.5
  76.4 52.3 all-gather.3

commit v6 on v4

--- a/solution.py
+++ b/solution.py
@@ -286,7 +286,7 @@
     )(place, term, turned, *u_near, u_far)
 
 
-def solve_body(p_raw, inverse, out, p, left_here):
+def solve_body(p_raw, inverse):
     squares = jnp.zeros((192, 192), F32)
     for i in range(4):
         stack = jnp.concatenate(thirds(p_raw[:, 1024 * i : 1024 * i + 1024]), 0)
@@ -301,67 +301,45 @@
         scale = both[:, k : k + 1] / both[k : k + 1, k : k + 1]
         both = both - jnp.where(row > k, scale * both[k : k + 1, :], 0.0)
     diagonal = jnp.sum(jnp.where(same, both[:, :64], 0.0), 1, keepdims=True)
-    solved = both[:, 64:] / jnp.sqrt(diagonal)
-    inverse[...] = solved
-    high, low = halves(solved)
-    solved_split = jnp.concatenate([high, high, low], 1)
-    for i in range(4):
-        at = slice(1024 * i, 1024 * i + 1024)
-        high, low = halves(p_raw[:, at])
-        high, low = halves(mm(solved_split, jnp.concatenate([high, low, high], 0)))
-        p[:, at] = jnp.concatenate([high, low, high], 0)
-        pltpu.make_async_copy(p.at[:, at], out.at[:, at], left_here.at[i]).start()
-    for i in range(4):
-        at = slice(1024 * i, 1024 * i + 1024)
-        pltpu.make_async_copy(p.at[:, at], out.at[:, at], left_here.at[i]).wait()
+    inverse[...] = both[:, 64:] / jnp.sqrt(diagonal)
 
 
 def solve(p_raw):
-    return pallas(
-        solve_body,
-        [shaped((64, 64)), pltpu.HBM((192, 4096), BF16)],
-        in_specs=[VMEM],
-        out_specs=[VMEM, HBM],
-        scratch_shapes=[pltpu.VMEM((192, 4096), BF16), pltpu.SemaphoreType.DMA((4,))],
-    )(p_raw)
-
-
-def last_body(inverse, w, turned, p_far, error, ctx, q_out, out, p, held, held_ctx, arrived, arrived_ctx, left_here, p_here):
+    return pallas(solve_body, shaped((64, 64)), in_specs=[VMEM], out_specs=VMEM)(p_raw)
+
+
+def last_body(inverse, w, turned, p_raw, error, ctx, q_out, out, held, held_ctx, arrived, arrived_ctx, left_here):
     ctx_blocks, blocks = Fetch(ctx, held_ctx, arrived_ctx, 1, ENDS_SMALL), Fetch(error, held, arrived, 1, ENDS_SMALL)
-    p_copy = pltpu.make_async_copy(p_far, p, p_here)
-    p_copy.start()
-    ctx_blocks.wait(0)
-    product = mm(turned[...], held_ctx[:, ENDS_SMALL[0]])
     q = mm(inverse[...], w[...], NN, lax.Precision.HIGHEST) * (1.0 / 16)
     q_out[...] = q
     high, low = halves(q)
     q_split = jnp.concatenate([high, high, low], 0).T
-    p_copy.wait()
+    high, low = halves(inverse[...])
+    inverse_split = jnp.concatenate([high, high, low], 1)
     stores = []
     for i, at in enumerate(ENDS_SMALL):
-        approx = mm(q_split, p[:, at])
+        high, low = halves(p_raw[:, at])
+        high, low = halves(mm(inverse_split, jnp.concatenate([high, low, high], 0)))
+        approx = mm(q_split, jnp.concatenate([high, low, high], 0))
+        ctx_blocks.wait(i)
+        product = mm(turned[...], held_ctx[:, at])
         blocks.wait(i)
         held[:, at] = (held[:, at] + product) - approx
         stores.append(pltpu.make_async_copy(held.at[:, at], out.at[:, at], left_here.at[i]))
         stores[-1].start()
-        if i < 4:
-            ctx_blocks.wait(i + 1)
-            product = mm(turned[...], held_ctx[:, ENDS_SMALL[i + 1]])
     for store in stores:
         store.wait()
 
 
-def last(inverse, w, turned, p, error, ctx):
+def last(inverse, w, turned, p_raw, error, ctx):
     return pallas(
         last_body,
         [shaped((64, 512)), shaped((512, 4096))],
         mib=24,
-        in_specs=[VMEM] * 3 + [HBM] * 3,
+        in_specs=[VMEM] * 4 + [HBM] * 2,
         out_specs=[VMEM, HBM],
-        scratch_shapes=[pltpu.VMEM((192, 4096), BF16), pltpu.VMEM((512, 4096), F32), pltpu.VMEM((1024, 4096), BF16)]
-        + [pltpu.SemaphoreType.DMA((5,))] * 3
-        + [pltpu.SemaphoreType.DMA],
-    )(inverse, w, turned, in_hbm(p), in_hbm(error), in_hbm(ctx))
+        scratch_shapes=[pltpu.VMEM((512, 4096), F32), pltpu.VMEM((1024, 4096), BF16)] + [pltpu.SemaphoreType.DMA((5,))] * 3,
+    )(inverse, w, turned, p_raw, in_hbm(error), in_hbm(ctx))
 
 
 def share_body(place, tokens, *refs):
@@ -413,7 +391,7 @@
 
     passed = other_core(after(cut_far(place, grad_out), near))
     blocks = [half[:8]] + [along_y(half[8 * d : 8 * d + 8], d) for d in (1, 2, 3)]
-    blocks[3] = after(blocks[3], pieces[2], passed)
+    blocks[3] = after(blocks[3], passed)
     summed = pair_sum(blocks)
     w0 = after(jnp.stack(pieces), summed)
     w1, w3 = [along_y(w0, d) for d in (-1, 1)]
@@ -438,14 +416,14 @@
     u_far = other_core(jnp.concatenate([u, u_near[1], u_near[2], after(u_near[3], w_term, their0, their3)], 0))
     w = collect(place, w_term, turned, u_near, u_far)
     w = [w] + [along_z(w, d) for d in (1, 2, 3)]
-    inverse, p = solve(p_raw)
-    w = pair_sum([w[0], w[1], w[2], after(w[3], p, w2)])
+    inverse = solve(p_raw)
+    w = pair_sum([w[0], w[1], w[2], after(w[3], inverse, w2)])
     their2 = other_core(after(w2, w))
     w = [w] + [along_y(w, d) for d in (1, 2, 3)]
     outs = share(place, tokens, [w0, w1, w2, w3], [their0, their1, their2, their3])
     w = pair_sum([w[0], w[1], w[2], after(w[3], outs[0])])
     outs = [outs[0]] + [along_z(outs[d], d) for d in (1, 2, 3)]
-    q_factor, new_error = last(inverse, w, turned, p, error, ctx_all)
+    q_factor, new_error = last(inverse, w, turned, p_raw, error, ctx_all)
     grad_ctx = join(place, [outs[0], outs[3], outs[2], after(outs[1], q_factor)])
     return (grad_ctx, q_factor.T, new_error[None])
 

time: 158 us -> 158 us (level)
    ppermute x15, waiting for transfers between devices: 15.8 us -> 12.6 us  [along_x(): lax.ppermute(value, 'fsdp', [(i, (i // 2 + d) % 4 * 2 + i % 2) for i in r...]
    ppermute x12, waiting for transfers between devices: 15 us -> 16.6 us  [along_y(): lax.ppermute(value, 'dp', [(i, (i // 4 + d) % 4 * 4 + i % 4) for i in ran...]
    pallas_call x1, Pallas kernels: 7.75 us -> 6.14 us  [solve(): pallas(solve_body, shaped((64, 64)), in_specs=[VMEM], out_specs=VMEM)(p_raw)]
  transfers between devices with their start and end apart: 47 -> 47, of which waited for: 18 -> 20; matrix products, arithmetic and copies ran while one was open for 2% -> 2% of each run, Pallas kernels for 27% -> 27%
where the time goes in v6:
time: 158 us; the launch traced here: 157 us
  starting transfers between devices  57.3 us (36%)
  Pallas kernels  43.4 us (27%)
  waiting for transfers between devices  36.7 us (23%)
  between operations  14.5 us (9%)
  local copies, waits for them, and re-layouts  4.83 us (3%)
    ppermute x15, starting transfers between devices, along_x(): lax.ppermute(value, 'fsdp', [(i, (i // 2 + d) % 4 * 2 + i % 2) for i in r...  18.5 us
    ppermute x12, waiting for transfers between devices, along_y(): lax.ppermute(value, 'dp', [(i, (i // 4 + d) % 4 * 4 + i % 4) for i in ran...  16.6 us
    ppermute x9, starting transfers between devices, along_z(): lax.ppermute(value, 'dp', [(i, i // 4 * 4 + (i % 4 + d) % 4) for i in ran...  16.1 us
    ppermute x15, waiting for transfers between devices, along_x(): lax.ppermute(value, 'fsdp', [(i, (i // 2 + d) % 4 * 2 + i % 2) for i in r...  12.6 us
    pallas_call x1, Pallas kernels, last(): pallas(last_body, [shaped((64, 512)), shaped((512, 4096))], mib=24, in_sp...  12.1 us
    ppermute x12, starting transfers between devices, along_y(): lax.ppermute(value, 'dp', [(i, (i // 4 + d) % 4 * 4 + i % 4) for i in ran...  11.8 us
    ppermute x9, starting transfers between devices, other_core(): return lax.ppermute(value, 'fsdp', [(i, i ^ 1) for i in range(8)])  10.9 us
    pallas_call x1, Pallas kernels, solve(): pallas(solve_body, shaped((64, 64)), in_specs=[VMEM], out_specs=VMEM)(p_raw)  6.14 us
  transfers between devices with their start and end apart: 47, of which 20 were waited for; matrix products, arithmetic and copies ran while one was open for 2% of the time, Pallas kernels for 27%

profile of v6, /device:TPU:1, one launch (start us, length us, event | category | flops | bytes accessed | tf_op | source)
XLA Modules:
  0.0 157.2 jit_solution(3932364469570466111)
XLA Ops:
  9.0 3.4 %collective-permute-start.3 = (bf16[256,512]{1,0:T(8,128)(2,1)S(1)}, bf16[256,512]{1,0:T(8,128)(2,1)S(1)}, u32[]{:S(2)}, u32[]{:S(2)}) collective-permute-start(bf16[256,512]{1,0:T(8,128)(2,1)S(1)} %constant_dynamic-slice_fusion), channel_id=1, source_target_pairs={{0,6},{1,7},{2,0},{3,1},{4,2},{5,3},{6,4},{7,5},{8,14},{9,15},{10,... | collective-permute-start | bytes 786440 | tf_op jit(solution)/shard_map/ppermute | solution.py:36
  12.3 2.7 %collective-permute-start.1 = (f32[64,512]{1,0:T(8,128)}, f32[64,512]{1,0:T(8,128)S(1)}, u32[]{:S(2)}, u32[]{:S(2)}) collective-permute-start(f32[64,512]{1,0:T(8,128)} %bitcast.15), channel_id=1, source_target_pairs={{0,6},{1,7},{2,0},{3,1},{4,2},{5,3},{6,4},{7,5},{8,14},{9,15},{10,... | collective-permute-start | bytes 393224 | tf_op jit(solution)/shard_map/ppermute | solution.py:36
  16.6 4.6 %shard_map.76.term = f32[64,4096]{1,0:T(8,128)S(1)} custom-call(s32[4]{0:T(128)S(1)} %pad_add_fusion.place, f32[64,512]{1,0:T(8,128)S(1)} %bitcast.18, f32[512,4096]{1,0:T(8,128)} %bitcast.21), custom_call_target="tpu_custom_call" | custom-call | tf_op jit(solution)/shard_map/pallas_call | solution.py:142
  22.1 3.9 %collective-permute-done.5.q3 = f32[64,512]{1,0:T(8,128)S(1)} collective-permute-done((f32[64,512]{1,0:T(8,128)}, f32[64,512]{1,0:T(8,128)S(1)}, u32[]{:S(2)}, u32[]{:S(2)}) %collective-permute-start.5) | collective-permute-done | bytes 131104 | tf_op jit(solution)/shard_map/ppermute | solution.py:36
  26.1 1.9 %collective-permute-start.6 = (f32[256,512]{1,0:T(8,128)S(1)}, f32[256,512]{1,0:T(8,128)S(1)}, u32[]{:S(2)}, u32[]{:S(2)}) collective-permute-start(f32[256,512]{1,0:T(8,128)S(1)} %pad_maximum_fusion.1), channel_id=1, source_target_pairs={{0,1},{1,0},{2,3},{3,2},{4,5},{5,4},{6,7},{7,6},{8,9},{9,8},{10,11... | collective-permute-start | bytes 1572872 | tf_op jit(solution)/shard_map/ppermute | solution.py:48
  29.6 2.4 %shard_map.77 = (f32[32,4096]{1,0:T(8,128)S(1)}, f32[32,4096]{1,0:T(8,128)S(1)}) custom-call(s32[4]{0:T(128)S(1)} %pad_add_fusion.place, f32[64,512]{1,0:T(8,128)S(1)} %bitcast.20, f32[64,512]{1,0:T(8,128)S(1)} %collective-permute-done.1.q1, f32[64,512]{1,0:T(8,128)S(1)} %collective-permute-done.4.q2, f32[64,512]{1,0:T(8,128)S(1)} %collective-permute-done.5.q3, ...), custom_call_target="tpu_custom_call" | custom-call | tf_op jit(solution)/shard_map/pallas_call | solution.py:172
  34.1 2.8 %collective-permute-start.10 = (f32[8,4096]{1,0:T(8,128)S(1)}, f32[8,4096]{1,0:T(8,128)S(1)}, u32[]{:S(2)}, u32[]{:S(2)}) collective-permute-start(f32[8,4096]{1,0:T(8,128)S(1)} %get-tuple-element.71), channel_id=1, source_target_pairs={{0,96},{8,104},{16,112},{24,120},{32,0},{40,8},{48,16},{56,24},{64... | collective-permute-start | bytes 393224 | tf_op jit(solution)/shard_map/ppermute | solution.py:40
  39.0 3.1 %collective-permute-done.10 = f32[8,4096]{1,0:T(8,128)S(1)} collective-permute-done((f32[8,4096]{1,0:T(8,128)S(1)}, f32[8,4096]{1,0:T(8,128)S(1)}, u32[]{:S(2)}, u32[]{:S(2)}) %collective-permute-start.10) | collective-permute-done | bytes 131104 | tf_op jit(solution)/shard_map/ppermute | solution.py:40
  42.8 3.9 %collective-permute-done.9 = f32[8,4096]{1,0:T(8,128)S(1)} collective-permute-done((f32[8,4096]{1,0:T(8,128)S(1)}, f32[8,4096]{1,0:T(8,128)S(1)}, u32[]{:S(2)}, u32[]{:S(2)}) %collective-permute-start.9) | collective-permute-done | bytes 131104 | tf_op jit(solution)/shard_map/ppermute | solution.py:40
  46.9 2.7 %collective-permute-start.15 = (f32[8,4096]{1,0:T(8,128)S(1)}, f32[8,4096]{1,0:T(8,128)S(1)}, u32[]{:S(2)}, u32[]{:S(2)}) collective-permute-start(f32[8,4096]{1,0:T(8,128)S(1)} %fusion), channel_id=1, source_target_pairs={{0,6},{1,7},{2,0},{3,1},{4,2},{5,3},{6,4},{7,5},{8,14},{9,15},{10,... | collective-permute-start | bytes 393224 | tf_op jit(solution)/shard_map/ppermute | solution.py:36
  52.9 1.8 %collective-permute-done.15 = f32[8,4096]{1,0:T(8,128)S(1)} collective-permute-done((f32[8,4096]{1,0:T(8,128)S(1)}, f32[8,4096]{1,0:T(8,128)S(1)}, u32[]{:S(2)}, u32[]{:S(2)}) %collective-permute-start.15) | collective-permute-done | bytes 131104 | tf_op jit(solution)/shard_map/ppermute | solution.py:36
  57.6 2.1 %collective-permute-start.21 = (bf16[2,128,512]{2,1,0:T(8,128)(2,1)S(1)}, bf16[2,128,512]{2,1,0:T(8,128)(2,1)S(1)}, u32[]{:S(2)}, u32[]{:S(2)}) collective-permute-start(bf16[2,128,512]{2,1,0:T(8,128)(2,1)S(1)} %get-tuple-element.46), channel_id=1, source_target_pairs={{0,6},{1,7},{2,0},{3,1},{4,2},{5,3},{6,4},{7,5},{8,14},{9,15},{10,... | collective-permute-start | bytes 786440 | tf_op jit(solution)/shard_map/ppermute | solution.py:36
  59.7 3.8 %collective-permute-start.18 = (f32[8,4096]{1,0:T(8,128)S(1)}, f32[8,4096]{1,0:T(8,128)S(1)}, u32[]{:S(2)}, u32[]{:S(2)}) collective-permute-start(f32[8,4096]{1,0:T(8,128)S(1)} %add_add_fusion.3), channel_id=1, source_target_pairs={{0,24},{8,0},{16,8},{24,16},{32,56},{40,32},{48,40},{56,48},{64,88... | collective-permute-start | bytes 393224 | tf_op jit(solution)/shard_map/ppermute | solution.py:44
  63.5 1.9 %collective-permute-done.18 = f32[8,4096]{1,0:T(8,128)S(1)} collective-permute-done((f32[8,4096]{1,0:T(8,128)S(1)}, f32[8,4096]{1,0:T(8,128)S(1)}, u32[]{:S(2)}, u32[]{:S(2)}) %collective-permute-start.18) | collective-permute-done | bytes 131104 | tf_op jit(solution)/shard_map/ppermute | solution.py:44
  65.4 4.6 %collective-permute-start.16 = (f32[8,4096]{1,0:T(8,128)S(1)}, f32[8,4096]{1,0:T(8,128)S(1)}, u32[]{:S(2)}, u32[]{:S(2)}) collective-permute-start(f32[8,4096]{1,0:T(8,128)S(1)} %add_add_fusion.3), channel_id=1, source_target_pairs={{0,16},{8,24},{16,0},{24,8},{32,48},{40,56},{48,32},{56,40},{64,80... | collective-permute-start | bytes 393224 | tf_op jit(solution)/shard_map/ppermute | solution.py:44
  70.0 3.2 %collective-permute-done.12.refs_1_ = bf16[4,256,512]{2,1,0:T(8,128)(2,1)S(1)} collective-permute-done((bf16[4,256,512]{2,1,0:T(8,128)(2,1)S(1)}, bf16[4,256,512]{2,1,0:T(8,128)(2,1)S(1)}, u32[]{:S(2)}, u32[]{:S(2)}) %collective-permute-start.12) | collective-permute-done | bytes 1048608 | tf_op jit(solution)/shard_map/ppermute | solution.py:40
  74.3 3.5 %collective-permute-start.26 = (bf16[4,256,512]{2,1,0:T(8,128)(2,1)S(1)}, bf16[4,256,512]{2,1,0:T(8,128)(2,1)S(1)}, u32[]{:S(2)}, u32[]{:S(2)}) collective-permute-start(bf16[4,256,512]{2,1,0:T(8,128)(2,1)S(1)} %collective-permute-done.12.refs_1_), channel_id=1, source_target_pairs={{0,1},{1,0},{2,3},{3,2},{4,5},{5,4},{6,7},{7,6},{8,9},{9,8},{10,11... | collective-permute-start | bytes 3145736 | tf_op jit(solution)/shard_map/ppermute | solution.py:48
  77.9 3.0 %collective-permute-start.27 = (bf16[2,128,512]{2,1,0:T(8,128)(2,1)S(1)}, bf16[2,128,512]{2,1,0:T(8,128)(2,1)S(1)}, u32[]{:S(2)}, u32[]{:S(2)}) collective-permute-start(bf16[2,128,512]{2,1,0:T(8,128)(2,1)S(1)} %get-tuple-element.51), channel_id=1, source_target_pairs={{0,4},{1,5},{2,6},{3,7},{4,0},{5,1},{6,2},{7,3},{8,12},{9,13},{10,... | collective-permute-start | bytes 786440 | tf_op jit(solution)/shard_map/ppermute | solution.py:36
  80.8 2.0 %collective-permute-start.23 = (f32[8,4096]{1,0:T(8,128)S(1)}, f32[8,4096]{1,0:T(8,128)S(1)}, u32[]{:S(2)}, u32[]{:S(2)}) collective-permute-start(f32[8,4096]{1,0:T(8,128)S(1)} %add_add_fusion.2.p0), channel_id=1, source_target_pairs={{0,64},{8,72},{16,80},{24,88},{32,96},{40,104},{48,112},{56,120},{... | collective-permute-start | bytes 393224 | tf_op jit(solution)/shard_map/ppermute | solution.py:40
  82.8 2.8 %collective-permute-done.22.p1 = f32[8,4096]{1,0:T(8,128)S(1)} collective-permute-done((f32[8,4096]{1,0:T(8,128)S(1)}, f32[8,4096]{1,0:T(8,128)S(1)}, u32[]{:S(2)}, u32[]{:S(2)}) %collective-permute-start.22) | collective-permute-done | bytes 131104 | tf_op jit(solution)/shard_map/ppermute | solution.py:40
  85.5 1.7 %collective-permute-done.27.c2 = bf16[2,128,512]{2,1,0:T(8,128)(2,1)S(1)} collective-permute-done((bf16[2,128,512]{2,1,0:T(8,128)(2,1)S(1)}, bf16[2,128,512]{2,1,0:T(8,128)(2,1)S(1)}, u32[]{:S(2)}, u32[]{:S(2)}) %collective-permute-start.27) | collective-permute-done | bytes 262176 | tf_op jit(solution)/shard_map/ppermute | solution.py:36
  87.2 2.9 %collective-permute-done.24.p3 = f32[8,4096]{1,0:T(8,128)S(1)} collective-permute-done((f32[8,4096]{1,0:T(8,128)S(1)}, f32[8,4096]{1,0:T(8,128)S(1)}, u32[]{:S(2)}, u32[]{:S(2)}) %collective-permute-start.24) | collective-permute-done | bytes 131104 | tf_op jit(solution)/shard_map/ppermute | solution.py:40
  91.2 2.1 %shard_map.80.turned = bf16[512,1024]{1,0:T(8,128)(2,1)S(1)} custom-call(s32[4]{0:T(128)S(1)} %pad_add_fusion.place, bf16[2,128,512]{2,1,0:T(8,128)(2,1)} %copy-done.11, bf16[2,128,512]{2,1,0:T(8,128)(2,1)} %copy-done.12, bf16[2,128,512]{2,1,0:T(8,128)(2,1)} %copy-done.14, bf16[2,128,512]{2,1,0:T(8,128)(2,1)} %copy-done.13), custom_call_target="tpu_custom_call" | custom-call | tf_op jit(solution)/shard_map/pallas_call | solution.py:214
  96.5 2.7 %collective-permute-start.30 = (f32[64,128]{1,0:T(8,128)S(1)}, f32[64,128]{1,0:T(8,128)S(1)}, u32[]{:S(2)}, u32[]{:S(2)}) collective-permute-start(f32[64,128]{1,0:T(8,128)S(1)} %get-tuple-element.55.u0), channel_id=1, source_target_pairs={{0,6},{1,7},{2,0},{3,1},{4,2},{5,3},{6,4},{7,5},{8,14},{9,15},{10,... | collective-permute-start | bytes 98312 | tf_op jit(solution)/shard_map/ppermute | solution.py:36
  99.2 2.4 %collective-permute-done.32.u3 = f32[64,128]{1,0:T(8,128)S(1)} collective-permute-done((f32[64,128]{1,0:T(8,128)S(1)}, f32[64,128]{1,0:T(8,128)S(1)}, u32[]{:S(2)}, u32[]{:S(2)}) %collective-permute-start.32) | collective-permute-done | bytes 32800 | tf_op jit(solution)/shard_map/ppermute | solution.py:36
  101.7 5.0 %shard_map.82.term = f32[512,64]{1,0:T(8,128)S(1)} custom-call(f32[64,4096]{1,0:T(8,128)S(1)} %get-tuple-element.57.p_raw, f32[512,4096]{1,0:T(8,128)} %bitcast.22), custom_call_target="tpu_custom_call" | custom-call | tf_op jit(solution)/shard_map/pallas_call | solution.py:259
  106.9 2.0 %collective-permute-start.34 = (f32[256,128]{1,0:T(8,128)S(1)}, f32[256,128]{1,0:T(8,128)S(1)}, u32[]{:S(2)}, u32[]{:S(2)}) collective-permute-start(f32[256,128]{1,0:T(8,128)S(1)} %pad_maximum_fusion.3), channel_id=1, source_target_pairs={{0,1},{1,0},{2,3},{3,2},{4,5},{5,4},{6,7},{7,6},{8,9},{9,8},{10,11... | collective-permute-start | bytes 393224 | tf_op jit(solution)/shard_map/ppermute | solution.py:48
  111.1 3.8 %collective-permute-start.37 = (f32[64,512]{1,0:T(8,128)S(1)}, f32[64,512]{1,0:T(8,128)S(1)}, u32[]{:S(2)}, u32[]{:S(2)}) collective-permute-start(f32[64,512]{1,0:T(8,128)S(1)} %shard_map.83), channel_id=1, source_target_pairs={{0,24},{8,0},{16,8},{24,16},{32,56},{40,32},{48,40},{56,48},{64,88... | collective-permute-start | bytes 393224 | tf_op jit(solution)/shard_map/ppermute | solution.py:44
  116.2 6.1 %shard_map.84.inverse = f32[64,64]{1,0:T(8,128)S(1)} custom-call(f32[64,4096]{1,0:T(8,128)S(1)} %get-tuple-element.57.p_raw), custom_call_target="tpu_custom_call" | custom-call | tf_op jit(solution)/shard_map/pallas_call | solution.py:308
  127.9 6.0 %shard_map.85 = (bf16[128,1024]{1,0:T(8,128)(2,1)S(1)}, bf16[128,1024]{1,0:T(8,128)(2,1)}, bf16[128,1024]{1,0:T(8,128)(2,1)}, bf16[128,1024]{1,0:T(8,128)(2,1)}) custom-call(s32[4]{0:T(128)S(1)} %pad_add_fusion.place, bf16[4,128,4096]{2,1,0:T(8,128)(2,1)S(1)} %bitcast.14, bf16[4,256,512]{2,1,0:T(8,128)(2,1)S(1)} %copy-done.4, ...), custom_call_target="tpu_custom_call" | custom-call | tf_op jit(solution)/shard_map/pallas_call | solution.py:360
  134.7 2.0 %collective-permute-start.39 = (bf16[128,1024]{1,0:T(8,128)(2,1)}, bf16[128,1024]{1,0:T(8,128)(2,1)S(1)}, u32[]{:S(2)}, u32[]{:S(2)}) collective-permute-start(bf16[128,1024]{1,0:T(8,128)(2,1)} %get-tuple-element.63), channel_id=1, source_target_pairs={{0,24},{8,0},{16,8},{24,16},{32,56},{40,32},{48,40},{56,48},{64,88... | collective-permute-start | bytes 786440 | tf_op jit(solution)/shard_map/ppermute | solution.py:44
  136.7 12.1 %shard_map.86 = (f32[64,512]{1,0:T(8,128)}, f32[512,4096]{1,0:T(8,128)}) custom-call(f32[64,64]{1,0:T(8,128)S(1)} %shard_map.84.inverse, f32[64,512]{1,0:T(8,128)S(1)} %add_add_fusion.w, bf16[512,1024]{1,0:T(8,128)(2,1)S(1)} %shard_map.80.turned, f32[64,4096]{1,0:T(8,128)S(1)} %get-tuple-element.57.p_raw, f32[512,4096]{1,0:T(8,128)} %bitcast.23, ...), custom_call_target="tpu_custom_call" | custom-call | tf_op jit(solution)/shard_map/pallas_call | solution.py:335
  (132 shorter events, 34.0 us)
Async XLA Ops:
  7.2 67.1 %all-gather.6.cloned.1.call-start = ((), (), s32[]{:S(2)}) async-start(), calls=%async_computation.1 | async-start | bytes 5242880 | tf_op jit(solution)/shard_map/all_gather | solution.py:381
  7.9 128.8 %all-gather.4.cloned.1.call-start = ((), (), s32[]{:S(2)}) async-start(), calls=%async_computation | async-start | bytes 9437184 | tf_op jit(solution)/shard_map/all_gather | solution.py:404
  9.0 12.5 %collective-permute-start.3 = (bf16[256,512]{1,0:T(8,128)(2,1)S(1)}, bf16[256,512]{1,0:T(8,128)(2,1)S(1)}, u32[]{:S(2)}, u32[]{:S(2)}) collective-permute-start(bf16[256,512]{1,0:T(8,128)(2,1)S(1)} %constant_dynamic-slice_fusion), channel_id=1, source_target_pairs={{0,6},{1,7},{2,0},{3,1},{4,2},{5,3},{6,4},{7,5},{8,14},{9,15},{10,... | collective-permute-start | bytes 786440 | tf_op jit(solution)/shard_map/ppermute | solution.py:36
  12.3 9.1 %collective-permute-start = (bf16[256,512]{1,0:T(8,128)(2,1)S(1)}, bf16[256,512]{1,0:T(8,128)(2,1)S(1)}, u32[]{:S(2)}, u32[]{:S(2)}) collective-permute-start(bf16[256,512]{1,0:T(8,128)(2,1)S(1)} %constant_dynamic-slice_fusion), channel_id=1, source_target_pairs={{0,2},{1,3},{2,4},{3,5},{4,6},{5,7},{6,0},{7,1},{8,10},{9,11},{10,... | collective-permute-start | bytes 786440 | tf_op jit(solution)/shard_map/ppermute | solution.py:36
  12.3 9.1 %collective-permute-start.1 = (f32[64,512]{1,0:T(8,128)}, f32[64,512]{1,0:T(8,128)S(1)}, u32[]{:S(2)}, u32[]{:S(2)}) collective-permute-start(f32[64,512]{1,0:T(8,128)} %bitcast.15), channel_id=1, source_target_pairs={{0,6},{1,7},{2,0},{3,1},{4,2},{5,3},{6,4},{7,5},{8,14},{9,15},{10,... | collective-permute-start | bytes 393224 | tf_op jit(solution)/shard_map/ppermute | solution.py:36
  15.0 11.0 %collective-permute-start.5 = (f32[64,512]{1,0:T(8,128)}, f32[64,512]{1,0:T(8,128)S(1)}, u32[]{:S(2)}, u32[]{:S(2)}) collective-permute-start(f32[64,512]{1,0:T(8,128)} %bitcast.17), channel_id=1, source_target_pairs={{0,2},{1,3},{2,4},{3,5},{4,6},{5,7},{6,0},{7,1},{8,10},{9,11},{10,... | collective-permute-start | bytes 393224 | tf_op jit(solution)/shard_map/ppermute | solution.py:36
  34.1 8.0 %collective-permute-start.10 = (f32[8,4096]{1,0:T(8,128)S(1)}, f32[8,4096]{1,0:T(8,128)S(1)}, u32[]{:S(2)}, u32[]{:S(2)}) collective-permute-start(f32[8,4096]{1,0:T(8,128)S(1)} %get-tuple-element.71), channel_id=1, source_target_pairs={{0,96},{8,104},{16,112},{24,120},{32,0},{40,8},{48,16},{56,24},{64... | collective-permute-start | bytes 393224 | tf_op jit(solution)/shard_map/ppermute | solution.py:40
  37.3 9.5 %collective-permute-start.9 = (f32[8,4096]{1,0:T(8,128)S(1)}, f32[8,4096]{1,0:T(8,128)S(1)}, u32[]{:S(2)}, u32[]{:S(2)}) collective-permute-start(f32[8,4096]{1,0:T(8,128)S(1)} %get-tuple-element.72), channel_id=1, source_target_pairs={{0,32},{8,40},{16,48},{24,56},{32,64},{40,72},{48,80},{56,88},{64,... | collective-permute-start | bytes 393224 | tf_op jit(solution)/shard_map/ppermute | solution.py:40
  38.9 10.6 %collective-permute-start.2 = (bf16[256,512]{1,0:T(8,128)(2,1)S(1)}, bf16[256,512]{1,0:T(8,128)(2,1)S(1)}, u32[]{:S(2)}, u32[]{:S(2)}) collective-permute-start(bf16[256,512]{1,0:T(8,128)(2,1)S(1)} %copy-done.16), channel_id=1, source_target_pairs={{0,4},{1,5},{2,6},{3,7},{4,0},{5,1},{6,2},{7,3},{8,12},{9,13},{10,... | collective-permute-start | bytes 786440 | tf_op jit(solution)/shard_map/ppermute | solution.py:36
  46.9 7.8 %collective-permute-start.15 = (f32[8,4096]{1,0:T(8,128)S(1)}, f32[8,4096]{1,0:T(8,128)S(1)}, u32[]{:S(2)}, u32[]{:S(2)}) collective-permute-start(f32[8,4096]{1,0:T(8,128)S(1)} %fusion), channel_id=1, source_target_pairs={{0,6},{1,7},{2,0},{3,1},{4,2},{5,3},{6,4},{7,5},{8,14},{9,15},{10,... | collective-permute-start | bytes 393224 | tf_op jit(solution)/shard_map/ppermute | solution.py:36
  49.7 23.5 %collective-permute-start.12 = (bf16[4,256,512]{2,1,0:T(8,128)(2,1)S(1)}, bf16[4,256,512]{2,1,0:T(8,128)(2,1)S(1)}, u32[]{:S(2)}, u32[]{:S(2)}) collective-permute-start(bf16[4,256,512]{2,1,0:T(8,128)(2,1)S(1)} %pad_maximum_fusion.refs_0_), channel_id=1, source_target_pairs={{0,96},{8,104},{16,112},{24,120},{32,0},{40,8},{48,16},{56,24},{64... | collective-permute-start | bytes 3145736 | tf_op jit(solution)/shard_map/ppermute | solution.py:40
  49.8 23.4 %collective-permute-start.19 = (bf16[4,256,512]{2,1,0:T(8,128)(2,1)S(1)}, bf16[4,256,512]{2,1,0:T(8,128)(2,1)S(1)}, u32[]{:S(2)}, u32[]{:S(2)}) collective-permute-start(bf16[4,256,512]{2,1,0:T(8,128)(2,1)S(1)} %pad_maximum_fusion.refs_0_), channel_id=1, source_target_pairs={{0,32},{8,40},{16,48},{24,56},{32,64},{40,72},{48,80},{56,88},{64,... | collective-permute-start | bytes 3145736 | tf_op jit(solution)/shard_map/ppermute | solution.py:40
  56.3 9.1 %collective-permute-start.20 = (bf16[2,128,512]{2,1,0:T(8,128)(2,1)S(1)}, bf16[2,128,512]{2,1,0:T(8,128)(2,1)S(1)}, u32[]{:S(2)}, u32[]{:S(2)}) collective-permute-start(bf16[2,128,512]{2,1,0:T(8,128)(2,1)S(1)} %get-tuple-element.45), channel_id=1, source_target_pairs={{0,2},{1,3},{2,4},{3,5},{4,6},{5,7},{6,0},{7,1},{8,10},{9,11},{10,... | collective-permute-start | bytes 786440 | tf_op jit(solution)/shard_map/ppermute | solution.py:36
  57.6 12.3 %collective-permute-start.21 = (bf16[2,128,512]{2,1,0:T(8,128)(2,1)S(1)}, bf16[2,128,512]{2,1,0:T(8,128)(2,1)S(1)}, u32[]{:S(2)}, u32[]{:S(2)}) collective-permute-start(bf16[2,128,512]{2,1,0:T(8,128)(2,1)S(1)} %get-tuple-element.46), channel_id=1, source_target_pairs={{0,6},{1,7},{2,0},{3,1},{4,2},{5,3},{6,4},{7,5},{8,14},{9,15},{10,... | collective-permute-start | bytes 786440 | tf_op jit(solution)/shard_map/ppermute | solution.py:36
  65.4 7.8 %collective-permute-start.17 = (f32[8,4096]{1,0:T(8,128)S(1)}, f32[8,4096]{1,0:T(8,128)S(1)}, u32[]{:S(2)}, u32[]{:S(2)}) collective-permute-start(f32[8,4096]{1,0:T(8,128)S(1)} %add_add_fusion.3), channel_id=1, source_target_pairs={{0,8},{8,16},{16,24},{24,0},{32,40},{40,48},{48,56},{56,32},{64,72... | collective-permute-start | bytes 393224 | tf_op jit(solution)/shard_map/ppermute | solution.py:44
  65.4 8.8 %collective-permute-start.16 = (f32[8,4096]{1,0:T(8,128)S(1)}, f32[8,4096]{1,0:T(8,128)S(1)}, u32[]{:S(2)}, u32[]{:S(2)}) collective-permute-start(f32[8,4096]{1,0:T(8,128)S(1)} %add_add_fusion.3), channel_id=1, source_target_pairs={{0,16},{8,24},{16,0},{24,8},{32,48},{40,56},{48,32},{56,40},{64,80... | collective-permute-start | bytes 393224 | tf_op jit(solution)/shard_map/ppermute | solution.py:44
  74.3 12.9 %collective-permute-start.26 = (bf16[4,256,512]{2,1,0:T(8,128)(2,1)S(1)}, bf16[4,256,512]{2,1,0:T(8,128)(2,1)S(1)}, u32[]{:S(2)}, u32[]{:S(2)}) collective-permute-start(bf16[4,256,512]{2,1,0:T(8,128)(2,1)S(1)} %collective-permute-done.12.refs_1_), channel_id=1, source_target_pairs={{0,1},{1,0},{2,3},{3,2},{4,5},{5,4},{6,7},{7,6},{8,9},{9,8},{10,11... | collective-permute-start | bytes 3145736 | tf_op jit(solution)/shard_map/ppermute | solution.py:48
  77.9 9.4 %collective-permute-start.27 = (bf16[2,128,512]{2,1,0:T(8,128)(2,1)S(1)}, bf16[2,128,512]{2,1,0:T(8,128)(2,1)S(1)}, u32[]{:S(2)}, u32[]{:S(2)}) collective-permute-start(bf16[2,128,512]{2,1,0:T(8,128)(2,1)S(1)} %get-tuple-element.51), channel_id=1, source_target_pairs={{0,4},{1,5},{2,6},{3,7},{4,0},{5,1},{6,2},{7,3},{8,12},{9,13},{10,... | collective-permute-start | bytes 786440 | tf_op jit(solution)/shard_map/ppermute | solution.py:36
  82.8 7.3 %collective-permute-start.24 = (f32[8,4096]{1,0:T(8,128)S(1)}, f32[8,4096]{1,0:T(8,128)S(1)}, u32[]{:S(2)}, u32[]{:S(2)}) collective-permute-start(f32[8,4096]{1,0:T(8,128)S(1)} %add_add_fusion.2.p0), channel_id=1, source_target_pairs={{0,32},{8,40},{16,48},{24,56},{32,64},{40,72},{48,80},{56,88},{64,... | collective-permute-start | bytes 393224 | tf_op jit(solution)/shard_map/ppermute | solution.py:40
  94.5 12.2 %collective-permute-start.29 = (bf16[4,256,512]{2,1,0:T(8,128)(2,1)S(1)}, bf16[4,256,512]{2,1,0:T(8,128)(2,1)S(1)}, u32[]{:S(2)}, u32[]{:S(2)}) collective-permute-start(bf16[4,256,512]{2,1,0:T(8,128)(2,1)S(1)} %copy-done.4), channel_id=1, source_target_pairs={{0,1},{1,0},{2,3},{3,2},{4,5},{5,4},{6,7},{7,6},{8,9},{9,8},{10,11... | collective-permute-start | bytes 3145736 | tf_op jit(solution)/shard_map/ppermute | solution.py:48
  94.6 12.1 %collective-permute-start.33 = (bf16[4,256,512]{2,1,0:T(8,128)(2,1)S(1)}, bf16[4,256,512]{2,1,0:T(8,128)(2,1)S(1)}, u32[]{:S(2)}, u32[]{:S(2)}) collective-permute-start(bf16[4,256,512]{2,1,0:T(8,128)(2,1)S(1)} %copy-done.10), channel_id=1, source_target_pairs={{0,1},{1,0},{2,3},{3,2},{4,5},{5,4},{6,7},{7,6},{8,9},{9,8},{10,11... | collective-permute-start | bytes 3145736 | tf_op jit(solution)/shard_map/ppermute | solution.py:48
  95.1 27.2 %collective-permute-start.25 = (bf16[4,256,512]{2,1,0:T(8,128)(2,1)S(1)}, bf16[4,256,512]{2,1,0:T(8,128)(2,1)S(1)}, u32[]{:S(2)}, u32[]{:S(2)}) collective-permute-start(bf16[4,256,512]{2,1,0:T(8,128)(2,1)S(1)} %copy-done.4), channel_id=1, source_target_pairs={{0,64},{8,72},{16,80},{24,88},{32,96},{40,104},{48,112},{56,120},{... | collective-permute-start | bytes 3145736 | tf_op jit(solution)/shard_map/ppermute | solution.py:40
  96.5 10.1 %collective-permute-start.30 = (f32[64,128]{1,0:T(8,128)S(1)}, f32[64,128]{1,0:T(8,128)S(1)}, u32[]{:S(2)}, u32[]{:S(2)}) collective-permute-start(f32[64,128]{1,0:T(8,128)S(1)} %get-tuple-element.55.u0), channel_id=1, source_target_pairs={{0,6},{1,7},{2,0},{3,1},{4,2},{5,3},{6,4},{7,5},{8,14},{9,15},{10,... | collective-permute-start | bytes 98312 | tf_op jit(solution)/shard_map/ppermute | solution.py:36
  111.1 11.2 %collective-permute-start.37 = (f32[64,512]{1,0:T(8,128)S(1)}, f32[64,512]{1,0:T(8,128)S(1)}, u32[]{:S(2)}, u32[]{:S(2)}) collective-permute-start(f32[64,512]{1,0:T(8,128)S(1)} %shard_map.83), channel_id=1, source_target_pairs={{0,24},{8,0},{16,8},{24,16},{32,56},{40,32},{48,40},{56,48},{64,88... | collective-permute-start | bytes 393224 | tf_op jit(solution)/shard_map/ppermute | solution.py:44
  114.9 8.9 %collective-permute-start.36 = (f32[64,512]{1,0:T(8,128)S(1)}, f32[64,512]{1,0:T(8,128)S(1)}, u32[]{:S(2)}, u32[]{:S(2)}) collective-permute-start(f32[64,512]{1,0:T(8,128)S(1)} %shard_map.83), channel_id=1, source_target_pairs={{0,8},{8,16},{16,24},{24,0},{32,40},{40,48},{48,56},{56,32},{64,72... | collective-permute-start | bytes 393224 | tf_op jit(solution)/shard_map/ppermute | solution.py:44
  114.9 8.9 %collective-permute-start.35 = (f32[64,512]{1,0:T(8,128)S(1)}, f32[64,512]{1,0:T(8,128)S(1)}, u32[]{:S(2)}, u32[]{:S(2)}) collective-permute-start(f32[64,512]{1,0:T(8,128)S(1)} %shard_map.83), channel_id=1, source_target_pairs={{0,16},{8,24},{16,0},{24,8},{32,48},{40,56},{48,32},{56,40},{64,80... | collective-permute-start | bytes 393224 | tf_op jit(solution)/shard_map/ppermute | solution.py:44
  124.9 11.7 %collective-permute-start.44 = (f32[64,512]{1,0:T(8,128)S(1)}, f32[64,512]{1,0:T(8,128)S(1)}, u32[]{:S(2)}, u32[]{:S(2)}) collective-permute-start(f32[64,512]{1,0:T(8,128)S(1)} %add_add_fusion.1), channel_id=1, source_target_pairs={{0,96},{8,104},{16,112},{24,120},{32,0},{40,8},{48,16},{56,24},{64... | collective-permute-start | bytes 393224 | tf_op jit(solution)/shard_map/ppermute | solution.py:40
  126.4 10.2 %collective-permute-start.43 = (f32[64,512]{1,0:T(8,128)S(1)}, f32[64,512]{1,0:T(8,128)S(1)}, u32[]{:S(2)}, u32[]{:S(2)}) collective-permute-start(f32[64,512]{1,0:T(8,128)S(1)} %add_add_fusion.1), channel_id=1, source_target_pairs={{0,32},{8,40},{16,48},{24,56},{32,64},{40,72},{48,80},{56,88},{64,... | collective-permute-start | bytes 393224 | tf_op jit(solution)/shard_map/ppermute | solution.py:40
  126.4 10.2 %collective-permute-start.42 = (f32[64,512]{1,0:T(8,128)S(1)}, f32[64,512]{1,0:T(8,128)S(1)}, u32[]{:S(2)}, u32[]{:S(2)}) collective-permute-start(f32[64,512]{1,0:T(8,128)S(1)} %add_add_fusion.1), channel_id=1, source_target_pairs={{0,64},{8,72},{16,80},{24,88},{32,96},{40,104},{48,112},{56,120},{... | collective-permute-start | bytes 393224 | tf_op jit(solution)/shard_map/ppermute | solution.py:40
  134.0 14.8 %collective-permute-start.41 = (bf16[128,1024]{1,0:T(8,128)(2,1)}, bf16[128,1024]{1,0:T(8,128)(2,1)S(1)}, u32[]{:S(2)}, u32[]{:S(2)}) collective-permute-start(bf16[128,1024]{1,0:T(8,128)(2,1)} %get-tuple-element.65), channel_id=1, source_target_pairs={{0,8},{8,16},{16,24},{24,0},{32,40},{40,48},{48,56},{56,32},{64,72... | collective-permute-start | bytes 786440 | tf_op jit(solution)/shard_map/ppermute | solution.py:44
  134.7 14.1 %collective-permute-start.39 = (bf16[128,1024]{1,0:T(8,128)(2,1)}, bf16[128,1024]{1,0:T(8,128)(2,1)S(1)}, u32[]{:S(2)}, u32[]{:S(2)}) collective-permute-start(bf16[128,1024]{1,0:T(8,128)(2,1)} %get-tuple-element.63), channel_id=1, source_target_pairs={{0,24},{8,0},{16,8},{24,16},{32,56},{40,32},{48,40},{56,48},{64,88... | collective-permute-start | bytes 786440 | tf_op jit(solution)/shard_map/ppermute | solution.py:44
  136.6 12.2 %collective-permute-start.40 = (bf16[128,1024]{1,0:T(8,128)(2,1)}, bf16[128,1024]{1,0:T(8,128)(2,1)S(1)}, u32[]{:S(2)}, u32[]{:S(2)}) collective-permute-start(bf16[128,1024]{1,0:T(8,128)(2,1)} %get-tuple-element.64), channel_id=1, source_target_pairs={{0,16},{8,24},{16,0},{24,8},{32,48},{40,56},{48,32},{56,40},{64,80... | collective-permute-start | bytes 786440 | tf_op jit(solution)/shard_map/ppermute | solution.py:44
  (36 other events, 353.7 us)
Sparse Core Ops, SparseCore 0:
  9.7 51.6 all-gather.5
  74.4 54.4 all-gather.3

commit v7 on v6

--- a/solution.py
+++ b/solution.py
@@ -412,13 +412,13 @@
     p_raw, u = middle(place, p_near, after(p_far, turned), ctx)
     u_near = [u] + [along_x(u, -d) for d in (1, 2, 3)]
     w_term = right(p_raw, error)
-    their0, their3 = other_core(after(w0, u)), other_core(after(w3, u))
-    u_far = other_core(jnp.concatenate([u, u_near[1], u_near[2], after(u_near[3], w_term, their0, their3)], 0))
+    their0 = other_core(after(w0, u))
+    u_far = other_core(jnp.concatenate([u, u_near[1], u_near[2], after(u_near[3], w_term, their0)], 0))
     w = collect(place, w_term, turned, u_near, u_far)
     w = [w] + [along_z(w, d) for d in (1, 2, 3)]
     inverse = solve(p_raw)
     w = pair_sum([w[0], w[1], w[2], after(w[3], inverse, w2)])
-    their2 = other_core(after(w2, w))
+    their2, their3 = [other_core(after(v, w)) for v in (w2, w3)]
     w = [w] + [along_y(w, d) for d in (1, 2, 3)]
     outs = share(place, tokens, [w0, w1, w2, w3], [their0, their1, their2, their3])
     w = pair_sum([w[0], w[1], w[2], after(w[3], outs[0])])

time: 158 us -> 158 us (level)
  starting transfers between devices: 57.3 us -> 59.2 us
  waiting for transfers between devices: 36.7 us -> 35.1 us
    ppermute x15, waiting for transfers between devices: 12.6 us -> 10.1 us  [along_x(): lax.ppermute(value, 'fsdp', [(i, (i // 2 + d) % 4 * 2 + i % 2) for i in r...]
    ppermute x9, starting transfers between devices: 16.1 us -> 18.1 us  [along_z(): lax.ppermute(value, 'dp', [(i, i // 4 * 4 + (i % 4 + d) % 4) for i in ran...]
  transfers between devices with their start and end apart: 47 -> 47, of which waited for: 20 -> 21; matrix products, arithmetic and copies ran while one was open for 2% -> 2% of each run, Pallas kernels for 27% -> 27%
where the time goes in v7:
time: 158 us
  starting transfers between devices  59.2 us (37%)
  Pallas kernels  43.4 us (27%)
  waiting for transfers between devices  35.1 us (22%)
  between operations  14.5 us (9%)
  local copies, waits for them, and re-layouts  4.83 us (3%)
    ppermute x15, starting transfers between devices, along_x(): lax.ppermute(value, 'fsdp', [(i, (i // 2 + d) % 4 * 2 + i % 2) for i in r...  18.5 us
    ppermute x9, starting transfers between devices, along_z(): lax.ppermute(value, 'dp', [(i, i // 4 * 4 + (i % 4 + d) % 4) for i in ran...  18.1 us
    ppermute x12, waiting for transfers between devices, along_y(): lax.ppermute(value, 'dp', [(i, (i // 4 + d) % 4 * 4 + i % 4) for i in ran...  17.5 us
    pallas_call x1, Pallas kernels, last(): pallas(last_body, [shaped((64, 512)), shaped((512, 4096))], mib=24, in_sp...  12.1 us
    ppermute x12, starting transfers between devices, along_y(): lax.ppermute(value, 'dp', [(i, (i // 4 + d) % 4 * 4 + i % 4) for i in ran...  11.8 us
    ppermute x9, starting transfers between devices, other_core(): return lax.ppermute(value, 'fsdp', [(i, i ^ 1) for i in range(8)])  10.6 us
    ppermute x15, waiting for transfers between devices, along_x(): lax.ppermute(value, 'fsdp', [(i, (i // 2 + d) % 4 * 2 + i % 2) for i in r...  10.1 us
    pallas_call x1, Pallas kernels, solve(): pallas(solve_body, shaped((64, 64)), in_specs=[VMEM], out_specs=VMEM)(p_raw)  6.14 us
  transfers between devices with their start and end apart: 47, of which 21 were waited for; matrix products, arithmetic and copies ran while one was open for 2% of the time, Pallas kernels for 27%

profile of v7, /device:TPU:1, one launch (start us, length us, event | category | flops | bytes accessed | tf_op | source)
XLA Modules:
  0.0 157.5 jit_solution(2208170889838361392)
XLA Ops:
  9.0 3.4 %collective-permute-start.3 = (bf16[256,512]{1,0:T(8,128)(2,1)S(1)}, bf16[256,512]{1,0:T(8,128)(2,1)S(1)}, u32[]{:S(2)}, u32[]{:S(2)}) collective-permute-start(bf16[256,512]{1,0:T(8,128)(2,1)S(1)} %constant_dynamic-slice_fusion), channel_id=1, source_target_pairs={{0,6},{1,7},{2,0},{3,1},{4,2},{5,3},{6,4},{7,5},{8,14},{9,15},{10,... | collective-permute-start | bytes 786440 | tf_op jit(solution)/shard_map/ppermute | solution.py:36
  12.3 2.7 %collective-permute-start.1 = (f32[64,512]{1,0:T(8,128)}, f32[64,512]{1,0:T(8,128)S(1)}, u32[]{:S(2)}, u32[]{:S(2)}) collective-permute-start(f32[64,512]{1,0:T(8,128)} %bitcast.15), channel_id=1, source_target_pairs={{0,6},{1,7},{2,0},{3,1},{4,2},{5,3},{6,4},{7,5},{8,14},{9,15},{10,... | collective-permute-start | bytes 393224 | tf_op jit(solution)/shard_map/ppermute | solution.py:36
  16.6 4.6 %shard_map.76.term = f32[64,4096]{1,0:T(8,128)S(1)} custom-call(s32[4]{0:T(128)S(1)} %pad_add_fusion.place, f32[64,512]{1,0:T(8,128)S(1)} %bitcast.18, f32[512,4096]{1,0:T(8,128)} %bitcast.21), custom_call_target="tpu_custom_call" | custom-call | tf_op jit(solution)/shard_map/pallas_call | solution.py:142
  22.1 3.9 %collective-permute-done.5.q3 = f32[64,512]{1,0:T(8,128)S(1)} collective-permute-done((f32[64,512]{1,0:T(8,128)}, f32[64,512]{1,0:T(8,128)S(1)}, u32[]{:S(2)}, u32[]{:S(2)}) %collective-permute-start.5) | collective-permute-done | bytes 131104 | tf_op jit(solution)/shard_map/ppermute | solution.py:36
  26.1 1.9 %collective-permute-start.6 = (f32[256,512]{1,0:T(8,128)S(1)}, f32[256,512]{1,0:T(8,128)S(1)}, u32[]{:S(2)}, u32[]{:S(2)}) collective-permute-start(f32[256,512]{1,0:T(8,128)S(1)} %pad_maximum_fusion.1), channel_id=1, source_target_pairs={{0,1},{1,0},{2,3},{3,2},{4,5},{5,4},{6,7},{7,6},{8,9},{9,8},{10,11... | collective-permute-start | bytes 1572872 | tf_op jit(solution)/shard_map/ppermute | solution.py:48
  29.6 2.4 %shard_map.77 = (f32[32,4096]{1,0:T(8,128)S(1)}, f32[32,4096]{1,0:T(8,128)S(1)}) custom-call(s32[4]{0:T(128)S(1)} %pad_add_fusion.place, f32[64,512]{1,0:T(8,128)S(1)} %bitcast.20, f32[64,512]{1,0:T(8,128)S(1)} %collective-permute-done.1.q1, f32[64,512]{1,0:T(8,128)S(1)} %collective-permute-done.4.q2, f32[64,512]{1,0:T(8,128)S(1)} %collective-permute-done.5.q3, ...), custom_call_target="tpu_custom_call" | custom-call | tf_op jit(solution)/shard_map/pallas_call | solution.py:172
  34.1 2.8 %collective-permute-start.10 = (f32[8,4096]{1,0:T(8,128)S(1)}, f32[8,4096]{1,0:T(8,128)S(1)}, u32[]{:S(2)}, u32[]{:S(2)}) collective-permute-start(f32[8,4096]{1,0:T(8,128)S(1)} %get-tuple-element.71), channel_id=1, source_target_pairs={{0,96},{8,104},{16,112},{24,120},{32,0},{40,8},{48,16},{56,24},{64... | collective-permute-start | bytes 393224 | tf_op jit(solution)/shard_map/ppermute | solution.py:40
  39.0 3.1 %collective-permute-done.10 = f32[8,4096]{1,0:T(8,128)S(1)} collective-permute-done((f32[8,4096]{1,0:T(8,128)S(1)}, f32[8,4096]{1,0:T(8,128)S(1)}, u32[]{:S(2)}, u32[]{:S(2)}) %collective-permute-start.10) | collective-permute-done | bytes 131104 | tf_op jit(solution)/shard_map/ppermute | solution.py:40
  42.8 3.9 %collective-permute-done.9 = f32[8,4096]{1,0:T(8,128)S(1)} collective-permute-done((f32[8,4096]{1,0:T(8,128)S(1)}, f32[8,4096]{1,0:T(8,128)S(1)}, u32[]{:S(2)}, u32[]{:S(2)}) %collective-permute-start.9) | collective-permute-done | bytes 131104 | tf_op jit(solution)/shard_map/ppermute | solution.py:40
  46.9 2.7 %collective-permute-start.15 = (f32[8,4096]{1,0:T(8,128)S(1)}, f32[8,4096]{1,0:T(8,128)S(1)}, u32[]{:S(2)}, u32[]{:S(2)}) collective-permute-start(f32[8,4096]{1,0:T(8,128)S(1)} %fusion), channel_id=1, source_target_pairs={{0,6},{1,7},{2,0},{3,1},{4,2},{5,3},{6,4},{7,5},{8,14},{9,15},{10,... | collective-permute-start | bytes 393224 | tf_op jit(solution)/shard_map/ppermute | solution.py:36
  51.3 1.6 %collective-permute-done.14 = f32[8,4096]{1,0:T(8,128)S(1)} collective-permute-done((f32[8,4096]{1,0:T(8,128)S(1)}, f32[8,4096]{1,0:T(8,128)S(1)}, u32[]{:S(2)}, u32[]{:S(2)}) %collective-permute-start.14) | collective-permute-done | bytes 131104 | tf_op jit(solution)/shard_map/ppermute | solution.py:36
  52.9 1.8 %collective-permute-done.15 = f32[8,4096]{1,0:T(8,128)S(1)} collective-permute-done((f32[8,4096]{1,0:T(8,128)S(1)}, f32[8,4096]{1,0:T(8,128)S(1)}, u32[]{:S(2)}, u32[]{:S(2)}) %collective-permute-start.15) | collective-permute-done | bytes 131104 | tf_op jit(solution)/shard_map/ppermute | solution.py:36
  57.6 2.1 %collective-permute-start.21 = (bf16[2,128,512]{2,1,0:T(8,128)(2,1)S(1)}, bf16[2,128,512]{2,1,0:T(8,128)(2,1)S(1)}, u32[]{:S(2)}, u32[]{:S(2)}) collective-permute-start(bf16[2,128,512]{2,1,0:T(8,128)(2,1)S(1)} %get-tuple-element.46), channel_id=1, source_target_pairs={{0,6},{1,7},{2,0},{3,1},{4,2},{5,3},{6,4},{7,5},{8,14},{9,15},{10,... | collective-permute-start | bytes 786440 | tf_op jit(solution)/shard_map/ppermute | solution.py:36
  59.7 3.8 %collective-permute-start.18 = (f32[8,4096]{1,0:T(8,128)S(1)}, f32[8,4096]{1,0:T(8,128)S(1)}, u32[]{:S(2)}, u32[]{:S(2)}) collective-permute-start(f32[8,4096]{1,0:T(8,128)S(1)} %add_add_fusion.3), channel_id=1, source_target_pairs={{0,24},{8,0},{16,8},{24,16},{32,56},{40,32},{48,40},{56,48},{64,88... | collective-permute-start | bytes 393224 | tf_op jit(solution)/shard_map/ppermute | solution.py:44
  63.5 1.9 %collective-permute-done.18 = f32[8,4096]{1,0:T(8,128)S(1)} collective-permute-done((f32[8,4096]{1,0:T(8,128)S(1)}, f32[8,4096]{1,0:T(8,128)S(1)}, u32[]{:S(2)}, u32[]{:S(2)}) %collective-permute-start.18) | collective-permute-done | bytes 131104 | tf_op jit(solution)/shard_map/ppermute | solution.py:44
  65.4 4.6 %collective-permute-start.16 = (f32[8,4096]{1,0:T(8,128)S(1)}, f32[8,4096]{1,0:T(8,128)S(1)}, u32[]{:S(2)}, u32[]{:S(2)}) collective-permute-start(f32[8,4096]{1,0:T(8,128)S(1)} %add_add_fusion.3), channel_id=1, source_target_pairs={{0,16},{8,24},{16,0},{24,8},{32,48},{40,56},{48,32},{56,40},{64,80... | collective-permute-start | bytes 393224 | tf_op jit(solution)/shard_map/ppermute | solution.py:44
  70.0 3.2 %collective-permute-done.12.refs_1_ = bf16[4,256,512]{2,1,0:T(8,128)(2,1)S(1)} collective-permute-done((bf16[4,256,512]{2,1,0:T(8,128)(2,1)S(1)}, bf16[4,256,512]{2,1,0:T(8,128)(2,1)S(1)}, u32[]{:S(2)}, u32[]{:S(2)}) %collective-permute-start.12) | collective-permute-done | bytes 1048608 | tf_op jit(solution)/shard_map/ppermute | solution.py:40
  74.3 3.5 %collective-permute-start.26 = (bf16[4,256,512]{2,1,0:T(8,128)(2,1)S(1)}, bf16[4,256,512]{2,1,0:T(8,128)(2,1)S(1)}, u32[]{:S(2)}, u32[]{:S(2)}) collective-permute-start(bf16[4,256,512]{2,1,0:T(8,128)(2,1)S(1)} %collective-permute-done.12.refs_1_), channel_id=1, source_target_pairs={{0,1},{1,0},{2,3},{3,2},{4,5},{5,4},{6,7},{7,6},{8,9},{9,8},{10,11... | collective-permute-start | bytes 3145736 | tf_op jit(solution)/shard_map/ppermute | solution.py:48
  77.8 3.0 %collective-permute-start.27 = (bf16[2,128,512]{2,1,0:T(8,128)(2,1)S(1)}, bf16[2,128,512]{2,1,0:T(8,128)(2,1)S(1)}, u32[]{:S(2)}, u32[]{:S(2)}) collective-permute-start(bf16[2,128,512]{2,1,0:T(8,128)(2,1)S(1)} %get-tuple-element.51), channel_id=1, source_target_pairs={{0,4},{1,5},{2,6},{3,7},{4,0},{5,1},{6,2},{7,3},{8,12},{9,13},{10,... | collective-permute-start | bytes 786440 | tf_op jit(solution)/shard_map/ppermute | solution.py:36
  80.8 2.0 %collective-permute-start.23 = (f32[8,4096]{1,0:T(8,128)S(1)}, f32[8,4096]{1,0:T(8,128)S(1)}, u32[]{:S(2)}, u32[]{:S(2)}) collective-permute-start(f32[8,4096]{1,0:T(8,128)S(1)} %add_add_fusion.2.p0), channel_id=1, source_target_pairs={{0,64},{8,72},{16,80},{24,88},{32,96},{40,104},{48,112},{56,120},{... | collective-permute-start | bytes 393224 | tf_op jit(solution)/shard_map/ppermute | solution.py:40
  82.8 2.8 %collective-permute-done.22.p1 = f32[8,4096]{1,0:T(8,128)S(1)} collective-permute-done((f32[8,4096]{1,0:T(8,128)S(1)}, f32[8,4096]{1,0:T(8,128)S(1)}, u32[]{:S(2)}, u32[]{:S(2)}) %collective-permute-start.22) | collective-permute-done | bytes 131104 | tf_op jit(solution)/shard_map/ppermute | solution.py:40
  85.5 1.7 %collective-permute-done.27.c2 = bf16[2,128,512]{2,1,0:T(8,128)(2,1)S(1)} collective-permute-done((bf16[2,128,512]{2,1,0:T(8,128)(2,1)S(1)}, bf16[2,128,512]{2,1,0:T(8,128)(2,1)S(1)}, u32[]{:S(2)}, u32[]{:S(2)}) %collective-permute-start.27) | collective-permute-done | bytes 262176 | tf_op jit(solution)/shard_map/ppermute | solution.py:36
  87.2 2.9 %collective-permute-done.24.p3 = f32[8,4096]{1,0:T(8,128)S(1)} collective-permute-done((f32[8,4096]{1,0:T(8,128)S(1)}, f32[8,4096]{1,0:T(8,128)S(1)}, u32[]{:S(2)}, u32[]{:S(2)}) %collective-permute-start.24) | collective-permute-done | bytes 131104 | tf_op jit(solution)/shard_map/ppermute | solution.py:40
  91.2 2.1 %shard_map.80.turned = bf16[512,1024]{1,0:T(8,128)(2,1)S(1)} custom-call(s32[4]{0:T(128)S(1)} %pad_add_fusion.place, bf16[2,128,512]{2,1,0:T(8,128)(2,1)} %copy-done.11, bf16[2,128,512]{2,1,0:T(8,128)(2,1)} %copy-done.12, bf16[2,128,512]{2,1,0:T(8,128)(2,1)} %copy-done.14, bf16[2,128,512]{2,1,0:T(8,128)(2,1)} %copy-done.13), custom_call_target="tpu_custom_call" | custom-call | tf_op jit(solution)/shard_map/pallas_call | solution.py:214
  96.1 2.7 %collective-permute-start.30 = (f32[64,128]{1,0:T(8,128)S(1)}, f32[64,128]{1,0:T(8,128)S(1)}, u32[]{:S(2)}, u32[]{:S(2)}) collective-permute-start(f32[64,128]{1,0:T(8,128)S(1)} %get-tuple-element.55.u0), channel_id=1, source_target_pairs={{0,6},{1,7},{2,0},{3,1},{4,2},{5,3},{6,4},{7,5},{8,14},{9,15},{10,... | collective-permute-start | bytes 98312 | tf_op jit(solution)/shard_map/ppermute | solution.py:36
  98.8 5.0 %shard_map.82.term = f32[512,64]{1,0:T(8,128)S(1)} custom-call(f32[64,4096]{1,0:T(8,128)S(1)} %get-tuple-element.57.p_raw, f32[512,4096]{1,0:T(8,128)} %bitcast.22), custom_call_target="tpu_custom_call" | custom-call | tf_op jit(solution)/shard_map/pallas_call | solution.py:259
  104.0 2.2 %collective-permute-start.33 = (f32[256,128]{1,0:T(8,128)S(1)}, f32[256,128]{1,0:T(8,128)S(1)}, u32[]{:S(2)}, u32[]{:S(2)}) collective-permute-start(f32[256,128]{1,0:T(8,128)S(1)} %pad_maximum_fusion.3), channel_id=1, source_target_pairs={{0,1},{1,0},{2,3},{3,2},{4,5},{5,4},{6,7},{7,6},{8,9},{9,8},{10,11... | collective-permute-start | bytes 393224 | tf_op jit(solution)/shard_map/ppermute | solution.py:48
  108.3 3.8 %collective-permute-start.36 = (f32[64,512]{1,0:T(8,128)S(1)}, f32[64,512]{1,0:T(8,128)S(1)}, u32[]{:S(2)}, u32[]{:S(2)}) collective-permute-start(f32[64,512]{1,0:T(8,128)S(1)} %shard_map.83), channel_id=1, source_target_pairs={{0,24},{8,0},{16,8},{24,16},{32,56},{40,32},{48,40},{56,48},{64,88... | collective-permute-start | bytes 393224 | tf_op jit(solution)/shard_map/ppermute | solution.py:44
  113.4 6.1 %shard_map.84.inverse = f32[64,64]{1,0:T(8,128)S(1)} custom-call(f32[64,4096]{1,0:T(8,128)S(1)} %get-tuple-element.57.p_raw), custom_call_target="tpu_custom_call" | custom-call | tf_op jit(solution)/shard_map/pallas_call | solution.py:308
  126.2 6.0 %shard_map.85 = (bf16[128,1024]{1,0:T(8,128)(2,1)S(1)}, bf16[128,1024]{1,0:T(8,128)(2,1)}, bf16[128,1024]{1,0:T(8,128)(2,1)}, bf16[128,1024]{1,0:T(8,128)(2,1)}) custom-call(s32[4]{0:T(128)S(1)} %pad_add_fusion.place, bf16[4,128,4096]{2,1,0:T(8,128)(2,1)S(1)} %bitcast.14, bf16[4,256,512]{2,1,0:T(8,128)(2,1)S(1)} %copy-done.4, ...), custom_call_target="tpu_custom_call" | custom-call | tf_op jit(solution)/shard_map/pallas_call | solution.py:360
  133.4 2.3 %collective-permute-start.39 = (bf16[128,1024]{1,0:T(8,128)(2,1)}, bf16[128,1024]{1,0:T(8,128)(2,1)S(1)}, u32[]{:S(2)}, u32[]{:S(2)}) collective-permute-start(bf16[128,1024]{1,0:T(8,128)(2,1)} %get-tuple-element.63), channel_id=1, source_target_pairs={{0,24},{8,0},{16,8},{24,16},{32,56},{40,32},{48,40},{56,48},{64,88... | collective-permute-start | bytes 786440 | tf_op jit(solution)/shard_map/ppermute | solution.py:44
  137.0 12.1 %shard_map.86 = (f32[64,512]{1,0:T(8,128)}, f32[512,4096]{1,0:T(8,128)}) custom-call(f32[64,64]{1,0:T(8,128)S(1)} %shard_map.84.inverse, f32[64,512]{1,0:T(8,128)S(1)} %add_add_fusion.w, bf16[512,1024]{1,0:T(8,128)(2,1)S(1)} %shard_map.80.turned, f32[64,4096]{1,0:T(8,128)S(1)} %get-tuple-element.57.p_raw, f32[512,4096]{1,0:T(8,128)} %bitcast.23, ...), custom_call_target="tpu_custom_call" | custom-call | tf_op jit(solution)/shard_map/pallas_call | solution.py:335
  (132 shorter events, 34.6 us)
Async XLA Ops:
  7.2 67.1 %all-gather.6.cloned.1.call-start = ((), (), s32[]{:S(2)}) async-start(), calls=%async_computation.1 | async-start | bytes 5242880 | tf_op jit(solution)/shard_map/all_gather | solution.py:381
  7.9 129.1 %all-gather.4.cloned.1.call-start = ((), (), s32[]{:S(2)}) async-start(), calls=%async_computation | async-start | bytes 9437184 | tf_op jit(solution)/shard_map/all_gather | solution.py:404
  9.0 12.5 %collective-permute-start.3 = (bf16[256,512]{1,0:T(8,128)(2,1)S(1)}, bf16[256,512]{1,0:T(8,128)(2,1)S(1)}, u32[]{:S(2)}, u32[]{:S(2)}) collective-permute-start(bf16[256,512]{1,0:T(8,128)(2,1)S(1)} %constant_dynamic-slice_fusion), channel_id=1, source_target_pairs={{0,6},{1,7},{2,0},{3,1},{4,2},{5,3},{6,4},{7,5},{8,14},{9,15},{10,... | collective-permute-start | bytes 786440 | tf_op jit(solution)/shard_map/ppermute | solution.py:36
  12.3 9.1 %collective-permute-start = (bf16[256,512]{1,0:T(8,128)(2,1)S(1)}, bf16[256,512]{1,0:T(8,128)(2,1)S(1)}, u32[]{:S(2)}, u32[]{:S(2)}) collective-permute-start(bf16[256,512]{1,0:T(8,128)(2,1)S(1)} %constant_dynamic-slice_fusion), channel_id=1, source_target_pairs={{0,2},{1,3},{2,4},{3,5},{4,6},{5,7},{6,0},{7,1},{8,10},{9,11},{10,... | collective-permute-start | bytes 786440 | tf_op jit(solution)/shard_map/ppermute | solution.py:36
  12.3 9.1 %collective-permute-start.1 = (f32[64,512]{1,0:T(8,128)}, f32[64,512]{1,0:T(8,128)S(1)}, u32[]{:S(2)}, u32[]{:S(2)}) collective-permute-start(f32[64,512]{1,0:T(8,128)} %bitcast.15), channel_id=1, source_target_pairs={{0,6},{1,7},{2,0},{3,1},{4,2},{5,3},{6,4},{7,5},{8,14},{9,15},{10,... | collective-permute-start | bytes 393224 | tf_op jit(solution)/shard_map/ppermute | solution.py:36
  15.0 11.0 %collective-permute-start.5 = (f32[64,512]{1,0:T(8,128)}, f32[64,512]{1,0:T(8,128)S(1)}, u32[]{:S(2)}, u32[]{:S(2)}) collective-permute-start(f32[64,512]{1,0:T(8,128)} %bitcast.17), channel_id=1, source_target_pairs={{0,2},{1,3},{2,4},{3,5},{4,6},{5,7},{6,0},{7,1},{8,10},{9,11},{10,... | collective-permute-start | bytes 393224 | tf_op jit(solution)/shard_map/ppermute | solution.py:36
  34.1 8.0 %collective-permute-start.10 = (f32[8,4096]{1,0:T(8,128)S(1)}, f32[8,4096]{1,0:T(8,128)S(1)}, u32[]{:S(2)}, u32[]{:S(2)}) collective-permute-start(f32[8,4096]{1,0:T(8,128)S(1)} %get-tuple-element.71), channel_id=1, source_target_pairs={{0,96},{8,104},{16,112},{24,120},{32,0},{40,8},{48,16},{56,24},{64... | collective-permute-start | bytes 393224 | tf_op jit(solution)/shard_map/ppermute | solution.py:40
  37.3 9.5 %collective-permute-start.9 = (f32[8,4096]{1,0:T(8,128)S(1)}, f32[8,4096]{1,0:T(8,128)S(1)}, u32[]{:S(2)}, u32[]{:S(2)}) collective-permute-start(f32[8,4096]{1,0:T(8,128)S(1)} %get-tuple-element.72), channel_id=1, source_target_pairs={{0,32},{8,40},{16,48},{24,56},{32,64},{40,72},{48,80},{56,88},{64,... | collective-permute-start | bytes 393224 | tf_op jit(solution)/shard_map/ppermute | solution.py:40
  38.9 10.6 %collective-permute-start.2 = (bf16[256,512]{1,0:T(8,128)(2,1)S(1)}, bf16[256,512]{1,0:T(8,128)(2,1)S(1)}, u32[]{:S(2)}, u32[]{:S(2)}) collective-permute-start(bf16[256,512]{1,0:T(8,128)(2,1)S(1)} %copy-done.16), channel_id=1, source_target_pairs={{0,4},{1,5},{2,6},{3,7},{4,0},{5,1},{6,2},{7,3},{8,12},{9,13},{10,... | collective-permute-start | bytes 786440 | tf_op jit(solution)/shard_map/ppermute | solution.py:36
  46.9 7.8 %collective-permute-start.15 = (f32[8,4096]{1,0:T(8,128)S(1)}, f32[8,4096]{1,0:T(8,128)S(1)}, u32[]{:S(2)}, u32[]{:S(2)}) collective-permute-start(f32[8,4096]{1,0:T(8,128)S(1)} %fusion), channel_id=1, source_target_pairs={{0,6},{1,7},{2,0},{3,1},{4,2},{5,3},{6,4},{7,5},{8,14},{9,15},{10,... | collective-permute-start | bytes 393224 | tf_op jit(solution)/shard_map/ppermute | solution.py:36
  49.7 23.5 %collective-permute-start.12 = (bf16[4,256,512]{2,1,0:T(8,128)(2,1)S(1)}, bf16[4,256,512]{2,1,0:T(8,128)(2,1)S(1)}, u32[]{:S(2)}, u32[]{:S(2)}) collective-permute-start(bf16[4,256,512]{2,1,0:T(8,128)(2,1)S(1)} %pad_maximum_fusion.refs_0_), channel_id=1, source_target_pairs={{0,96},{8,104},{16,112},{24,120},{32,0},{40,8},{48,16},{56,24},{64... | collective-permute-start | bytes 3145736 | tf_op jit(solution)/shard_map/ppermute | solution.py:40
  49.8 23.4 %collective-permute-start.19 = (bf16[4,256,512]{2,1,0:T(8,128)(2,1)S(1)}, bf16[4,256,512]{2,1,0:T(8,128)(2,1)S(1)}, u32[]{:S(2)}, u32[]{:S(2)}) collective-permute-start(bf16[4,256,512]{2,1,0:T(8,128)(2,1)S(1)} %pad_maximum_fusion.refs_0_), channel_id=1, source_target_pairs={{0,32},{8,40},{16,48},{24,56},{32,64},{40,72},{48,80},{56,88},{64,... | collective-permute-start | bytes 3145736 | tf_op jit(solution)/shard_map/ppermute | solution.py:40
  56.3 9.1 %collective-permute-start.20 = (bf16[2,128,512]{2,1,0:T(8,128)(2,1)S(1)}, bf16[2,128,512]{2,1,0:T(8,128)(2,1)S(1)}, u32[]{:S(2)}, u32[]{:S(2)}) collective-permute-start(bf16[2,128,512]{2,1,0:T(8,128)(2,1)S(1)} %get-tuple-element.45), channel_id=1, source_target_pairs={{0,2},{1,3},{2,4},{3,5},{4,6},{5,7},{6,0},{7,1},{8,10},{9,11},{10,... | collective-permute-start | bytes 786440 | tf_op jit(solution)/shard_map/ppermute | solution.py:36
  57.6 12.3 %collective-permute-start.21 = (bf16[2,128,512]{2,1,0:T(8,128)(2,1)S(1)}, bf16[2,128,512]{2,1,0:T(8,128)(2,1)S(1)}, u32[]{:S(2)}, u32[]{:S(2)}) collective-permute-start(bf16[2,128,512]{2,1,0:T(8,128)(2,1)S(1)} %get-tuple-element.46), channel_id=1, source_target_pairs={{0,6},{1,7},{2,0},{3,1},{4,2},{5,3},{6,4},{7,5},{8,14},{9,15},{10,... | collective-permute-start | bytes 786440 | tf_op jit(solution)/shard_map/ppermute | solution.py:36
  65.4 7.8 %collective-permute-start.17 = (f32[8,4096]{1,0:T(8,128)S(1)}, f32[8,4096]{1,0:T(8,128)S(1)}, u32[]{:S(2)}, u32[]{:S(2)}) collective-permute-start(f32[8,4096]{1,0:T(8,128)S(1)} %add_add_fusion.3), channel_id=1, source_target_pairs={{0,8},{8,16},{16,24},{24,0},{32,40},{40,48},{48,56},{56,32},{64,72... | collective-permute-start | bytes 393224 | tf_op jit(solution)/shard_map/ppermute | solution.py:44
  65.4 8.8 %collective-permute-start.16 = (f32[8,4096]{1,0:T(8,128)S(1)}, f32[8,4096]{1,0:T(8,128)S(1)}, u32[]{:S(2)}, u32[]{:S(2)}) collective-permute-start(f32[8,4096]{1,0:T(8,128)S(1)} %add_add_fusion.3), channel_id=1, source_target_pairs={{0,16},{8,24},{16,0},{24,8},{32,48},{40,56},{48,32},{56,40},{64,80... | collective-permute-start | bytes 393224 | tf_op jit(solution)/shard_map/ppermute | solution.py:44
  74.3 12.9 %collective-permute-start.26 = (bf16[4,256,512]{2,1,0:T(8,128)(2,1)S(1)}, bf16[4,256,512]{2,1,0:T(8,128)(2,1)S(1)}, u32[]{:S(2)}, u32[]{:S(2)}) collective-permute-start(bf16[4,256,512]{2,1,0:T(8,128)(2,1)S(1)} %collective-permute-done.12.refs_1_), channel_id=1, source_target_pairs={{0,1},{1,0},{2,3},{3,2},{4,5},{5,4},{6,7},{7,6},{8,9},{9,8},{10,11... | collective-permute-start | bytes 3145736 | tf_op jit(solution)/shard_map/ppermute | solution.py:48
  77.8 9.4 %collective-permute-start.27 = (bf16[2,128,512]{2,1,0:T(8,128)(2,1)S(1)}, bf16[2,128,512]{2,1,0:T(8,128)(2,1)S(1)}, u32[]{:S(2)}, u32[]{:S(2)}) collective-permute-start(bf16[2,128,512]{2,1,0:T(8,128)(2,1)S(1)} %get-tuple-element.51), channel_id=1, source_target_pairs={{0,4},{1,5},{2,6},{3,7},{4,0},{5,1},{6,2},{7,3},{8,12},{9,13},{10,... | collective-permute-start | bytes 786440 | tf_op jit(solution)/shard_map/ppermute | solution.py:36
  82.8 7.3 %collective-permute-start.24 = (f32[8,4096]{1,0:T(8,128)S(1)}, f32[8,4096]{1,0:T(8,128)S(1)}, u32[]{:S(2)}, u32[]{:S(2)}) collective-permute-start(f32[8,4096]{1,0:T(8,128)S(1)} %add_add_fusion.2.p0), channel_id=1, source_target_pairs={{0,32},{8,40},{16,48},{24,56},{32,64},{40,72},{48,80},{56,88},{64,... | collective-permute-start | bytes 393224 | tf_op jit(solution)/shard_map/ppermute | solution.py:40
  94.4 9.4 %collective-permute-start.29 = (bf16[4,256,512]{2,1,0:T(8,128)(2,1)S(1)}, bf16[4,256,512]{2,1,0:T(8,128)(2,1)S(1)}, u32[]{:S(2)}, u32[]{:S(2)}) collective-permute-start(bf16[4,256,512]{2,1,0:T(8,128)(2,1)S(1)} %copy-done.4), channel_id=1, source_target_pairs={{0,1},{1,0},{2,3},{3,2},{4,5},{5,4},{6,7},{7,6},{8,9},{9,8},{10,11... | collective-permute-start | bytes 3145736 | tf_op jit(solution)/shard_map/ppermute | solution.py:48
  94.5 25.9 %collective-permute-start.25 = (bf16[4,256,512]{2,1,0:T(8,128)(2,1)S(1)}, bf16[4,256,512]{2,1,0:T(8,128)(2,1)S(1)}, u32[]{:S(2)}, u32[]{:S(2)}) collective-permute-start(bf16[4,256,512]{2,1,0:T(8,128)(2,1)S(1)} %copy-done.4), channel_id=1, source_target_pairs={{0,64},{8,72},{16,80},{24,88},{32,96},{40,104},{48,112},{56,120},{... | collective-permute-start | bytes 3145736 | tf_op jit(solution)/shard_map/ppermute | solution.py:40
  96.1 7.7 %collective-permute-start.32 = (f32[64,128]{1,0:T(8,128)S(1)}, f32[64,128]{1,0:T(8,128)S(1)}, u32[]{:S(2)}, u32[]{:S(2)}) collective-permute-start(f32[64,128]{1,0:T(8,128)S(1)} %get-tuple-element.55.u0), channel_id=1, source_target_pairs={{0,2},{1,3},{2,4},{3,5},{4,6},{5,7},{6,0},{7,1},{8,10},{9,11},{10,... | collective-permute-start | bytes 98312 | tf_op jit(solution)/shard_map/ppermute | solution.py:36
  96.1 7.7 %collective-permute-start.30 = (f32[64,128]{1,0:T(8,128)S(1)}, f32[64,128]{1,0:T(8,128)S(1)}, u32[]{:S(2)}, u32[]{:S(2)}) collective-permute-start(f32[64,128]{1,0:T(8,128)S(1)} %get-tuple-element.55.u0), channel_id=1, source_target_pairs={{0,6},{1,7},{2,0},{3,1},{4,2},{5,3},{6,4},{7,5},{8,14},{9,15},{10,... | collective-permute-start | bytes 98312 | tf_op jit(solution)/shard_map/ppermute | solution.py:36
  108.3 12.1 %collective-permute-start.36 = (f32[64,512]{1,0:T(8,128)S(1)}, f32[64,512]{1,0:T(8,128)S(1)}, u32[]{:S(2)}, u32[]{:S(2)}) collective-permute-start(f32[64,512]{1,0:T(8,128)S(1)} %shard_map.83), channel_id=1, source_target_pairs={{0,24},{8,0},{16,8},{24,16},{32,56},{40,32},{48,40},{56,48},{64,88... | collective-permute-start | bytes 393224 | tf_op jit(solution)/shard_map/ppermute | solution.py:44
  112.2 8.9 %collective-permute-start.35 = (f32[64,512]{1,0:T(8,128)S(1)}, f32[64,512]{1,0:T(8,128)S(1)}, u32[]{:S(2)}, u32[]{:S(2)}) collective-permute-start(f32[64,512]{1,0:T(8,128)S(1)} %shard_map.83), channel_id=1, source_target_pairs={{0,8},{8,16},{16,24},{24,0},{32,40},{40,48},{48,56},{56,32},{64,72... | collective-permute-start | bytes 393224 | tf_op jit(solution)/shard_map/ppermute | solution.py:44
  112.2 8.9 %collective-permute-start.34 = (f32[64,512]{1,0:T(8,128)S(1)}, f32[64,512]{1,0:T(8,128)S(1)}, u32[]{:S(2)}, u32[]{:S(2)}) collective-permute-start(f32[64,512]{1,0:T(8,128)S(1)} %shard_map.83), channel_id=1, source_target_pairs={{0,16},{8,24},{16,0},{24,8},{32,48},{40,56},{48,32},{56,40},{64,80... | collective-permute-start | bytes 393224 | tf_op jit(solution)/shard_map/ppermute | solution.py:44
  122.3 13.5 %collective-permute-start.44 = (f32[64,512]{1,0:T(8,128)S(1)}, f32[64,512]{1,0:T(8,128)S(1)}, u32[]{:S(2)}, u32[]{:S(2)}) collective-permute-start(f32[64,512]{1,0:T(8,128)S(1)} %add_add_fusion.1), channel_id=1, source_target_pairs={{0,96},{8,104},{16,112},{24,120},{32,0},{40,8},{48,16},{56,24},{64... | collective-permute-start | bytes 393224 | tf_op jit(solution)/shard_map/ppermute | solution.py:40
  123.7 13.2 %collective-permute-start.43 = (f32[64,512]{1,0:T(8,128)S(1)}, f32[64,512]{1,0:T(8,128)S(1)}, u32[]{:S(2)}, u32[]{:S(2)}) collective-permute-start(f32[64,512]{1,0:T(8,128)S(1)} %add_add_fusion.1), channel_id=1, source_target_pairs={{0,32},{8,40},{16,48},{24,56},{32,64},{40,72},{48,80},{56,88},{64,... | collective-permute-start | bytes 393224 | tf_op jit(solution)/shard_map/ppermute | solution.py:40
  123.8 13.2 %collective-permute-start.42 = (f32[64,512]{1,0:T(8,128)S(1)}, f32[64,512]{1,0:T(8,128)S(1)}, u32[]{:S(2)}, u32[]{:S(2)}) collective-permute-start(f32[64,512]{1,0:T(8,128)S(1)} %add_add_fusion.1), channel_id=1, source_target_pairs={{0,64},{8,72},{16,80},{24,88},{32,96},{40,104},{48,112},{56,120},{... | collective-permute-start | bytes 393224 | tf_op jit(solution)/shard_map/ppermute | solution.py:40
  132.2 16.9 %collective-permute-start.41 = (bf16[128,1024]{1,0:T(8,128)(2,1)}, bf16[128,1024]{1,0:T(8,128)(2,1)S(1)}, u32[]{:S(2)}, u32[]{:S(2)}) collective-permute-start(bf16[128,1024]{1,0:T(8,128)(2,1)} %get-tuple-element.65), channel_id=1, source_target_pairs={{0,8},{8,16},{16,24},{24,0},{32,40},{40,48},{48,56},{56,32},{64,72... | collective-permute-start | bytes 786440 | tf_op jit(solution)/shard_map/ppermute | solution.py:44
  133.4 15.7 %collective-permute-start.39 = (bf16[128,1024]{1,0:T(8,128)(2,1)}, bf16[128,1024]{1,0:T(8,128)(2,1)S(1)}, u32[]{:S(2)}, u32[]{:S(2)}) collective-permute-start(bf16[128,1024]{1,0:T(8,128)(2,1)} %get-tuple-element.63), channel_id=1, source_target_pairs={{0,24},{8,0},{16,8},{24,16},{32,56},{40,32},{48,40},{56,48},{64,88... | collective-permute-start | bytes 786440 | tf_op jit(solution)/shard_map/ppermute | solution.py:44
  135.8 13.4 %collective-permute-start.40 = (bf16[128,1024]{1,0:T(8,128)(2,1)}, bf16[128,1024]{1,0:T(8,128)(2,1)S(1)}, u32[]{:S(2)}, u32[]{:S(2)}) collective-permute-start(bf16[128,1024]{1,0:T(8,128)(2,1)} %get-tuple-element.64), channel_id=1, source_target_pairs={{0,16},{8,24},{16,0},{24,8},{32,48},{40,56},{48,32},{56,40},{64,80... | collective-permute-start | bytes 786440 | tf_op jit(solution)/shard_map/ppermute | solution.py:44
  (36 other events, 358.4 us)
Sparse Core Ops, SparseCore 0:
  9.7 51.6 all-gather.5
  74.4 54.4 all-gather.3
